TPU v7x, 32 devices: a whole 2x2x4 slice. The times are simulated.
32 devices in a mesh: seq: 8 (over z, x), head: 4 (over y, core).
Axes of the slice: x: 2, y: 2, z: 4, core: 2. Of those that a mesh axis runs over, the one named last changes fastest.
Arguments:
- queries: bfloat16 [8192, 2048], P('seq', 'head'), may hold values from -6 to 6
- key_rows: bfloat16 [8192, 2048], P('seq', 'head'), may hold values from -6 to 6
- value_rows: bfloat16 [8192, 4096], P('seq', 'head'), may hold values from -6 to 6
- out_gate: bfloat16 [8192, 4096], P('seq', 'head'), may hold values from -6 to 6
- write_rate: float32 [32, 8192], P('head', 'seq'), may hold values from 0.00390625 to 1
- log_gate: float32 [32, 8192], P('head', 'seq'), may hold values from -1 to 0, as said below
- doc_start: int32 [8192], P('seq'), may hold values 0 or 1
- norm_gain: float32 [128], replicated, may hold values from 0.1 to 1.9
- out_weight: bfloat16 [4096, 2048], P('head'), may hold values from -0.125 to 0.125
Outputs:
- mixed: bfloat16 [8192, 2048], P('seq', 'head')
Inputs may be any that keep to these rules, and one draw needn't show every extreme that they name: `log_gate`: log of the per-token decay factor of each value head's state.
All inputs are finite; a program needn't handle non-finite values. No bound on the sum of `doc_start` on one device may be relied on, other than what follows from the above.
Results may differ from a plain program's by a relative error of at most 0.027.
Values may be sent and summed in bfloat16 or wider, within the bound.
No kernel may reach another device: no remote copies, remote signals or barrier semaphores. Data moves between devices by JAX's collectives and lax.ppermute only.
A program may use at most 128 MiB of HBM per device.

v0:
```python
import jax
import jax.numpy as jnp
from jax import lax
from jax.sharding import PartitionSpec as P

DK = 128
DV = 128
SPAN = 64


highest = lax.Precision.HIGHEST


def shifted(block, axis, distance):
    devices = range(lax.axis_size(axis))
    route = [(i - distance, i) for i in devices if i - distance in devices]
    return lax.ppermute(block, axis, route)


def unit_rows(values):
    return values * lax.rsqrt(jnp.sum(values * values, axis=-1, keepdims=True) + 1e-06)


def block_parts(queries, keys, values, rates, logs, starts):
    cumlog = jnp.cumsum(logs, axis=-1)
    resets = jnp.cumsum(starts, axis=-1)
    token_positions = jnp.arange(SPAN)
    lower_tri = token_positions[:, None] >= token_positions[None, :]
    same_doc = (resets[..., :, None] == resets[..., None, :]) & lower_tri
    log_gap = cumlog[..., :, None] - cumlog[..., None, :]
    decays = jnp.where(same_doc, jnp.exp(jnp.where(same_doc, log_gap, 0.0)), 0.0)
    last_log = cumlog[..., -1:]
    head_keep = jnp.exp(cumlog) * (resets == 0.0)
    tail_keep = jnp.exp(last_log - cumlog) * (resets == resets[..., -1:])
    whole_keep = jnp.exp(cumlog[..., -1]) * (resets[..., -1] == 0.0)
    identity = jnp.eye(SPAN, dtype=jnp.float32)
    key_inner = jnp.einsum("...ik,...jk->...ij", keys, keys, precision=highest)
    coupling = rates[..., :, None] * key_inner * decays * (1.0 - identity)
    inverse = identity - coupling
    powered = coupling
    extent = 1
    while 2 * extent < SPAN:
        powered = jnp.matmul(powered, powered, precision=highest)
        inverse = jnp.matmul(inverse, identity + powered, precision=highest)
        extent = extent * 2
    erase_keys = jnp.matmul(inverse, (rates * head_keep)[..., None] * keys, precision=highest)
    write_vals = jnp.matmul(inverse, rates[..., None] * values, precision=highest)
    scores = jnp.einsum("...ik,...jk->...ij", queries, keys, precision=highest) * decays
    return (queries, keys, erase_keys, write_vals, scores, head_keep, tail_keep, whole_keep)


def state_terms(parts, states):
    queries, keys, erase_keys, write_vals, scores, head_keep, tail_keep, whole_keep = parts
    seen = jnp.einsum("...ck,...vk->...cv", queries, states, precision=highest)
    erased = jnp.einsum("...ck,...vk->...cv", erase_keys, states, precision=highest)
    return (head_keep[..., None] * seen - jnp.matmul(scores, erased, precision=highest), erased)


def block_step(parts, state_now):
    queries, keys, erase_keys, write_vals, scores, head_keep, tail_keep, whole_keep = parts
    terms, erased = state_terms(parts, state_now)
    output = terms + jnp.matmul(scores, write_vals, precision=highest)
    fresh_vals = write_vals - erased
    state_next = whole_keep[..., None, None] * state_now + jnp.einsum(
        "...cv,...ck->...vk", tail_keep[..., None] * fresh_vals, keys, precision=highest
    )
    return (output, state_next)


def block_transition(parts):
    queries, keys, erase_keys, write_vals, scores, head_keep, tail_keep, whole_keep = parts
    eye_keys = jnp.eye(DK, dtype=jnp.float32)
    moves = whole_keep[..., None, None] * eye_keys - jnp.einsum(
        "...ck,...cj->...kj", erase_keys, tail_keep[..., None] * keys, precision=highest
    )
    carried = jnp.einsum(
        "...cv,...ck->...vk", tail_keep[..., None] * write_vals, keys, precision=highest
    )
    return (moves, carried)


def blocks_first(array_in):
    return jnp.moveaxis(array_in, 1, 0)


def local(
    queries, key_rows, value_rows, out_gate, write_rate, log_gate, doc_start, norm_gain, out_weight
):
    tokens_here = queries.shape[0]
    heads_here = value_rows.shape[1] // DV
    keys_here = key_rows.shape[1] // DK
    per_key = heads_here // keys_here
    blocks = tokens_here // SPAN

    def by_head(values, width):
        spread = values.reshape(blocks, SPAN, heads_here, width)
        return jnp.transpose(spread, (2, 0, 1, 3))

    query_unit = unit_rows(queries.astype(jnp.float32).reshape(tokens_here, keys_here, DK))
    key_unit = unit_rows(key_rows.astype(jnp.float32).reshape(tokens_here, keys_here, DK))
    query_heads = by_head(jnp.repeat(query_unit, per_key, axis=1), DK)
    key_heads = by_head(jnp.repeat(key_unit, per_key, axis=1), DK)
    value_heads = by_head(value_rows.astype(jnp.float32).reshape(tokens_here, heads_here, DV), DV)
    rates = write_rate.reshape(heads_here, blocks, SPAN)
    logs = log_gate.reshape(heads_here, blocks, SPAN)
    starts = jnp.broadcast_to(
        doc_start.astype(jnp.float32).reshape(1, blocks, SPAN), (heads_here, blocks, SPAN)
    )
    parts = block_parts(query_heads, key_heads, value_heads, rates, logs, starts)
    moves, carried = block_transition(parts)
    eye_heads = jnp.broadcast_to(jnp.eye(DK, dtype=jnp.float32), (heads_here, DK, DK))
    empty = jnp.zeros((heads_here, DV, DK), jnp.float32)

    def fold_blocks(carry, pair):
        total_move, total_state = carry
        move_now, carried_now = pair
        next_move = jnp.matmul(total_move, move_now, precision=highest)
        next_state = jnp.matmul(total_state, move_now, precision=highest) + carried_now
        return ((next_move, next_state), carry)

    (shard_move, shard_state), (prefix_moves, prefix_states) = lax.scan(
        fold_blocks, (eye_heads, empty), (blocks_first(moves), blocks_first(carried))
    )

    def pass_state(round_index, start_state):
        shard_end = jnp.matmul(start_state, shard_move, precision=highest) + shard_state
        return shifted(shard_end.astype(jnp.bfloat16), "seq", 1).astype(shard_end.dtype)

    start_state = lax.fori_loop(0, lax.axis_size("seq") - 1, pass_state, empty)

    def advance(state_now, inputs_now):
        output, state_next = block_step(inputs_now, state_now)
        return (state_next, output)

    final_state, outputs = lax.scan(advance, start_state, jax.tree.map(blocks_first, parts))
    attended = blocks_first(outputs)
    attended = jnp.transpose(attended, (1, 2, 0, 3)).reshape(tokens_here, heads_here, DV)
    gate_vals = out_gate.astype(jnp.float32).reshape(tokens_here, heads_here, DV)
    scale_rows = lax.rsqrt(jnp.mean(attended * attended, axis=-1, keepdims=True) + 1e-06)
    normed = (attended * scale_rows * norm_gain * jax.nn.silu(gate_vals)).astype(jnp.bfloat16)
    normed = normed.reshape(tokens_here, heads_here * DV)
    summed = lax.psum_scatter(
        lax.dot_general(
            out_weight, normed, (((0,), (1,)), ((), ())), preferred_element_type=jnp.float32
        ).astype(jnp.bfloat16),
        "head",
        scatter_dimension=0,
        tiled=True,
    )
    return jnp.transpose(summed)


def solution(mesh):
    placed = (
        P("seq", "head"),
        P("seq", "head"),
        P("seq", "head"),
        P("seq", "head"),
        P("head", "seq"),
        P("head", "seq"),
        P("seq"),
        P(),
        P("head", None),
    )
    return jax.shard_map(
        local, mesh=mesh, in_specs=placed, out_specs=P("seq", "head"), check_vma=False
    )
```

profile of v0, /device:TPU:8, one launch (start us, length us, event | category | flops | bytes accessed | tf_op | source)
XLA Modules:
  0.0 544.8 jit_solution(16580683565727149631)
XLA Ops:
  9.6 2.4 broadcast_multiply_fusion.1
  17.5 8.1 %multiply_multiply_fusion = f32[8,16,64,64]{3,2,1,0:T(8,128)S(1)} fusion(f32[8,16,64,128]{3,2,1,0:T(8,128)S(1)} %bitcast.188, f32[64,64]{1,0:T(8,128)S(1)} %broadcast_subtract_fusion, f32[8,16,64]{2,1,0:T(8,128)S(1)} %reduce_window_sum.18, f32[8,16,64]{2,1,0:T(8,128)S(1)} %reduce_window_sum.17, f32[8,16,64]{2,1,0:T(8,128)S(1)} %mul.185, ...), kind=kOutput, calls=%fused_computation.85 | convolution fusion | flops 809500672 | bytes 6410240 | tf_op jit(solution)/shard_map/...ik,...jk->...ij/dot_general | solution.py:37
  25.7 6.0 %fusion.86 = f32[8,16,64,64]{3,2,1,0:T(8,128)S(1)} fusion(f32[8,16,64,64]{3,2,1,0:T(8,128)S(1)} %multiply_multiply_fusion), kind=kOutput, calls=%fused_computation.121 | convolution fusion | flops 402653184 | bytes 4194304 | tf_op jit(solution)/shard_map/dot_general | solution.py:43
  31.6 5.4 fusion.87
  37.1 5.5 %fusion.62 = f32[8,16,64,64]{3,2,1,0:T(8,128)S(1)} fusion(f32[8,16,64,64]{3,2,1,0:T(8,128)S(1)} %fusion.86, f32[8,16,64,64]{3,2,1,0:T(8,128)S(1)} %multiply_multiply_fusion, f32[64,64]{1,0:T(8,128)S(1)} %fusion.84), kind=kOutput, calls=%fused_computation.82 | convolution fusion | flops 403701760 | bytes 6307840 | tf_op jit(solution)/shard_map/dot_general | solution.py:44
  42.5 5.6 %fusion.88 = f32[8,16,64,64]{3,2,1,0:T(8,128)S(1)} fusion(f32[8,16,64,64]{3,2,1,0:T(8,128)S(1)} %fusion.87), kind=kOutput, calls=%fused_computation.123 | convolution fusion | flops 402653184 | bytes 4194304 | tf_op jit(solution)/shard_map/dot_general | solution.py:43
  48.2 5.4 fusion.60
  53.5 5.6 %fusion.89 = f32[8,16,64,64]{3,2,1,0:T(8,128)S(1)} fusion(f32[8,16,64,64]{3,2,1,0:T(8,128)S(1)} %fusion.88), kind=kOutput, calls=%fused_computation.124 | convolution fusion | flops 402653184 | bytes 4194304 | tf_op jit(solution)/shard_map/dot_general | solution.py:43
  59.2 5.3 fusion.58
  64.5 5.8 %fusion.90 = f32[8,16,64,64]{3,2,1,0:T(8,128)S(1)} fusion(f32[8,16,64,64]{3,2,1,0:T(8,128)S(1)} %fusion.89), kind=kOutput, calls=%fused_computation.125 | convolution fusion | flops 402653184 | bytes 4194304 | tf_op jit(solution)/shard_map/dot_general | solution.py:43
  70.4 5.4 fusion.56
  77.2 5.3 fusion.54
  82.6 6.2 %fusion.46 = f32[8,16,64,128]{3,2,1,0:T(8,128)} fusion(f32[8,16,64,64]{3,2,1,0:T(8,128)S(1)} %fusion.54, f32[16,64,8,128]{3,2,1,0:T(8,128)S(1)} %bitcast.198, f32[8,16,64]{2,1,0:T(8,128)S(1)} %mul.185), kind=kOutput, calls=%fused_computation.63 | convolution fusion | flops 806354944 | bytes 10518528 | tf_op jit(solution)/shard_map/dot_general | solution.py:47
  88.7 5.8 %fusion.52 = f32[8,16,64,128]{3,2,1,0:T(8,128)} fusion(f32[8,16,64,64]{3,2,1,0:T(8,128)S(1)} %fusion.54, f32[8,16,64,128]{3,2,1,0:T(8,128)S(1)} %bitcast.189, f32[8,16,64]{2,1,0:T(8,128)S(1)} %get-tuple-element.274), kind=kOutput, calls=%fused_computation.72 | convolution fusion | flops 806354944 | bytes 10518528 | tf_op jit(solution)/shard_map/dot_general | solution.py:46
  94.7 19.8 %fusion.68 = f32[16,8,128,128]{3,2,0,1:T(8,128)} fusion(f32[8,16,64,128]{3,2,1,0:T(8,128)} %bitcast.190, f32[8,16,64,128]{3,2,1,0:T(8,128)} %fusion.46, f32[8,16,64]{2,1,0:T(8,128)S(1)} %get-tuple-element.273), kind=kOutput, calls=%fused_computation.87 | convolution fusion | flops 1611661312 | bytes 16809984 | tf_op jit(solution)/shard_map/...cv,...ck->...vk/dot_general | solution.py:76
  114.5 18.4 %bitcast_subtract_fusion.1 = f32[16,8,128,128]{3,2,0,1:T(8,128)} fusion(f32[128,128]{1,0:T(8,128)S(1)} %fusion.83, f32[16,8]{0,1:T(8,128)S(1)} %copy-done.11, f32[8,16,64,128]{3,2,1,0:T(8,128)S(1)} %copy-done.4, f32[8,16,64,128]{3,2,1,0:T(8,128)S(1)} %bitcast.192, f32[8,16,64]{2,1,0:T(8,128)S(1)} %get-tuple-element.273), kind=kOutput, calls=%fused_computation.52 | convolution fusion | flops 1615855616 | bytes 16876032 | tf_op jit(solution)/shard_map/...ck,...cj->...kj/dot_general | solution.py:73
  132.9 88.9 %while.37 = (s32[]{:T(128)}, f32[8,128,128]{1,2,0:T(8,128)S(1)}, f32[8,128,128]{1,2,0:T(8,128)S(1)}, f32[16,8,128,128]{3,2,0,1:T(8,128)}, f32[16,8,128,128]{3,2,0,1:T(8,128)}, /*index=5*/s32[]{:T(128)}, s32[]{:T(128)}) while((s32[]{:T(128)}, f32[8,128,128]{1,2,0:T(8,128)S(1)}, f32[8,128,128]{1,2,0:T(8,128)S(1)}, ...), condition=%wide.region_4.5_spmd.clone, body=%wide.region_3.4_spmd.clone.sunk | while | flops 402915328 | bytes 7865435 | solution.py:121
  223.9 2.1 reshape.140
  227.3 2.4 broadcast_multiply_fusion
  230.3 3.3 copy-done.3
  233.6 8.9 %bitcast_multiply_fusion.1 = f32[16,8,64,64]{3,2,0,1:T(8,128)} fusion(f32[8,16,64,128]{3,2,1,0:T(8,128)S(1)} %bitcast.196, f32[8,16,64,128]{3,2,1,0:T(8,128)S(1)} %bitcast.193, f32[16,8,64]{2,0,1:T(8,128)S(1)} %bitcast.201, f32[16,8,64]{2,0,1:T(8,128)S(1)} %bitcast.200, pred[64,64]{1,0:T(8,128)(4,1)S(1)} %iota_compare_fusion.1), kind=kOutput, calls=%fused_computation.61 | convolution fusion | flops 808452096 | bytes 10555392 | tf_op jit(solution)/shard_map/...ik,...jk->...ij/dot_general | solution.py:48
  242.5 72.3 %while.38 = (s32[]{:T(128)}, f32[8,128,128]{2,1,0:T(8,128)S(1)}, f32[8,128,128]{2,1,0:T(8,128)S(1)}, f32[8,128,128]{2,1,0:T(8,128)S(1)}, s32[]{:T(128)}, /*index=5*/s32[]{:T(128)}) while((s32[]{:T(128)}, f32[8,128,128]{2,1,0:T(8,128)S(1)}, f32[8,128,128]{2,1,0:T(8,128)S(1)}, f32[8,128,128]{2,1,0:T(8,128)S(1)}, s32[]{:T(128)}, ...), condition=%wide.region_6.7_spmd.clone, body=%wide.region_5.6_spmd.clone.sunk | while | flops 201850880 | bytes 3670135 | solution.py:129
  243.2 3.4 collective-permute-start
  246.6 7.4 %collective-permute-done = bf16[8,128,128]{2,1,0:T(8,128)(2,1)S(1)} collective-permute-done((bf16[8,128,128]{2,1,0:T(8,128)(2,1)S(1)}, bf16[8,128,128]{2,1,0:T(8,128)(2,1)S(1)}, u32[]{:S(2)}, u32[]{:S(2)}) %collective-permute-start) | collective-permute-done | bytes 262176 | tf_op jit(solution)/shard_map/while/body/eval_jaxpr/ppermute | solution.py:17
  254.8 2.5 collective-permute-start
  257.3 7.5 %collective-permute-done = bf16[8,128,128]{2,1,0:T(8,128)(2,1)S(1)} collective-permute-done((bf16[8,128,128]{2,1,0:T(8,128)(2,1)S(1)}, bf16[8,128,128]{2,1,0:T(8,128)(2,1)S(1)}, u32[]{:S(2)}, u32[]{:S(2)}) %collective-permute-start) | collective-permute-done | bytes 262176 | tf_op jit(solution)/shard_map/while/body/eval_jaxpr/ppermute | solution.py:17
  267.5 7.2 %collective-permute-done = bf16[8,128,128]{2,1,0:T(8,128)(2,1)S(1)} collective-permute-done((bf16[8,128,128]{2,1,0:T(8,128)(2,1)S(1)}, bf16[8,128,128]{2,1,0:T(8,128)(2,1)S(1)}, u32[]{:S(2)}, u32[]{:S(2)}) %collective-permute-start) | collective-permute-done | bytes 262176 | tf_op jit(solution)/shard_map/while/body/eval_jaxpr/ppermute | solution.py:17
  277.4 7.2 %collective-permute-done = bf16[8,128,128]{2,1,0:T(8,128)(2,1)S(1)} collective-permute-done((bf16[8,128,128]{2,1,0:T(8,128)(2,1)S(1)}, bf16[8,128,128]{2,1,0:T(8,128)(2,1)S(1)}, u32[]{:S(2)}, u32[]{:S(2)}) %collective-permute-start) | collective-permute-done | bytes 262176 | tf_op jit(solution)/shard_map/while/body/eval_jaxpr/ppermute | solution.py:17
  287.3 7.2 %collective-permute-done = bf16[8,128,128]{2,1,0:T(8,128)(2,1)S(1)} collective-permute-done((bf16[8,128,128]{2,1,0:T(8,128)(2,1)S(1)}, bf16[8,128,128]{2,1,0:T(8,128)(2,1)S(1)}, u32[]{:S(2)}, u32[]{:S(2)}) %collective-permute-start) | collective-permute-done | bytes 262176 | tf_op jit(solution)/shard_map/while/body/eval_jaxpr/ppermute | solution.py:17
  297.3 7.6 %collective-permute-done = bf16[8,128,128]{2,1,0:T(8,128)(2,1)S(1)} collective-permute-done((bf16[8,128,128]{2,1,0:T(8,128)(2,1)S(1)}, bf16[8,128,128]{2,1,0:T(8,128)(2,1)S(1)}, u32[]{:S(2)}, u32[]{:S(2)}) %collective-permute-start) | collective-permute-done | bytes 262176 | tf_op jit(solution)/shard_map/while/body/eval_jaxpr/ppermute | solution.py:17
  307.5 7.2 %collective-permute-done = bf16[8,128,128]{2,1,0:T(8,128)(2,1)S(1)} collective-permute-done((bf16[8,128,128]{2,1,0:T(8,128)(2,1)S(1)}, bf16[8,128,128]{2,1,0:T(8,128)(2,1)S(1)}, u32[]{:S(2)}, u32[]{:S(2)}) %collective-permute-start) | collective-permute-done | bytes 262176 | tf_op jit(solution)/shard_map/while/body/eval_jaxpr/ppermute | solution.py:17
  314.8 159.8 %while.36 = (s32[]{:T(128)}, f32[8,128,128]{2,1,0:T(8,128)S(1)}, f32[16,8,64,128]{3,2,1,0:T(8,128)}, f32[16,8]{1,0:T(8,128)S(1)}, f32[16,8,64]{2,0,1:T(8,128)S(1...) while((s32[]{:T(128)}, f32[8,128,128]{2,1,0:T(8,128)S(1)}, ...), condition=%wide.region_9.10_spmd, body=%wide.region_8.9_spmd.sunk | while | flops 403243008 | bytes 6045917 | solution.py:135
  320.4 2.1 fusion.152
  322.5 2.2 convolution_add_fusion.4
  330.4 2.1 fusion.152
  332.5 2.2 convolution_add_fusion.4
  340.4 2.1 fusion.152
  342.5 2.2 convolution_add_fusion.4
  350.4 2.2 fusion.152
  352.5 2.2 convolution_add_fusion.4
  360.4 2.1 fusion.152
  362.5 2.2 convolution_add_fusion.4
  372.4 2.2 convolution_add_fusion.4
  382.4 2.2 convolution_add_fusion.4
  390.2 2.1 fusion.152
  392.4 2.2 convolution_add_fusion.4
  400.2 2.2 fusion.152
  402.4 2.2 convolution_add_fusion.4
  410.2 2.1 fusion.152
  412.4 2.2 convolution_add_fusion.4
  420.2 2.1 fusion.152
  422.3 2.2 convolution_add_fusion.4
  430.2 2.1 fusion.152
  432.3 2.2 convolution_add_fusion.4
  442.3 2.2 convolution_add_fusion.4
  450.1 2.1 fusion.152
  452.2 2.2 convolution_add_fusion.4
  462.2 2.2 convolution_add_fusion.4
  470.0 2.1 fusion.152
  472.2 2.2 convolution_add_fusion.4
  474.6 3.3 multiply_reduce_fusion
  478.2 5.6 %copy.84 = f32[16,64,8,128]{3,2,1,0:T(8,128)S(1)} copy(f32[16,64,8,128]{3,1,2,0:T(8,128)} %bitcast.199) | data formatting | bytes 8388608 | tf_op jit(solution)/shard_map/transpose;transpose | solution.py:137
  486.0 6.9 %convert_bitcast_fusion.1 = bf16[2048,1024]{0,1:T(8,128)(2,1)} fusion(bf16[1024,2048]{1,0:T(8,128)(2,1)S(1)} %copy-done.15, bf16[1024,1024]{1,0:T(8,128)(2,1)S(1)} %copy-done.16, f32[128,8,8,128]{3,2,1,0:T(8,128)S(1)} %bitcast.202, f32[128,8,8,128]{3,2,1,0:T(8,128)S(1)} %bitcast.203, f32[1024]{0:T(1024)S(1)} %broadcast_bitcast_fusion), kind=kOutput, calls=%fused_computation.66 | convolution fusion | flops 4306501632 | bytes 18878464 | tf_op jit(solution)/shard_map/dot_general | solution.py:143
  492.9 44.9 %reduce-scatter.2.cloned.1.call-done = bf16[512,1024]{0,1:T(8,128)(2,1)} async-done(((bf16[2048,1024]{0,1:T(8,128)(2,1)}), bf16[512,1024]{0,1:T(8,128)(2,1)}) %reduce-scatter.2.cloned.1.call-update) | async-done | bytes 1048592 | tf_op jit(solution)/shard_map/reduce_scatter | solution.py:142
  (272 shorter events, 216.1 us)
Async XLA Ops:
  6.5 477.3 %copy-start = (f32[128]{0:T(128)S(1)}, f32[128]{0:T(128)}, u32[]{:S(2)}) copy-start(f32[128]{0:T(128)} %param.22) | copy-start | bytes 1540
  6.5 531.3 %reduce-scatter.2.cloned.1.call-start = ((), (), s32[]{:S(2)}) async-start(), calls=%async_computation.1 | async-start | bytes 5242880 | tf_op jit(solution)/shard_map/reduce_scatter | solution.py:142
  9.6 2.6 copy-start.14
  9.6 2.7 copy-start.12
  9.6 6.6 %copy-start.13 = (f32[8,1024]{1,0:T(8,128)S(1)}, f32[8,1024]{1,0:T(8,128)}, u32[]{:S(2)}) copy-start(f32[8,1024]{1,0:T(8,128)} %param.19) | copy-start | bytes 98308
  16.5 9.2 %copy-start.9 = (f32[8,16]{1,0:T(8,128)}, f32[8,16]{1,0:T(8,128)S(1)}, u32[]{:S(2)}) copy-start(f32[8,16]{1,0:T(8,128)S(1)} %get-tuple-element.276) | copy-start | bytes 1540
  17.5 71.2 %copy-start.1 = (f32[1024,4,2,128]{3,0,2,1:T(8,128)}, f32[1024,4,2,128]{3,0,2,1:T(8,128)S(1)}, u32[]{:S(2)}) copy-start(f32[1024,4,2,128]{3,0,2,1:T(8,128)S(1)} %broadcast_in_dim.28) | copy-start | bytes 12582916
  70.4 5.4 copy-start.8
  88.7 5.9 %copy-start.11 = (f32[16,8]{0,1:T(8,128)S(1)}, f32[16,8]{0,1:T(8,128)}, u32[]{:S(2)}) copy-start(f32[16,8]{0,1:T(8,128)} %select_bitcast_fusion) | copy-start | bytes 1540
  94.7 19.8 %copy-start.2 = (f32[1024,4,2,128]{3,0,2,1:T(8,128)S(1)}, f32[1024,4,2,128]{3,0,2,1:T(8,128)}, u32[]{:S(2)}) copy-start(f32[1024,4,2,128]{3,0,2,1:T(8,128)} %copy-done.1) | copy-start | bytes 12582916
  94.7 19.8 %copy-start.4 = (f32[8,16,64,128]{3,2,1,0:T(8,128)S(1)}, f32[8,16,64,128]{3,2,1,0:T(8,128)}, u32[]{:S(2)}) copy-start(f32[8,16,64,128]{3,2,1,0:T(8,128)} %fusion.52) | copy-start | bytes 12582916
  227.3 2.6 copy-start.10
  229.9 3.7 copy-start.3
  230.3 12.2 %copy-start.5 = (f32[1024,4,2,128]{3,0,2,1:T(8,128)}, f32[1024,4,2,128]{3,0,2,1:T(8,128)S(1)}, u32[]{:S(2)}) copy-start(f32[1024,4,2,128]{3,0,2,1:T(8,128)S(1)} %broadcast_in_dim.31) | copy-start | bytes 12582916
  233.6 8.9 %copy-start.6 = (f32[8,128,128]{2,1,0:T(8,128)S(1)}, f32[8,128,128]{2,1,0:T(8,128)}, u32[]{:S(2)}) copy-start(f32[8,128,128]{2,1,0:T(8,128)} %copy.73) | copy-start | bytes 1572868
  233.6 8.9 %copy-start.7 = (f32[8,128,128]{2,1,0:T(8,128)S(1)}, f32[8,128,128]{2,1,0:T(8,128)}, u32[]{:S(2)}) copy-start(f32[8,128,128]{2,1,0:T(8,128)} %copy.74) | copy-start | bytes 1572868
  243.2 10.8 %collective-permute-start = (bf16[8,128,128]{2,1,0:T(8,128)(2,1)S(1)}, bf16[8,128,128]{2,1,0:T(8,128)(2,1)S(1)}, u32[]{:S(2)}, u32[]{:S(2)}) collective-permute-start(bf16[8,128,128]{2,1,0:T(8,128)(2,1)S(1)} %fusion.160), channel_id=1, source_target_pairs={{0,4},{4,8},{8,12},{12,16},{16,20},{20,24},{24,28},{1,5},{5,9},{9,... | collective-permute-start | bytes 786440 | tf_op jit(solution)/shard_map/while/body/eval_jaxpr/ppermute | solution.py:17
  254.8 10.0 %collective-permute-start = (bf16[8,128,128]{2,1,0:T(8,128)(2,1)S(1)}, bf16[8,128,128]{2,1,0:T(8,128)(2,1)S(1)}, u32[]{:S(2)}, u32[]{:S(2)}) collective-permute-start(bf16[8,128,128]{2,1,0:T(8,128)(2,1)S(1)} %fusion.160), channel_id=1, source_target_pairs={{0,4},{4,8},{8,12},{12,16},{16,20},{20,24},{24,28},{1,5},{5,9},{9,... | collective-permute-start | bytes 786440 | tf_op jit(solution)/shard_map/while/body/eval_jaxpr/ppermute | solution.py:17
  265.6 9.2 %collective-permute-start = (bf16[8,128,128]{2,1,0:T(8,128)(2,1)S(1)}, bf16[8,128,128]{2,1,0:T(8,128)(2,1)S(1)}, u32[]{:S(2)}, u32[]{:S(2)}) collective-permute-start(bf16[8,128,128]{2,1,0:T(8,128)(2,1)S(1)} %fusion.160), channel_id=1, source_target_pairs={{0,4},{4,8},{8,12},{12,16},{16,20},{20,24},{24,28},{1,5},{5,9},{9,... | collective-permute-start | bytes 786440 | tf_op jit(solution)/shard_map/while/body/eval_jaxpr/ppermute | solution.py:17
  275.5 9.2 %collective-permute-start = (bf16[8,128,128]{2,1,0:T(8,128)(2,1)S(1)}, bf16[8,128,128]{2,1,0:T(8,128)(2,1)S(1)}, u32[]{:S(2)}, u32[]{:S(2)}) collective-permute-start(bf16[8,128,128]{2,1,0:T(8,128)(2,1)S(1)} %fusion.160), channel_id=1, source_target_pairs={{0,4},{4,8},{8,12},{12,16},{16,20},{20,24},{24,28},{1,5},{5,9},{9,... | collective-permute-start | bytes 786440 | tf_op jit(solution)/shard_map/while/body/eval_jaxpr/ppermute | solution.py:17
  285.4 9.2 %collective-permute-start = (bf16[8,128,128]{2,1,0:T(8,128)(2,1)S(1)}, bf16[8,128,128]{2,1,0:T(8,128)(2,1)S(1)}, u32[]{:S(2)}, u32[]{:S(2)}) collective-permute-start(bf16[8,128,128]{2,1,0:T(8,128)(2,1)S(1)} %fusion.160), channel_id=1, source_target_pairs={{0,4},{4,8},{8,12},{12,16},{16,20},{20,24},{24,28},{1,5},{5,9},{9,... | collective-permute-start | bytes 786440 | tf_op jit(solution)/shard_map/while/body/eval_jaxpr/ppermute | solution.py:17
  295.3 9.5 %collective-permute-start = (bf16[8,128,128]{2,1,0:T(8,128)(2,1)S(1)}, bf16[8,128,128]{2,1,0:T(8,128)(2,1)S(1)}, u32[]{:S(2)}, u32[]{:S(2)}) collective-permute-start(bf16[8,128,128]{2,1,0:T(8,128)(2,1)S(1)} %fusion.160), channel_id=1, source_target_pairs={{0,4},{4,8},{8,12},{12,16},{16,20},{20,24},{24,28},{1,5},{5,9},{9,... | collective-permute-start | bytes 786440 | tf_op jit(solution)/shard_map/while/body/eval_jaxpr/ppermute | solution.py:17
  305.6 9.2 %collective-permute-start = (bf16[8,128,128]{2,1,0:T(8,128)(2,1)S(1)}, bf16[8,128,128]{2,1,0:T(8,128)(2,1)S(1)}, u32[]{:S(2)}, u32[]{:S(2)}) collective-permute-start(bf16[8,128,128]{2,1,0:T(8,128)(2,1)S(1)} %fusion.160), channel_id=1, source_target_pairs={{0,4},{4,8},{8,12},{12,16},{16,20},{20,24},{24,28},{1,5},{5,9},{9,... | collective-permute-start | bytes 786440 | tf_op jit(solution)/shard_map/while/body/eval_jaxpr/ppermute | solution.py:17
  478.2 6.8 %copy-start.16 = (bf16[1024,1024]{1,0:T(8,128)(2,1)S(1)}, bf16[1024,1024]{1,0:T(8,128)(2,1)}, u32[]{:S(2)}) copy-start(bf16[1024,1024]{1,0:T(8,128)(2,1)} %param.18) | copy-start | bytes 6291460
  483.8 2.2 copy-start.15
Sparse Core Ops, SparseCore 0:
  493.0 44.7 reduce-scatter.1
where the time goes:
time: 554 us; the launch traced here: 545 us
  matrix products  359 us (65%)
  waiting for transfers between devices  96.4 us (17%)
  local copies, waits for them, and re-layouts  41.7 us (8%)
  other arithmetic  16 us (3%)
  starting transfers between devices  15.5 us (3%)
  between operations  14.1 us (3%)
    ppermute x7, waiting for transfers between devices, shifted(): return lax.ppermute(block, axis, route)  51.4 us
    reduce_scatter x1, waiting for transfers between devices, local(): lax.psum_scatter(lax.dot_general(out_weight, normed, (((0,), (1,)), ((),...  44.9 us
    dot_general x16, matrix products, block_step(): jnp.einsum('...cv,...ck->...vk', tail_keep[..., None] * fresh_vals, keys,...  35.9 us
    dot_general x16, matrix products, block_step(): output = terms + jnp.matmul(scores, write_vals, precision=highest)  34.1 us
    dot_general x16, matrix products, state_terms(): seen = jnp.einsum('...ck,...vk->...cv', queries, states, precision=highest)  33.4 us
    dot_general x16, matrix products, state_terms(): jnp.einsum('...ck,...vk->...cv', erase_keys, states, precision=highest)  33.4 us
    dot_general x16, matrix products, fold_blocks(): next_move = jnp.matmul(total_move, move_now, precision=highest)  33.2 us
    dot_general x16, matrix products, fold_blocks(): jnp.matmul(total_state, move_now, precision=highest) + carried_now  33 us
  transfers between devices with their start and end apart: 8, of which 8 were waited for; matrix products, arithmetic and copies ran while one was open for 0% of the time, Pallas kernels for 0%

commit v1 on v0

v1 whole, which is shorter than its diff:
```python
import functools

import jax
import jax.numpy as jnp
from jax import lax
from jax.experimental import pallas as pl
from jax.experimental.pallas import tpu as pltpu
from jax.sharding import PartitionSpec as P

DK = 128
DV = 128
BLK = 128
EPS = 1e-06
FAR = -1e30
F32 = jnp.float32
BF16 = jnp.bfloat16
MIB = 1024 * 1024


def dot(a, b):
    return jnp.dot(a, b, preferred_element_type=F32)


def dot_t(a, b):
    return lax.dot_general(a, b, (((1,), (1,)), ((), ())), preferred_element_type=F32)


def running_sum(values):
    lane = lax.broadcasted_iota(jnp.int32, values.shape, 1)
    step = 1
    while step < BLK:
        values = values + jnp.where(lane >= step, pltpu.roll(values, step, 1), 0.0)
        step *= 2
    return values


def columns_of(rows):
    pad = BLK - rows.shape[0]
    return jnp.transpose(jnp.concatenate([rows, jnp.zeros((pad, BLK), F32)], axis=0))


def doc_mask(reset_col, reset_row, strict):
    i = lax.broadcasted_iota(jnp.int32, (BLK, BLK), 0)
    j = lax.broadcasted_iota(jnp.int32, (BLK, BLK), 1)
    below = (i > j) if strict else (i >= j)
    return jnp.where(below & (reset_col == reset_row), 0.0, FAR)


def merge_masks():
    i = lax.broadcasted_iota(jnp.int32, (BLK, BLK), 0)
    j = lax.broadcasted_iota(jnp.int32, (BLK, BLK), 1)
    masks = []
    size = 1
    while size < BLK:
        same_pair = (i // (2 * size)) == (j // (2 * size))
        masks.append(same_pair & ((i // size) % 2 == 1) & ((j // size) % 2 == 0))
        size *= 2
    return masks, i == j


def shard_kernel(
    per_key, blocks, keys_here,
    log_ref, rate_ref, start_ref, k_ref, v_ref,
    wu_ref, zc_ref, rows_ref, end_ref,
    logs, rates, norms, kt, mask, db, keep, state,
):
    key = pl.program_id(0)
    count = per_key * blocks
    for k in range(keys_here):

        @pl.when(key == k)
        def _():
            for h in range(per_key):
                head = k * per_key + h
                for c in range(blocks):
                    at = h * blocks + c
                    span = slice(c * BLK, (c + 1) * BLK)
                    logs[at : at + 1, :] = log_ref[head : head + 1, span]
                    rates[at : at + 1, :] = rate_ref[head : head + 1, span]

    starts = start_ref[...].astype(F32)
    sums = running_sum(jnp.concatenate([logs[...], starts], axis=0))
    cum, reset = sums[:count], sums[count:]

    for c in range(blocks):
        flipped = jnp.transpose(k_ref[c * BLK : (c + 1) * BLK, :].astype(F32))
        kt[c] = flipped.astype(BF16)
        norms[c : c + 1, :] = jnp.sum(flipped * flipped, axis=0, keepdims=True)

    @pl.when(key == 0)
    def _():
        reset_cols = columns_of(reset)
        for c in range(blocks):
            mask[c] = doc_mask(reset_cols[:, c : c + 1], reset[c : c + 1, :], True)

    scale = lax.rsqrt(norms[...] + EPS)
    log_scale = jnp.concatenate([-0.5 * jnp.log(norms[...] + EPS)] * per_key, axis=0)
    scale = jnp.concatenate([scale] * per_key, axis=0)
    resets = jnp.concatenate([reset] * per_key, axis=0)
    rate = rates[...]
    last = cum[:, BLK - 1 :]
    last_reset = resets[:, BLK - 1 :]
    left_cols = columns_of(cum + jnp.log(rate) + log_scale)
    right = cum - log_scale
    head_keep = jnp.where(resets == 0.0, jnp.exp(cum), 0.0)
    tail = jnp.where(resets == last_reset, jnp.exp(last - cum), 0.0) * scale
    erase_row = rate * head_keep * scale
    whole = jnp.where(last_reset == 0.0, jnp.exp(last), 0.0)
    whole = jnp.broadcast_to(whole, (count, BLK))
    for at in range(count):
        keep[key * count + at] = whole[at : at + 1, :]
    rows_ref[0, 0:count, :] = cum
    rows_ref[0, count : 2 * count, :] = right
    rows_ref[0, 2 * count :, :] = reset

    masks, diag = merge_masks()
    inner = [dot(k_ref[c * BLK : (c + 1) * BLK, :], kt[c]) for c in range(blocks)]
    lower = []
    for at in range(count):
        c = at % blocks
        gap = left_cols[:, at : at + 1] - right[at : at + 1, :] + mask[c]
        lower.append(inner[c] * jnp.exp(gap))
    inverse = [jnp.where(diag, 1.0, 0.0) - jnp.where(masks[0], m, 0.0) for m in lower]
    lower = [m.astype(BF16) for m in lower]
    for level in masks[1:]:
        edge = [jnp.where(level, m, jnp.zeros_like(m)) for m in lower]
        now = [t.astype(BF16) for t in inverse]
        half = [dot(t, e).astype(BF16) for t, e in zip(now, edge)]
        inverse = [t - dot(f, b) for t, f, b in zip(inverse, half, now)]
    for at in range(count):
        c, h = at % blocks, at // blocks
        span = slice(c * BLK, (c + 1) * BLK)
        t = inverse[at]
        erase = dot((t * erase_row[at : at + 1, :]).astype(BF16), k_ref[span, :])
        write = dot((t * rate[at : at + 1, :]).astype(BF16), v_ref[span, h * DV : (h + 1) * DV])
        wu_ref[at, :, :DK] = erase.astype(BF16)
        wu_ref[at, :, DK:] = write.astype(BF16)
    for at in range(count):
        c = at % blocks
        tailed = (kt[c].astype(F32) * tail[at : at + 1, :]).astype(BF16)
        db[key * count + at] = dot(tailed, wu_ref[at]).astype(BF16)

    @pl.when(key == keys_here - 1)
    def _():
        heads_here = per_key * keys_here
        i = lax.broadcasted_iota(jnp.int32, (DK, DK), 0)
        j = lax.broadcasted_iota(jnp.int32, (DK, DK), 1)
        for h in range(heads_here):
            state[h, :, :DV] = jnp.zeros((DK, DV), F32)
            state[h, :, DV:] = jnp.where(i == j, 1.0, 0.0)

        def advance(c, carry):
            for h in range(heads_here):
                now = state[h]
                low = now.astype(BF16)
                zc_ref[h, c] = low
                at = h * blocks + c
                moved = dot(db[at, :, :DK], low)
                g = keep[at]
                state[h, :, :DV] = g * now[:, :DV] - moved[:, :DV] + db[at, :, DK:].astype(F32)
                state[h, :, DV:] = g * now[:, DV:] - moved[:, DV:]
            return carry

        lax.fori_loop(0, blocks, advance, 0)
        for h in range(heads_here):
            end_ref[h] = state[h].astype(BF16)


def shard_pass(log_gate, write_rate, starts, key_rows, value_rows, per_key):
    tokens_here = key_rows.shape[0]
    keys_here = key_rows.shape[1] // DK
    heads_here = keys_here * per_key
    blocks = tokens_here // BLK
    count = per_key * blocks
    wide = DK + DV
    whole = lambda *shape: pl.BlockSpec(shape, lambda key: (0,) * len(shape))
    return pl.pallas_call(
        functools.partial(shard_kernel, per_key, blocks, keys_here),
        grid=(keys_here,),
        in_specs=[
            whole(heads_here, tokens_here),
            whole(heads_here, tokens_here),
            whole(blocks, BLK),
            pl.BlockSpec((tokens_here, DK), lambda key: (0, key)),
            pl.BlockSpec((tokens_here, per_key * DV), lambda key: (0, key)),
        ],
        out_specs=[
            pl.BlockSpec((count, BLK, wide), lambda key: (key, 0, 0)),
            whole(heads_here, blocks, DK, wide),
            pl.BlockSpec((1, 2 * count + blocks, BLK), lambda key: (key, 0, 0)),
            whole(heads_here, DK, wide),
        ],
        out_shape=[
            jax.ShapeDtypeStruct((keys_here * count, BLK, wide), BF16),
            jax.ShapeDtypeStruct((heads_here, blocks, DK, wide), BF16),
            jax.ShapeDtypeStruct((keys_here, 2 * count + blocks, BLK), F32),
            jax.ShapeDtypeStruct((heads_here, DK, wide), BF16),
        ],
        scratch_shapes=[
            pltpu.VMEM((count, BLK), F32),
            pltpu.VMEM((count, BLK), F32),
            pltpu.VMEM((blocks, BLK), F32),
            pltpu.VMEM((blocks, DK, BLK), BF16),
            pltpu.VMEM((blocks, BLK, BLK), F32),
            pltpu.VMEM((keys_here * count, DK, wide), BF16),
            pltpu.VMEM((keys_here * count, 1, BLK), F32),
            pltpu.VMEM((heads_here, DK, wide), F32),
        ],
        compiler_params=pltpu.CompilerParams(vmem_limit_bytes=48 * MIB),
        cost_estimate=pl.CostEstimate(
            flops=keys_here * count * 18 * 2 * BLK**3, bytes_accessed=12 * MIB, transcendentals=0
        ),
        name="shard_pass",
    )(log_gate, write_rate, starts, key_rows, value_rows)


def local_kernel(per_key, blocks, rows_ref, q_ref, k_ref, wu_ref, zc_ref, out_ref, carry_ref):
    count = per_key * blocks
    cum = rows_ref[0, 0:count, :]
    right = rows_ref[0, count : 2 * count, :]
    reset = rows_ref[0, 2 * count :, :]
    cols = columns_of(jnp.concatenate([cum, reset], axis=0))
    units, inner, masks = [], [], []
    for c in range(blocks):
        span = slice(c * BLK, (c + 1) * BLK)
        query = q_ref[span, :].astype(F32)
        units.append(jnp.sum(query * query, axis=1, keepdims=True) + EPS)
        inner.append(dot_t(q_ref[span, :], k_ref[span, :]))
        masks.append(doc_mask(cols[:, count + c : count + c + 1], reset[c : c + 1, :], False))
    scores = []
    for at in range(count):
        c = at % blocks
        left = cols[:, at : at + 1] - 0.5 * jnp.log(units[c])
        gap = left - right[at : at + 1, :] + masks[c]
        scores.append((inner[c] * jnp.exp(gap)).astype(BF16))
    seen = [dot(scores[at], wu_ref[at]) for at in range(count)]
    for at in range(count):
        c, h = at % blocks, at // blocks
        span = slice(c * BLK, (c + 1) * BLK)
        reset_col = cols[:, count + c : count + c + 1]
        keep = jnp.where(reset_col == 0.0, jnp.exp(cols[:, at : at + 1]), 0.0) * lax.rsqrt(units[c])
        g = (keep * q_ref[span, :].astype(F32) - seen[at][:, :DK]).astype(BF16)
        both = dot(g, zc_ref[h, c])
        out_ref[span, h * DV : (h + 1) * DV] = both[:, :DV] + seen[at][:, DK:]
        carry_ref[span, h * DK : (h + 1) * DK] = both[:, DV:].astype(BF16)


def local_pass(key, rows, queries, key_rows, wu, zc, per_key):
    tokens_here = queries.shape[0]
    blocks = tokens_here // BLK
    count = per_key * blocks
    wide = DK + DV
    return pl.pallas_call(
        functools.partial(local_kernel, per_key, blocks),
        grid=(1,),
        in_specs=[
            pl.BlockSpec((1, 2 * count + blocks, BLK), lambda i: (key, 0, 0)),
            pl.BlockSpec((tokens_here, DK), lambda i: (0, key)),
            pl.BlockSpec((tokens_here, DK), lambda i: (0, key)),
            pl.BlockSpec((count, BLK, wide), lambda i: (key, 0, 0)),
            pl.BlockSpec((per_key, blocks, DK, wide), lambda i: (key, 0, 0, 0)),
        ],
        out_specs=[
            pl.BlockSpec((tokens_here, per_key * DV), lambda i: (0, 0)),
            pl.BlockSpec((tokens_here, per_key * DK), lambda i: (0, 0)),
        ],
        out_shape=[
            jax.ShapeDtypeStruct((tokens_here, per_key * DV), F32),
            jax.ShapeDtypeStruct((tokens_here, per_key * DK), BF16),
        ],
        compiler_params=pltpu.CompilerParams(vmem_limit_bytes=32 * MIB),
        cost_estimate=pl.CostEstimate(
            flops=count * 8 * 2 * BLK**3, bytes_accessed=4 * MIB, transcendentals=0
        ),
        name="local_pass",
    )(rows, queries, key_rows, wu, zc)


def finish_kernel(
    per_key, keys_here, sends, order,
    me_ref, *refs,
):
    outs = refs[:keys_here]
    carries = refs[keys_here : 2 * keys_here]
    start_ref, gate_ref, gain_ref, weight_ref, send_ref, keep_ref, normed = refs[2 * keys_here :]
    step = pl.program_id(0)

    @pl.when(step == 0)
    def _():
        for key in range(keys_here):
            for h in range(per_key):
                head = key * per_key + h
                span = slice(h * DV, (h + 1) * DV)
                wide = slice(head * DV, (head + 1) * DV)
                seen = outs[key][:, span] + dot(carries[key][:, span], start_ref[head])
                spread = jnp.mean(seen * seen, axis=1, keepdims=True)
                gate = gate_ref[:, wide].astype(F32)
                gated = gain_ref[...] * (gate / (1.0 + jnp.exp(-gate)))
                normed[:, wide] = (seen * lax.rsqrt(spread + EPS) * gated).astype(BF16)

    part = dot(normed[...], weight_ref[...]).astype(BF16)

    @pl.when(step < sends)
    def _():
        send_ref[...] = part

    @pl.when(step >= sends)
    def _():
        keep_ref[...] = part


def bit_reversed(size):
    order = [0]
    bit = 1
    while bit < size:
        order = [p for p in order] + [p | bit for p in order]
        bit *= 2
    half = size // 2
    reach = []

    def split(group, bit):
        if len(group) == 1:
            return group
        return split([p for p in group if not p & bit], 2 * bit) + split(
            [p for p in group if p & bit], 2 * bit
        )

    return split(list(range(size)), 1)


def finish_pass(index, rows, me, outs, carries, start, out_gate, gain, weight, per_key, groups):
    heads_here = out_gate.shape[1] // DV
    keys_here = len(outs)
    columns = weight.shape[1] // groups
    order = bit_reversed(groups)
    half = groups // 2
    order = order[half:] + order[:half]

    def column_of(step, me_ref):
        place = order[0]
        for at in range(1, groups):
            place = jnp.where(step == at, order[at], place)
        return (0, me_ref[0] ^ place)

    per_head = pl.BlockSpec((rows, per_key * DV), lambda step, me_ref: (index, 0))
    grid_spec = pltpu.PrefetchScalarGridSpec(
        num_scalar_prefetch=1,
        grid=(groups,),
        in_specs=[per_head] * (2 * keys_here)
        + [
            pl.BlockSpec((heads_here, DK, DV), lambda step, me_ref: (0, 0, 0)),
            pl.BlockSpec((rows, heads_here * DV), lambda step, me_ref: (index, 0)),
            pl.BlockSpec((1, DV), lambda step, me_ref: (0, 0)),
            pl.BlockSpec((weight.shape[0], columns), column_of),
        ],
        out_specs=[
            pl.BlockSpec((rows, columns), lambda step, me_ref: (0, jnp.minimum(step, half - 1))),
            pl.BlockSpec((rows, columns), lambda step, me_ref: (0, jnp.maximum(step - half, 0))),
        ],
        scratch_shapes=[pltpu.VMEM((rows, heads_here * DV), BF16)],
    )
    return pl.pallas_call(
        functools.partial(finish_kernel, per_key, keys_here, half, order),
        grid_spec=grid_spec,
        out_shape=[jax.ShapeDtypeStruct((rows, half * columns), BF16)] * 2,
        compiler_params=pltpu.CompilerParams(vmem_limit_bytes=32 * MIB),
        cost_estimate=pl.CostEstimate(
            flops=2 * rows * weight.shape[0] * weight.shape[1],
            bytes_accessed=8 * MIB,
            transcendentals=0,
        ),
        name="finish_pass",
    )(me, *outs, *carries, start, out_gate, gain, weight)


def compose_kernel(wide, later_ref, earlier_ref, out_ref):
    for h in range(later_ref.shape[0]):
        later = later_ref[h]
        moved = dot(later[:, DV:], earlier_ref[h])
        out_ref[h, :, :DV] = (moved[:, :DV] + later[:, :DV].astype(F32)).astype(BF16)
        if wide:
            out_ref[h, :, DV:] = moved[:, DV:].astype(BF16)


def compose(later, earlier):
    return pl.pallas_call(
        functools.partial(compose_kernel, earlier.shape[2] > DV),
        out_shape=jax.ShapeDtypeStruct(earlier.shape, BF16),
        cost_estimate=pl.CostEstimate(
            flops=2 * earlier.size * DK, bytes_accessed=4 * earlier.size, transcendentals=0
        ),
        name="compose",
    )(later, earlier)


def route(axis, target):
    size = lax.axis_size(axis)
    return [(i, target(i)) for i in range(size) if target(i) is not None]


def start_states(end, work):
    size = lax.axis_size("seq")
    heads = end.shape[0]
    me = lax.axis_index("seq")
    if size == 8 and heads % 2 == 0:
        half = heads // 2
        odd = me % 2 == 1
        pair = me // 2
        mine = jnp.where(odd, end[half:], end[:half])
        theirs = jnp.where(odd, end[:half], end[half:])
        got = lax.ppermute(theirs, "seq", route("seq", lambda i: i ^ 1))
        mine, got = work(mine, got)
        first = jnp.where(odd, got, mine)
        second = jnp.where(odd, mine, got)
        both = compose(second, first)
        before = lax.ppermute(both, "seq", route("seq", lambda i: i + 2 if i < 6 else None))
        both, before = work(both, before)
        third = compose(both, before[:, :, :DV])
        near = lax.ppermute(third, "seq", [(2, 4), (3, 5)])
        far = lax.ppermute(third, "seq", [(2, 6), (3, 7)])
        before, (near, far) = work(before, (near, far))
        here = jnp.where(pair == 2, near, compose(before, far))
        then = compose(first, here)
        own = jnp.where(odd, then, here)
        other = jnp.where(odd, here, then)
        back = lax.ppermute(other, "seq", route("seq", lambda i: i ^ 1))
        own, back = work(own, back)
        return jnp.concatenate(
            [jnp.where(odd, back, own), jnp.where(odd, own, back)], axis=0
        )

    def hop(step, state):
        return lax.ppermute(
            compose(end, state), "seq", route("seq", lambda i: i + 1 if i + 1 < size else None)
        )

    return lax.fori_loop(0, size - 1, hop, jnp.zeros((heads, DK, DV), BF16))


def local(
    queries, key_rows, value_rows, out_gate, write_rate, log_gate, doc_start, norm_gain, out_weight
):
    tokens_here = queries.shape[0]
    heads_here = value_rows.shape[1] // DV
    keys_here = key_rows.shape[1] // DK
    per_key = heads_here // keys_here
    groups = lax.axis_size("head")
    starts = doc_start.reshape(tokens_here // BLK, BLK)
    wu, zc, rows, end = shard_pass(
        log_gate, write_rate, starts, key_rows, value_rows, per_key
    )
    outs, carries = [], []

    def work(ready, coming):
        key = len(outs)
        if key < keys_here:
            held, ready = lax.optimization_barrier((rows, ready))
            out, carry = local_pass(key, held, queries, key_rows, wu, zc, per_key)
            outs.append(out)
            carries.append(carry)
        return ready, coming

    start = start_states(end, work)
    while len(outs) < keys_here:
        work(start, start)

    me = lax.axis_index("head").reshape(1).astype(jnp.int32)
    chunks = 4
    rows_each = tokens_here // chunks
    pieces = []
    for index in range(chunks):
        send, keep = finish_pass(
            index, rows_each, me, outs, carries, start, out_gate,
            norm_gain.reshape(1, DV), out_weight, per_key, groups,
        )
        bit = 1
        while bit < groups:
            got = lax.ppermute(send, "head", route("head", lambda i: i ^ bit))
            total = keep.astype(F32) + got.astype(F32)
            bit *= 2
            if bit < groups:
                width = total.shape[1] // 2
                keep = total[:, :width]
                send = total[:, width:].astype(BF16)
            else:
                keep = total
        pieces.append(keep.astype(BF16))
    return jnp.concatenate(pieces, axis=0)


def solution(mesh):
    placed = (
        P("seq", "head"),
        P("seq", "head"),
        P("seq", "head"),
        P("seq", "head"),
        P("head", "seq"),
        P("head", "seq"),
        P("seq"),
        P(),
        P("head", None),
    )
    return jax.shard_map(
        local, mesh=mesh, in_specs=placed, out_specs=P("seq", "head"), check_vma=False
    )
```

time: 554 us -> 121 us (0.22); the launches traced: 545 us -> 120 us
  matrix products: 359 us -> 0 us
  waiting for transfers between devices: 96.4 us -> 32.3 us
  Pallas kernels: 0 us -> 46.6 us
  local copies, waits for them, and re-layouts: 41.7 us -> 16.6 us
  between operations: 14.1 us -> 0.26 us
  other arithmetic: 16 us -> 5.5 us
    dot_general x136 -> x0, matrix products: 359 us -> none  [the longest x16 35.9 us: block_step(): jnp.einsum('...cv,...ck->...vk', tail_keep[..., None] * fresh_vals, keys,...]
    pallas_call x0 -> x13, Pallas kernels: none -> 46.6 us  [the longest x1 19.9 us: shard_pass(): pl.pallas_call(functools.partial(shard_kernel, per_key, blocks, keys_here...]
    reduce_scatter x1 -> x0, waiting for transfers between devices: 44.9 us -> none  [local(): lax.psum_scatter(lax.dot_general(out_weight, normed, (((0,), (1,)), ((),...]
    dynamic_slice x48 -> x0, local copies, waits for them, and re-layouts: 20.7 us -> none  [the longest x32 20.5 us: local(): lax.scan(fold_blocks, (eye_heads, empty), (blocks_first(moves), blocks_fi...]
    ppermute x7 -> x13, waiting for transfers between devices: 51.4 us -> 32.3 us  [the longest x8 20 us: local(): got = lax.ppermute(send, 'head', route('head', lambda i: i ^ bit))]
    unnamed x37 -> x34, local copies, waits for them, and re-layouts: 7.44 us -> 15.7 us
    reduce_sum x3 -> x0, other arithmetic: 5.64 us -> none  [the longest x1 3.34 us: local(): jnp.mean(attended * attended, axis=-1, keepdims=True) + 1e-06]
    mul x5 -> x0, other arithmetic: 5.64 us -> none  [the longest x2 4.84 us: unit_rows(): values * lax.rsqrt(jnp.sum(values * values, axis=-1, keepdims=True) + 1e-06)]
  transfers between devices with their start and end apart: 8 -> 13, of which waited for: 8 -> 6; matrix products, arithmetic and copies ran while one was open for 0% -> 1% of each run, Pallas kernels for 0% -> 15%
where the time goes in v1:
time: 121 us; the launch traced here: 120 us
  Pallas kernels  46.6 us (39%)
  waiting for transfers between devices  32.3 us (27%)
  starting transfers between devices  19.2 us (16%)
  local copies, waits for them, and re-layouts  16.6 us (14%)
  other arithmetic  5.5 us (5%)
    ppermute x8, waiting for transfers between devices, local(): got = lax.ppermute(send, 'head', route('head', lambda i: i ^ bit))  20 us
    pallas_call x1, Pallas kernels, shard_pass(): pl.pallas_call(functools.partial(shard_kernel, per_key, blocks, keys_here...  19.9 us
    unnamed x34, local copies, waits for them, and re-layouts  15.7 us
    pallas_call x4, Pallas kernels, finish_pass(): pl.pallas_call(functools.partial(finish_kernel, per_key, keys_here, half,...  12.7 us
    pallas_call x4, Pallas kernels, compose(): pl.pallas_call(functools.partial(compose_kernel, earlier.shape[2] > DV),...  7.38 us
    pallas_call x4, Pallas kernels, local_pass(): pl.pallas_call(functools.partial(local_kernel, per_key, blocks), grid=(1,...  6.65 us
    ppermute x1, waiting for transfers between devices, start_states(): got = lax.ppermute(theirs, 'seq', route('seq', lambda i: i ^ 1))  6.55 us
    ppermute x1, waiting for transfers between devices, start_states(): lax.ppermute(both, 'seq', route('seq', lambda i: i + 2 if i < 6 else None))  5.78 us
  transfers between devices with their start and end apart: 13, of which 6 were waited for; matrix products, arithmetic and copies ran while one was open for 1% of the time, Pallas kernels for 15%

profile of v1, /device:TPU:8, one launch (start us, length us, event | category | flops | bytes accessed | tf_op | source)
XLA Modules:
  0.0 120.5 jit_solution(11460436597053468664)
XLA Ops:
  0.0 1.2 %copy-done.6 = bf16[1024,512]{1,0:T(8,128)(2,1)S(1)} copy-done((bf16[1024,512]{1,0:T(8,128)(2,1)S(1)}, bf16[1024,512]{1,0:T(8,128)(2,1)}, u32[]{:S(2)}) %copy-start.6) | copy-done | bytes 1048600
  1.2 1.6 %copy-done.12 = bf16[1024,1024]{1,0:T(8,128)(2,1)S(1)} copy-done((bf16[1024,1024]{1,0:T(8,128)(2,1)S(1)}, bf16[1024,1024]{1,0:T(8,128)(2,1)}, u32[]{:S(2)}) %copy-start.12) | copy-done | bytes 2097176
  2.8 0.8 copy-done.13
  3.6 0.8 copy-done.14
  4.3 0.7 copy-done.15
  5.0 19.9 %shard_pass.1 = (bf16[64,128,256]{2,1,0:T(8,128)(2,1)}, bf16[8,8,128,256]{3,2,1,0:T(8,128)(2,1)}, f32[4,40,128]{2,1,0:T(8,128)S(1)}, bf16[8,128,256]{2,1,0:T(8,128)(2,1)S(1)}) custom-call(f32[8,1024]{1,0:T(8,128)S(1)} %copy-done.13, f32[8,1024]{1,0:T(8,128)S(1)} %copy-done.14, s32[8,128]{1,0:T(8,128)S(1)} %bitcast.7, bf16[1024,512]{1,0:T(8,128)(2,1)S(1)} %copy-done.6, ...), custom_call_target="tpu_custom_call" | custom-call | flops 4831838208 | bytes 12582912 | tf_op jit(solution)/shard_map/shard_pass/pallas_call | solution.py:177
  25.0 1.6 %collective-permute-start = (bf16[4,128,256]{2,1,0:T(8,128)(2,1)S(1)}, bf16[4,128,256]{2,1,0:T(8,128)(2,1)S(1)}, u32[]{:S(2)}, u32[]{:S(2)}) collective-permute-start(bf16[4,128,256]{2,1,0:T(8,128)(2,1)S(1)} %get-tuple-element.63), channel_id=1, source_target_pairs={{0,4},{4,0},{8,12},{12,8},{16,20},{20,16},{24,28},{28,24},{1,5},{5... | collective-permute-start | bytes 786440 | tf_op jit(solution)/shard_map/ppermute | solution.py:411
  26.6 6.5 %collective-permute-done = bf16[4,128,256]{2,1,0:T(8,128)(2,1)S(1)} collective-permute-done((bf16[4,128,256]{2,1,0:T(8,128)(2,1)S(1)}, bf16[4,128,256]{2,1,0:T(8,128)(2,1)S(1)}, u32[]{:S(2)}, u32[]{:S(2)}) %collective-permute-start) | collective-permute-done | bytes 262176 | tf_op jit(solution)/shard_map/ppermute | solution.py:411
  33.1 0.8 broadcast_select_fusion
  33.9 1.9 %compose.4.later_ref = bf16[4,128,256]{2,1,0:T(8,128)(2,1)} custom-call(bf16[4,128,256]{2,1,0:T(8,128)(2,1)} %get-tuple-element.62.later_ref, bf16[4,128,256]{2,1,0:T(8,128)(2,1)} %get-tuple-element.61.earlier_ref.later_ref), custom_call_target="tpu_custom_call" | custom-call | flops 33554432 | bytes 524288 | tf_op jit(solution)/shard_map/compose/pallas_call | solution.py:386
  35.9 3.5 %collective-permute-start.1 = (bf16[4,128,256]{2,1,0:T(8,128)(2,1)}, bf16[4,128,256]{2,1,0:T(8,128)(2,1)S(1)}, u32[]{:S(2)}, u32[]{:S(2)}) collective-permute-start(bf16[4,128,256]{2,1,0:T(8,128)(2,1)} %compose.4.later_ref), channel_id=1, source_target_pairs={{0,8},{4,12},{8,16},{12,20},{16,24},{20,28},{1,9},{5,13},{9,17},{1... | collective-permute-start | bytes 786440 | tf_op jit(solution)/shard_map/ppermute | solution.py:416
  39.4 5.8 %collective-permute-done.1.later_ref = bf16[4,128,256]{2,1,0:T(8,128)(2,1)S(1)} collective-permute-done((bf16[4,128,256]{2,1,0:T(8,128)(2,1)}, bf16[4,128,256]{2,1,0:T(8,128)(2,1)S(1)}, u32[]{:S(2)}, u32[]{:S(2)}) %collective-permute-start.1) | collective-permute-done | bytes 262176 | tf_op jit(solution)/shard_map/ppermute | solution.py:416
  45.1 0.7 slice.50.earlier_ref
  45.9 1.8 %compose.5 = bf16[4,128,128]{2,1,0:T(8,128)(2,1)} custom-call(bf16[4,128,256]{2,1,0:T(8,128)(2,1)} %compose.4.later_ref, bf16[4,128,128]{2,1,0:T(8,128)(2,1)} %slice.50.earlier_ref), custom_call_target="tpu_custom_call" | custom-call | flops 16777216 | bytes 262144 | tf_op jit(solution)/shard_map/compose/pallas_call | solution.py:386
  47.7 5.1 %collective-permute-start.3 = (bf16[4,128,128]{2,1,0:T(8,128)(2,1)}, bf16[4,128,128]{2,1,0:T(8,128)(2,1)}, u32[]{:S(2)}, u32[]{:S(2)}) collective-permute-start(bf16[4,128,128]{2,1,0:T(8,128)(2,1)} %compose.5), channel_id=1, source_target_pairs={{8,24},{12,28},{9,25},{13,29},{10,26},{14,30},{11,27},{15,31}} | collective-permute-start | bytes 393224 | tf_op jit(solution)/shard_map/ppermute | solution.py:420
  52.8 1.9 %collective-permute-start.2 = (bf16[4,128,128]{2,1,0:T(8,128)(2,1)}, bf16[4,128,128]{2,1,0:T(8,128)(2,1)}, u32[]{:S(2)}, u32[]{:S(2)}) collective-permute-start(bf16[4,128,128]{2,1,0:T(8,128)(2,1)} %compose.5), channel_id=1, source_target_pairs={{8,16},{12,20},{9,17},{13,21},{10,18},{14,22},{11,19},{15,23}} | collective-permute-start | bytes 393224 | tf_op jit(solution)/shard_map/ppermute | solution.py:419
  54.8 2.2 %copy-done.1 = bf16[64,128,256]{2,1,0:T(8,128)(2,1)S(1)} copy-done((bf16[64,128,256]{2,1,0:T(8,128)(2,1)S(1)}, bf16[64,128,256]{2,1,0:T(8,128)(2,1)}, u32[]{:S(2)}) %copy-start.1) | copy-done | bytes 4194328
  56.9 2.2 %copy-done.3 = bf16[8,8,128,256]{3,2,1,0:T(8,128)(2,1)S(1)} copy-done((bf16[8,8,128,256]{3,2,1,0:T(8,128)(2,1)S(1)}, bf16[8,8,128,256]{3,2,1,0:T(8,128)(2,1)}, u32[]{:S(2)}) %copy-start.3) | copy-done | bytes 4194328
  59.1 1.6 %local_pass.4 = (f32[1024,256]{1,0:T(8,128)S(1)}, bf16[1024,256]{1,0:T(8,128)(2,1)S(1)}) custom-call(f32[4,40,128]{2,1,0:T(8,128)S(1)} %get-tuple-element.46.rows_ref, bf16[1024,512]{1,0:T(8,128)(2,1)S(1)} %copy-done.8, bf16[1024,512]{1,0:T(8,128)(2,1)S(1)} %copy-done.7, bf16[64,128,256]{2,1,0:T(8,128)(2,1)S(1)} %copy-done.1, ...), custom_call_target="tpu_custom_call" | custom-call | flops 536870912 | bytes 4194304 | tf_op jit(solution)/shard_map/local_pass/pallas_call | solution.py:253
  60.8 0.0 copy-start.9
  60.8 0.8 copy-done.9
  61.6 0.0 collective-permute-done.3.earlier_ref
  61.6 1.8 %compose.6 = bf16[4,128,128]{2,1,0:T(8,128)(2,1)} custom-call(bf16[4,128,256]{2,1,0:T(8,128)(2,1)} %copy-done.16, bf16[4,128,128]{2,1,0:T(8,128)(2,1)} %collective-permute-done.3.earlier_ref), custom_call_target="tpu_custom_call" | custom-call | flops 16777216 | bytes 262144 | tf_op jit(solution)/shard_map/compose/pallas_call | solution.py:386
  63.4 1.6 %broadcast_select_fusion.4.earlier_ref = bf16[4,128,128]{2,1,0:T(8,128)(2,1)} fusion(bf16[4,128,128]{2,1,0:T(8,128)(2,1)} %collective-permute-done.2, bf16[4,128,128]{2,1,0:T(8,128)(2,1)} %compose.6, pred[]{:T(512)S(6)} %eq.9), kind=kLoop, calls=%fused_computation.22 | loop fusion | flops 65536 | bytes 393217 | tf_op jit(solution)/shard_map/jit(_where)/select_n | solution.py:422
  65.0 1.8 %compose.7 = bf16[4,128,128]{2,1,0:T(8,128)(2,1)} custom-call(bf16[4,128,256]{2,1,0:T(8,128)(2,1)} %get-tuple-element.61.earlier_ref.later_ref, bf16[4,128,128]{2,1,0:T(8,128)(2,1)} %broadcast_select_fusion.4.earlier_ref), custom_call_target="tpu_custom_call" | custom-call | flops 16777216 | bytes 262144 | tf_op jit(solution)/shard_map/compose/pallas_call | solution.py:386
  66.8 1.0 broadcast_select_fusion.7
  67.8 1.6 %collective-permute-start.4 = (bf16[4,128,128]{2,1,0:T(8,128)(2,1)S(1)}, bf16[4,128,128]{2,1,0:T(8,128)(2,1)S(1)}, u32[]{:S(2)}, u32[]{:S(2)}) collective-permute-start(bf16[4,128,128]{2,1,0:T(8,128)(2,1)S(1)} %get-tuple-element.67), channel_id=1, source_target_pairs={{0,4},{4,0},{8,12},{12,8},{16,20},{20,16},{24,28},{28,24},{1,5},{5... | collective-permute-start | bytes 393224 | tf_op jit(solution)/shard_map/ppermute | solution.py:426
  69.3 2.2 %copy-done.2 = bf16[64,128,256]{2,1,0:T(8,128)(2,1)S(1)} copy-done((bf16[64,128,256]{2,1,0:T(8,128)(2,1)S(1)}, bf16[64,128,256]{2,1,0:T(8,128)(2,1)}, u32[]{:S(2)}) %copy-start.2) | copy-done | bytes 4194328
  71.5 2.2 %copy-done.4 = bf16[8,8,128,256]{3,2,1,0:T(8,128)(2,1)S(1)} copy-done((bf16[8,8,128,256]{3,2,1,0:T(8,128)(2,1)S(1)}, bf16[8,8,128,256]{3,2,1,0:T(8,128)(2,1)}, u32[]{:S(2)}) %copy-start.4) | copy-done | bytes 4194328
  73.7 1.7 %local_pass.5 = (f32[1024,256]{1,0:T(8,128)S(1)}, bf16[1024,256]{1,0:T(8,128)(2,1)S(1)}) custom-call(f32[4,40,128]{2,1,0:T(8,128)S(1)} %get-tuple-element.46.rows_ref, bf16[1024,512]{1,0:T(8,128)(2,1)S(1)} %copy-done.8, bf16[1024,512]{1,0:T(8,128)(2,1)S(1)} %copy-done.7, bf16[64,128,256]{2,1,0:T(8,128)(2,1)S(1)} %copy-done.2, ...), custom_call_target="tpu_custom_call" | custom-call | flops 536870912 | bytes 4194304 | tf_op jit(solution)/shard_map/local_pass/pallas_call | solution.py:253
  75.4 1.7 %local_pass.6 = (f32[1024,256]{1,0:T(8,128)S(1)}, bf16[1024,256]{1,0:T(8,128)(2,1)S(1)}) custom-call(f32[4,40,128]{2,1,0:T(8,128)S(1)} %get-tuple-element.46.rows_ref, bf16[1024,512]{1,0:T(8,128)(2,1)S(1)} %copy-done.8, bf16[1024,512]{1,0:T(8,128)(2,1)S(1)} %copy-done.7, bf16[64,128,256]{2,1,0:T(8,128)(2,1)S(1)} %copy-done.2, ...), custom_call_target="tpu_custom_call" | custom-call | flops 536870912 | bytes 4194304 | tf_op jit(solution)/shard_map/local_pass/pallas_call | solution.py:253
  77.1 0.0 copy-start
  77.1 0.0 copy-start.5
  77.1 0.0 copy-start.10
  77.1 0.0 copy-start.11
  77.1 1.7 %local_pass.7 = (f32[1024,256]{1,0:T(8,128)S(1)}, bf16[1024,256]{1,0:T(8,128)(2,1)S(1)}) custom-call(f32[4,40,128]{2,1,0:T(8,128)S(1)} %get-tuple-element.46.rows_ref, bf16[1024,512]{1,0:T(8,128)(2,1)S(1)} %copy-done.8, bf16[1024,512]{1,0:T(8,128)(2,1)S(1)} %copy-done.7, bf16[64,128,256]{2,1,0:T(8,128)(2,1)S(1)} %copy-done.2, ...), custom_call_target="tpu_custom_call" | custom-call | flops 536870912 | bytes 4194304 | tf_op jit(solution)/shard_map/local_pass/pallas_call | solution.py:253
  78.9 0.4 copy-done
  79.3 0.7 copy-done.5
  80.0 0.0 copy-done.10
  80.0 3.2 %finish_pass.4 = (bf16[256,1024]{1,0:T(8,128)(2,1)S(1)}, bf16[256,1024]{1,0:T(8,128)(2,1)S(1)}) custom-call(s32[1]{0:T(128)} %bitcast.me_ref, f32[1024,256]{1,0:T(8,128)S(1)} %get-tuple-element.38.refs_0_, f32[1024,256]{1,0:T(8,128)S(1)} %get-tuple-element.41.refs_1_, f32[1024,256]{1,0:T(8,128)S(1)} %get-tuple-element.43.refs_2_, ...), custom_call_target="tpu_custom_call" | custom-call | flops 1073741824 | bytes 8388608 | tf_op jit(solution)/shard_map/finish_pass/pallas_call | solution.py:362
  83.2 0.1 collective-permute-start.5
  83.2 3.2 %finish_pass.5 = (bf16[256,1024]{1,0:T(8,128)(2,1)S(1)}, bf16[256,1024]{1,0:T(8,128)(2,1)S(1)}) custom-call(s32[1]{0:T(128)} %bitcast.me_ref, f32[1024,256]{1,0:T(8,128)S(1)} %get-tuple-element.38.refs_0_, f32[1024,256]{1,0:T(8,128)S(1)} %get-tuple-element.41.refs_1_, f32[1024,256]{1,0:T(8,128)S(1)} %get-tuple-element.43.refs_2_, ...), custom_call_target="tpu_custom_call" | custom-call | flops 1073741824 | bytes 8388608 | tf_op jit(solution)/shard_map/finish_pass/pallas_call | solution.py:362
  86.4 0.5 collective-permute-start.7
  87.0 3.2 %finish_pass.6 = (bf16[256,1024]{1,0:T(8,128)(2,1)S(1)}, bf16[256,1024]{1,0:T(8,128)(2,1)S(1)}) custom-call(s32[1]{0:T(128)} %bitcast.me_ref, f32[1024,256]{1,0:T(8,128)S(1)} %get-tuple-element.38.refs_0_, f32[1024,256]{1,0:T(8,128)S(1)} %get-tuple-element.41.refs_1_, f32[1024,256]{1,0:T(8,128)S(1)} %get-tuple-element.43.refs_2_, ...), custom_call_target="tpu_custom_call" | custom-call | flops 1073741824 | bytes 8388608 | tf_op jit(solution)/shard_map/finish_pass/pallas_call | solution.py:362
  90.1 0.1 collective-permute-start.9
  90.2 3.2 %finish_pass.7 = (bf16[256,1024]{1,0:T(8,128)(2,1)S(1)}, bf16[256,1024]{1,0:T(8,128)(2,1)S(1)}) custom-call(s32[1]{0:T(128)} %bitcast.me_ref, f32[1024,256]{1,0:T(8,128)S(1)} %get-tuple-element.38.refs_0_, f32[1024,256]{1,0:T(8,128)S(1)} %get-tuple-element.41.refs_1_, f32[1024,256]{1,0:T(8,128)S(1)} %get-tuple-element.43.refs_2_, ...), custom_call_target="tpu_custom_call" | custom-call | flops 1073741824 | bytes 8388608 | tf_op jit(solution)/shard_map/finish_pass/pallas_call | solution.py:362
  93.4 0.5 collective-permute-start.11
  93.9 0.2 convert_add_fusion.3
  94.2 1.6 %collective-permute-start.6 = (bf16[256,512]{1,0:T(8,128)(2,1)S(1)}, bf16[256,512]{1,0:T(8,128)(2,1)S(1)}, u32[]{:S(2)}, u32[]{:S(2)}) collective-permute-start(bf16[256,512]{1,0:T(8,128)(2,1)S(1)} %slice.82), channel_id=1, source_target_pairs={{0,2},{1,3},{2,0},{3,1},{4,6},{5,7},{6,4},{7,5},{8,10},{9,11},{10,... | collective-permute-start | bytes 786440 | tf_op jit(solution)/shard_map/ppermute | solution.py:478
  95.7 0.2 convert_add_fusion.2
  96.0 0.6 collective-permute-start.8
  96.5 0.2 convert_add_fusion.1
  96.8 1.6 %collective-permute-start.10 = (bf16[256,512]{1,0:T(8,128)(2,1)S(1)}, bf16[256,512]{1,0:T(8,128)(2,1)S(1)}, u32[]{:S(2)}, u32[]{:S(2)}) collective-permute-start(bf16[256,512]{1,0:T(8,128)(2,1)S(1)} %slice.80), channel_id=1, source_target_pairs={{0,2},{1,3},{2,0},{3,1},{4,6},{5,7},{6,4},{7,5},{8,10},{9,11},{10,... | collective-permute-start | bytes 786440 | tf_op jit(solution)/shard_map/ppermute | solution.py:478
  98.4 0.2 convert_add_fusion
  98.6 0.6 collective-permute-start.12
  99.1 4.3 %collective-permute-done.6 = bf16[256,512]{1,0:T(8,128)(2,1)S(1)} collective-permute-done((bf16[256,512]{1,0:T(8,128)(2,1)S(1)}, bf16[256,512]{1,0:T(8,128)(2,1)S(1)}, u32[]{:S(2)}, u32[]{:S(2)}) %collective-permute-start.6) | collective-permute-done | bytes 262176 | tf_op jit(solution)/shard_map/ppermute | solution.py:478
  103.4 0.1 fusion.3
  103.5 5.5 %collective-permute-done.8 = bf16[256,512]{1,0:T(8,128)(2,1)S(1)} collective-permute-done((bf16[256,512]{1,0:T(8,128)(2,1)S(1)}, bf16[256,512]{1,0:T(8,128)(2,1)S(1)}, u32[]{:S(2)}, u32[]{:S(2)}) %collective-permute-start.8) | collective-permute-done | bytes 262176 | tf_op jit(solution)/shard_map/ppermute | solution.py:478
  109.0 0.1 fusion.2
  109.1 5.5 %collective-permute-done.10 = bf16[256,512]{1,0:T(8,128)(2,1)S(1)} collective-permute-done((bf16[256,512]{1,0:T(8,128)(2,1)S(1)}, bf16[256,512]{1,0:T(8,128)(2,1)S(1)}, u32[]{:S(2)}, u32[]{:S(2)}) %collective-permute-start.10) | collective-permute-done | bytes 262176 | tf_op jit(solution)/shard_map/ppermute | solution.py:478
  114.6 0.1 fusion.1
  114.7 4.6 %collective-permute-done.12 = bf16[256,512]{1,0:T(8,128)(2,1)S(1)} collective-permute-done((bf16[256,512]{1,0:T(8,128)(2,1)S(1)}, bf16[256,512]{1,0:T(8,128)(2,1)S(1)}, u32[]{:S(2)}, u32[]{:S(2)}) %collective-permute-start.12) | collective-permute-done | bytes 262176 | tf_op jit(solution)/shard_map/ppermute | solution.py:478
  119.3 0.1 fusion
  119.4 1.0 pad_maximum_fusion
  (29 shorter events, 0.3 us)
Async XLA Ops:
  0.0 1.2 %copy-start.6 = (bf16[1024,512]{1,0:T(8,128)(2,1)S(1)}, bf16[1024,512]{1,0:T(8,128)(2,1)}, u32[]{:S(2)}) copy-start(bf16[1024,512]{1,0:T(8,128)(2,1)} %k_ref.9) | copy-start | bytes 3145732
  1.2 1.6 %copy-start.12 = (bf16[1024,1024]{1,0:T(8,128)(2,1)S(1)}, bf16[1024,1024]{1,0:T(8,128)(2,1)}, u32[]{:S(2)}) copy-start(bf16[1024,1024]{1,0:T(8,128)(2,1)} %v_ref.1) | copy-start | bytes 6291460
  2.8 0.8 copy-start.13
  3.6 0.8 copy-start.14
  4.3 0.7 copy-start.15
  24.9 29.8 %copy-start.7 = (bf16[1024,512]{1,0:T(8,128)(2,1)S(1)}, bf16[1024,512]{1,0:T(8,128)(2,1)}, u32[]{:S(2)}) copy-start(bf16[1024,512]{1,0:T(8,128)(2,1)} %k_ref.9) | copy-start | bytes 3145732
  24.9 29.8 %copy-start.8 = (bf16[1024,512]{1,0:T(8,128)(2,1)S(1)}, bf16[1024,512]{1,0:T(8,128)(2,1)}, u32[]{:S(2)}) copy-start(bf16[1024,512]{1,0:T(8,128)(2,1)} %q_ref.7) | copy-start | bytes 3145732
  25.0 8.1 %collective-permute-start = (bf16[4,128,256]{2,1,0:T(8,128)(2,1)S(1)}, bf16[4,128,256]{2,1,0:T(8,128)(2,1)S(1)}, u32[]{:S(2)}, u32[]{:S(2)}) collective-permute-start(bf16[4,128,256]{2,1,0:T(8,128)(2,1)S(1)} %get-tuple-element.63), channel_id=1, source_target_pairs={{0,4},{4,0},{8,12},{12,8},{16,20},{20,16},{24,28},{28,24},{1,5},{5... | collective-permute-start | bytes 786440 | tf_op jit(solution)/shard_map/ppermute | solution.py:411
  35.9 9.3 %collective-permute-start.1 = (bf16[4,128,256]{2,1,0:T(8,128)(2,1)}, bf16[4,128,256]{2,1,0:T(8,128)(2,1)S(1)}, u32[]{:S(2)}, u32[]{:S(2)}) collective-permute-start(bf16[4,128,256]{2,1,0:T(8,128)(2,1)} %compose.4.later_ref), channel_id=1, source_target_pairs={{0,8},{4,12},{8,16},{12,20},{16,24},{20,28},{1,9},{5,13},{9,17},{1... | collective-permute-start | bytes 786440 | tf_op jit(solution)/shard_map/ppermute | solution.py:416
  45.1 15.6 %copy-start.16 = (bf16[4,128,256]{2,1,0:T(8,128)(2,1)}, bf16[4,128,256]{2,1,0:T(8,128)(2,1)S(1)}, u32[]{:S(2)}) copy-start(bf16[4,128,256]{2,1,0:T(8,128)(2,1)S(1)} %collective-permute-done.1.later_ref) | copy-start | bytes 786436
  47.7 13.9 %collective-permute-start.3 = (bf16[4,128,128]{2,1,0:T(8,128)(2,1)}, bf16[4,128,128]{2,1,0:T(8,128)(2,1)}, u32[]{:S(2)}, u32[]{:S(2)}) collective-permute-start(bf16[4,128,128]{2,1,0:T(8,128)(2,1)} %compose.5), channel_id=1, source_target_pairs={{8,24},{12,28},{9,25},{13,29},{10,26},{14,30},{11,27},{15,31}} | collective-permute-start | bytes 393224 | tf_op jit(solution)/shard_map/ppermute | solution.py:420
  52.8 10.6 %collective-permute-start.2 = (bf16[4,128,128]{2,1,0:T(8,128)(2,1)}, bf16[4,128,128]{2,1,0:T(8,128)(2,1)}, u32[]{:S(2)}, u32[]{:S(2)}) collective-permute-start(bf16[4,128,128]{2,1,0:T(8,128)(2,1)} %compose.5), channel_id=1, source_target_pairs={{8,16},{12,20},{9,17},{13,21},{10,18},{14,22},{11,19},{15,23}} | collective-permute-start | bytes 393224 | tf_op jit(solution)/shard_map/ppermute | solution.py:419
  54.8 2.2 %copy-start.1 = (bf16[64,128,256]{2,1,0:T(8,128)(2,1)S(1)}, bf16[64,128,256]{2,1,0:T(8,128)(2,1)}, u32[]{:S(2)}) copy-start(bf16[64,128,256]{2,1,0:T(8,128)(2,1)} %get-tuple-element.36.wu_ref) | copy-start | bytes 12582916
  56.9 2.2 %copy-start.3 = (bf16[8,8,128,256]{3,2,1,0:T(8,128)(2,1)S(1)}, bf16[8,8,128,256]{3,2,1,0:T(8,128)(2,1)}, u32[]{:S(2)}) copy-start(bf16[8,8,128,256]{3,2,1,0:T(8,128)(2,1)} %get-tuple-element.37.zc_ref) | copy-start | bytes 12582916
  60.8 0.8 copy-start.9
  67.8 11.0 %collective-permute-start.4 = (bf16[4,128,128]{2,1,0:T(8,128)(2,1)S(1)}, bf16[4,128,128]{2,1,0:T(8,128)(2,1)S(1)}, u32[]{:S(2)}, u32[]{:S(2)}) collective-permute-start(bf16[4,128,128]{2,1,0:T(8,128)(2,1)S(1)} %get-tuple-element.67), channel_id=1, source_target_pairs={{0,4},{4,0},{8,12},{12,8},{16,20},{20,16},{24,28},{28,24},{1,5},{5... | collective-permute-start | bytes 393224 | tf_op jit(solution)/shard_map/ppermute | solution.py:426
  69.3 2.2 %copy-start.2 = (bf16[64,128,256]{2,1,0:T(8,128)(2,1)S(1)}, bf16[64,128,256]{2,1,0:T(8,128)(2,1)}, u32[]{:S(2)}) copy-start(bf16[64,128,256]{2,1,0:T(8,128)(2,1)} %get-tuple-element.36.wu_ref) | copy-start | bytes 12582916
  71.5 2.2 %copy-start.4 = (bf16[8,8,128,256]{3,2,1,0:T(8,128)(2,1)S(1)}, bf16[8,8,128,256]{3,2,1,0:T(8,128)(2,1)}, u32[]{:S(2)}) copy-start(bf16[8,8,128,256]{3,2,1,0:T(8,128)(2,1)} %get-tuple-element.37.zc_ref) | copy-start | bytes 12582916
  77.1 2.2 %copy-start = (bf16[1024,2048]{1,0:T(8,128)(2,1)S(1)}, bf16[1024,2048]{1,0:T(8,128)(2,1)}, u32[]{:S(2)}) copy-start(bf16[1024,2048]{1,0:T(8,128)(2,1)} %refs_11_.7) | copy-start | bytes 12582916
  77.1 2.9 %copy-start.5 = (bf16[1024,1024]{1,0:T(8,128)(2,1)S(1)}, bf16[1024,1024]{1,0:T(8,128)(2,1)}, u32[]{:S(2)}) copy-start(bf16[1024,1024]{1,0:T(8,128)(2,1)} %refs_9_.7) | copy-start | bytes 6291460
  77.1 2.9 %copy-start.10 = (bf16[1024,256]{1,0:T(8,128)(2,1)S(1)}, bf16[1024,256]{1,0:T(8,128)(2,1)}, u32[]{:S(2)}) copy-start(bf16[1024,256]{1,0:T(8,128)(2,1)} %copy-done.9) | copy-start | bytes 1572868
  77.1 2.9 %copy-start.11 = (f32[128]{0:T(128)S(1)}, f32[128]{0:T(128)}, u32[]{:S(2)}) copy-start(f32[128]{0:T(128)} %param.16) | copy-start | bytes 1540
  83.2 10.8 %collective-permute-start.5 = (bf16[256,1024]{1,0:T(8,128)(2,1)S(1)}, bf16[256,1024]{1,0:T(8,128)(2,1)S(1)}, u32[]{:S(2)}, u32[]{:S(2)}) collective-permute-start(bf16[256,1024]{1,0:T(8,128)(2,1)S(1)} %get-tuple-element.54), channel_id=1, source_target_pairs={{0,1},{1,0},{2,3},{3,2},{4,5},{5,4},{6,7},{7,6},{8,9},{9,8},{10,11... | collective-permute-start | bytes 1572872 | tf_op jit(solution)/shard_map/ppermute | solution.py:478
  86.4 9.3 %collective-permute-start.7 = (bf16[256,1024]{1,0:T(8,128)(2,1)S(1)}, bf16[256,1024]{1,0:T(8,128)(2,1)S(1)}, u32[]{:S(2)}, u32[]{:S(2)}) collective-permute-start(bf16[256,1024]{1,0:T(8,128)(2,1)S(1)} %get-tuple-element.56), channel_id=1, source_target_pairs={{0,1},{1,0},{2,3},{3,2},{4,5},{5,4},{6,7},{7,6},{8,9},{9,8},{10,11... | collective-permute-start | bytes 1572872 | tf_op jit(solution)/shard_map/ppermute | solution.py:478
  90.1 6.4 %collective-permute-start.9 = (bf16[256,1024]{1,0:T(8,128)(2,1)S(1)}, bf16[256,1024]{1,0:T(8,128)(2,1)S(1)}, u32[]{:S(2)}, u32[]{:S(2)}) collective-permute-start(bf16[256,1024]{1,0:T(8,128)(2,1)S(1)} %get-tuple-element.58), channel_id=1, source_target_pairs={{0,1},{1,0},{2,3},{3,2},{4,5},{5,4},{6,7},{7,6},{8,9},{9,8},{10,11... | collective-permute-start | bytes 1572872 | tf_op jit(solution)/shard_map/ppermute | solution.py:478
  93.4 4.9 %collective-permute-start.11 = (bf16[256,1024]{1,0:T(8,128)(2,1)S(1)}, bf16[256,1024]{1,0:T(8,128)(2,1)S(1)}, u32[]{:S(2)}, u32[]{:S(2)}) collective-permute-start(bf16[256,1024]{1,0:T(8,128)(2,1)S(1)} %get-tuple-element.60), channel_id=1, source_target_pairs={{0,1},{1,0},{2,3},{3,2},{4,5},{5,4},{6,7},{7,6},{8,9},{9,8},{10,11... | collective-permute-start | bytes 1572872 | tf_op jit(solution)/shard_map/ppermute | solution.py:478
  94.2 9.2 %collective-permute-start.6 = (bf16[256,512]{1,0:T(8,128)(2,1)S(1)}, bf16[256,512]{1,0:T(8,128)(2,1)S(1)}, u32[]{:S(2)}, u32[]{:S(2)}) collective-permute-start(bf16[256,512]{1,0:T(8,128)(2,1)S(1)} %slice.82), channel_id=1, source_target_pairs={{0,2},{1,3},{2,0},{3,1},{4,6},{5,7},{6,4},{7,5},{8,10},{9,11},{10,... | collective-permute-start | bytes 786440 | tf_op jit(solution)/shard_map/ppermute | solution.py:478
  96.0 13.0 %collective-permute-start.8 = (bf16[256,512]{1,0:T(8,128)(2,1)S(1)}, bf16[256,512]{1,0:T(8,128)(2,1)S(1)}, u32[]{:S(2)}, u32[]{:S(2)}) collective-permute-start(bf16[256,512]{1,0:T(8,128)(2,1)S(1)} %slice.81), channel_id=1, source_target_pairs={{0,2},{1,3},{2,0},{3,1},{4,6},{5,7},{6,4},{7,5},{8,10},{9,11},{10,... | collective-permute-start | bytes 786440 | tf_op jit(solution)/shard_map/ppermute | solution.py:478
  96.8 17.9 %collective-permute-start.10 = (bf16[256,512]{1,0:T(8,128)(2,1)S(1)}, bf16[256,512]{1,0:T(8,128)(2,1)S(1)}, u32[]{:S(2)}, u32[]{:S(2)}) collective-permute-start(bf16[256,512]{1,0:T(8,128)(2,1)S(1)} %slice.80), channel_id=1, source_target_pairs={{0,2},{1,3},{2,0},{3,1},{4,6},{5,7},{6,4},{7,5},{8,10},{9,11},{10,... | collective-permute-start | bytes 786440 | tf_op jit(solution)/shard_map/ppermute | solution.py:478
  98.6 20.8 %collective-permute-start.12 = (bf16[256,512]{1,0:T(8,128)(2,1)S(1)}, bf16[256,512]{1,0:T(8,128)(2,1)S(1)}, u32[]{:S(2)}, u32[]{:S(2)}) collective-permute-start(bf16[256,512]{1,0:T(8,128)(2,1)S(1)} %slice.79), channel_id=1, source_target_pairs={{0,2},{1,3},{2,0},{3,1},{4,6},{5,7},{6,4},{7,5},{8,10},{9,11},{10,... | collective-permute-start | bytes 786440 | tf_op jit(solution)/shard_map/ppermute | solution.py:478

commit v2 on v1

--- a/solution.py
+++ b/solution.py
@@ -60,8 +60,8 @@
 
 def shard_kernel(
     per_key, blocks, keys_here,
-    log_ref, rate_ref, start_ref, k_ref, v_ref,
-    wu_ref, zc_ref, rows_ref, end_ref,
+    me_ref, log_ref, rate_ref, start_ref, k_ref, v_ref,
+    wu_ref, zc_ref, rows_ref, mine_ref, theirs_ref,
     logs, rates, norms, kt, mask, db, keep, state,
 ):
     key = pl.program_id(0)
@@ -162,11 +162,22 @@
             return carry
 
         lax.fori_loop(0, blocks, advance, 0)
+        half = mine_ref.shape[0]
+        odd = lax.rem(me_ref[0], 2) == 1
         for h in range(heads_here):
-            end_ref[h] = state[h].astype(BF16)
-
-
-def shard_pass(log_gate, write_rate, starts, key_rows, value_rows, per_key):
+            ends = state[h].astype(BF16)
+            ours = odd if h >= half else jnp.logical_not(odd)
+
+            @pl.when(ours)
+            def _():
+                mine_ref[h % half] = ends
+
+            @pl.when(jnp.logical_not(ours))
+            def _():
+                theirs_ref[h % half] = ends
+
+
+def shard_pass(me, log_gate, write_rate, starts, key_rows, value_rows, per_key):
     tokens_here = key_rows.shape[0]
     keys_here = key_rows.shape[1] // DK
     heads_here = keys_here * per_key
@@ -178,6 +189,7 @@
         functools.partial(shard_kernel, per_key, blocks, keys_here),
         grid=(keys_here,),
         in_specs=[
+            pl.BlockSpec(memory_space=pltpu.SMEM),
             whole(heads_here, tokens_here),
             whole(heads_here, tokens_here),
             whole(blocks, BLK),
@@ -188,13 +200,15 @@
             pl.BlockSpec((count, BLK, wide), lambda key: (key, 0, 0)),
             whole(heads_here, blocks, DK, wide),
             pl.BlockSpec((1, 2 * count + blocks, BLK), lambda key: (key, 0, 0)),
-            whole(heads_here, DK, wide),
+            whole(heads_here // 2, DK, wide),
+            whole(heads_here // 2, DK, wide),
         ],
         out_shape=[
             jax.ShapeDtypeStruct((keys_here * count, BLK, wide), BF16),
             jax.ShapeDtypeStruct((heads_here, blocks, DK, wide), BF16),
             jax.ShapeDtypeStruct((keys_here, 2 * count + blocks, BLK), F32),
-            jax.ShapeDtypeStruct((heads_here, DK, wide), BF16),
+            jax.ShapeDtypeStruct((heads_here // 2, DK, wide), BF16),
+            jax.ShapeDtypeStruct((heads_here // 2, DK, wide), BF16),
         ],
         scratch_shapes=[
             pltpu.VMEM((count, BLK), F32),
@@ -206,12 +220,12 @@
             pltpu.VMEM((keys_here * count, 1, BLK), F32),
             pltpu.VMEM((heads_here, DK, wide), F32),
         ],
-        compiler_params=pltpu.CompilerParams(vmem_limit_bytes=48 * MIB),
+        compiler_params=pltpu.CompilerParams(vmem_limit_bytes=62 * MIB),
         cost_estimate=pl.CostEstimate(
             flops=keys_here * count * 18 * 2 * BLK**3, bytes_accessed=12 * MIB, transcendentals=0
         ),
         name="shard_pass",
-    )(log_gate, write_rate, starts, key_rows, value_rows)
+    )(me, log_gate, write_rate, starts, key_rows, value_rows)
 
 
 def local_kernel(per_key, blocks, rows_ref, q_ref, k_ref, wu_ref, zc_ref, out_ref, carry_ref):
@@ -280,9 +294,11 @@
     per_key, keys_here, sends, order,
     me_ref, *refs,
 ):
+    half = keys_here * per_key // 2
+    odd = lax.rem(me_ref[1], 2) == 1
     outs = refs[:keys_here]
     carries = refs[keys_here : 2 * keys_here]
-    start_ref, gate_ref, gain_ref, weight_ref, send_ref, keep_ref, normed = refs[2 * keys_here :]
+    own_ref, back_ref, gate_ref, gain_ref, weight_ref, send_ref, keep_ref, normed = refs[2 * keys_here :]
     step = pl.program_id(0)
 
     @pl.when(step == 0)
@@ -292,7 +308,9 @@
                 head = key * per_key + h
                 span = slice(h * DV, (h + 1) * DV)
                 wide = slice(head * DV, (head + 1) * DV)
-                seen = outs[key][:, span] + dot(carries[key][:, span], start_ref[head])
+                own, back = own_ref[head % half], back_ref[head % half]
+                start = jnp.where(odd, own, back) if head >= half else jnp.where(odd, back, own)
+                seen = outs[key][:, span] + dot(carries[key][:, span], start)
                 spread = jnp.mean(seen * seen, axis=1, keepdims=True)
                 gate = gate_ref[:, wide].astype(F32)
                 gated = gain_ref[...] * (gate / (1.0 + jnp.exp(-gate)))
@@ -328,7 +346,7 @@
     return split(list(range(size)), 1)
 
 
-def finish_pass(index, rows, me, outs, carries, start, out_gate, gain, weight, per_key, groups):
+def finish_pass(index, rows, me, outs, carries, own, back, out_gate, gain, weight, per_key, groups):
     heads_here = out_gate.shape[1] // DV
     keys_here = len(outs)
     columns = weight.shape[1] // groups
@@ -348,7 +366,8 @@
         grid=(groups,),
         in_specs=[per_head] * (2 * keys_here)
         + [
-            pl.BlockSpec((heads_here, DK, DV), lambda step, me_ref: (0, 0, 0)),
+            pl.BlockSpec((heads_here // 2, DK, DV), lambda step, me_ref: (0, 0, 0)),
+            pl.BlockSpec((heads_here // 2, DK, DV), lambda step, me_ref: (0, 0, 0)),
             pl.BlockSpec((rows, heads_here * DV), lambda step, me_ref: (index, 0)),
             pl.BlockSpec((1, DV), lambda step, me_ref: (0, 0)),
             pl.BlockSpec((weight.shape[0], columns), column_of),
@@ -370,26 +389,98 @@
             transcendentals=0,
         ),
         name="finish_pass",
-    )(me, *outs, *carries, start, out_gate, gain, weight)
-
-
-def compose_kernel(wide, later_ref, earlier_ref, out_ref):
-    for h in range(later_ref.shape[0]):
-        later = later_ref[h]
-        moved = dot(later[:, DV:], earlier_ref[h])
-        out_ref[h, :, :DV] = (moved[:, :DV] + later[:, :DV].astype(F32)).astype(BF16)
-        if wide:
-            out_ref[h, :, DV:] = moved[:, DV:].astype(BF16)
-
-
-def compose(later, earlier):
+    )(me, *outs, *carries, own, back, out_gate, gain, weight)
+
+
+def composed(later, earlier, h):
+    return dot(later[h, :, DV:], earlier[h]) + later[h, :, :DV].astype(F32)
+
+
+def pair_kernel(me_ref, mine_ref, got_ref, both_ref):
+    odd = lax.rem(me_ref[0], 2) == 1
+
+    def join(second, first):
+        for h in range(both_ref.shape[0]):
+            moved = dot(second[h, :, DV:], first[h])
+            both_ref[h, :, :DV] = (moved[:, :DV] + second[h, :, :DV].astype(F32)).astype(BF16)
+            both_ref[h, :, DV:] = moved[:, DV:].astype(BF16)
+
+    @pl.when(odd)
+    def _():
+        join(mine_ref, got_ref)
+
+    @pl.when(jnp.logical_not(odd))
+    def _():
+        join(got_ref, mine_ref)
+
+
+def step_kernel(later_ref, earlier_ref, out_ref):
+    for h in range(out_ref.shape[0]):
+        out_ref[h] = composed(later_ref, earlier_ref, h).astype(BF16)
+
+
+def last_kernel(me_ref, mine_ref, got_ref, before_ref, near_ref, far_ref, own_ref, other_ref):
+    odd = lax.rem(me_ref[0], 2) == 1
+    third = lax.div(me_ref[0], 2) == 2
+
+    def fill(first, here_ref, then_ref):
+        for h in range(own_ref.shape[0]):
+            here = composed(before_ref, far_ref, h).astype(BF16)
+            here_ref[h] = jnp.where(third, near_ref[h], here)
+        for h in range(own_ref.shape[0]):
+            then_ref[h] = composed(first, here_ref, h).astype(BF16)
+
+    @pl.when(odd)
+    def _():
+        fill(got_ref, other_ref, own_ref)
+
+    @pl.when(jnp.logical_not(odd))
+    def _():
+        fill(mine_ref, own_ref, other_ref)
+
+
+SMALL = pltpu.CompilerParams(vmem_limit_bytes=8 * MIB)
+ONE = pl.BlockSpec(memory_space=pltpu.SMEM)
+
+
+def plain(array):
+    return pl.BlockSpec(array.shape, lambda i: (0,) * array.ndim)
+
+
+def small_call(kernel, name, outs, me, *arrays):
+    heads = arrays[0].shape[0]
+    state = jax.ShapeDtypeStruct((heads, DK, DV), BF16)
+    scalars = [] if me is None else [me]
     return pl.pallas_call(
-        functools.partial(compose_kernel, earlier.shape[2] > DV),
-        out_shape=jax.ShapeDtypeStruct(earlier.shape, BF16),
+        kernel,
+        grid=(1,),
+        in_specs=[ONE] * len(scalars) + [plain(a) for a in arrays],
+        out_specs=[plain(a) for a in outs],
+        out_shape=outs,
+        compiler_params=SMALL,
         cost_estimate=pl.CostEstimate(
-            flops=2 * earlier.size * DK, bytes_accessed=4 * earlier.size, transcendentals=0
+            flops=heads * 4 * DK**3, bytes_accessed=MIB, transcendentals=0
         ),
-        name="compose",
+        name=name,
+    )(*scalars, *arrays)
+
+
+def step_call(later, earlier):
+    heads = later.shape[0]
+    return pl.pallas_call(
+        step_kernel,
+        grid=(1,),
+        in_specs=[
+            pl.BlockSpec((heads, DK, DK + DV), lambda i: (0, 0, 0)),
+            pl.BlockSpec((heads, DK, DV), lambda i: (0, 0, 0)),
+        ],
+        out_specs=pl.BlockSpec((heads, DK, DV), lambda i: (0, 0, 0)),
+        out_shape=jax.ShapeDtypeStruct((heads, DK, DV), BF16),
+        compiler_params=SMALL,
+        cost_estimate=pl.CostEstimate(
+            flops=heads * 2 * DK**3, bytes_accessed=MIB, transcendentals=0
+        ),
+        name="step",
     )(later, earlier)
 
 
@@ -398,43 +489,38 @@
     return [(i, target(i)) for i in range(size) if target(i) is not None]
 
 
-def start_states(end, work):
+def start_states(me, mine, theirs, work):
     size = lax.axis_size("seq")
-    heads = end.shape[0]
-    me = lax.axis_index("seq")
-    if size == 8 and heads % 2 == 0:
-        half = heads // 2
-        odd = me % 2 == 1
-        pair = me // 2
-        mine = jnp.where(odd, end[half:], end[:half])
-        theirs = jnp.where(odd, end[:half], end[half:])
-        got = lax.ppermute(theirs, "seq", route("seq", lambda i: i ^ 1))
-        mine, got = work(mine, got)
-        first = jnp.where(odd, got, mine)
-        second = jnp.where(odd, mine, got)
-        both = compose(second, first)
-        before = lax.ppermute(both, "seq", route("seq", lambda i: i + 2 if i < 6 else None))
-        both, before = work(both, before)
-        third = compose(both, before[:, :, :DV])
+    half = mine.shape[0]
+    state = jax.ShapeDtypeStruct((half, DK, DV), BF16)
+    swap = route("seq", lambda i: i ^ 1)
+    if size == 8:
+        got = work(lax.ppermute(theirs, "seq", swap))
+        both, = small_call(
+            pair_kernel, "pair", [jax.ShapeDtypeStruct(mine.shape, BF16)], me, mine, got
+        )
+        before = work(
+            lax.ppermute(both, "seq", route("seq", lambda i: i + 2 if i < 6 else None))
+        )
+        third = step_call(both, before)
         near = lax.ppermute(third, "seq", [(2, 4), (3, 5)])
-        far = lax.ppermute(third, "seq", [(2, 6), (3, 7)])
-        before, (near, far) = work(before, (near, far))
-        here = jnp.where(pair == 2, near, compose(before, far))
-        then = compose(first, here)
-        own = jnp.where(odd, then, here)
-        other = jnp.where(odd, here, then)
-        back = lax.ppermute(other, "seq", route("seq", lambda i: i ^ 1))
-        own, back = work(own, back)
-        return jnp.concatenate(
-            [jnp.where(odd, back, own), jnp.where(odd, own, back)], axis=0
+        far = work(lax.ppermute(third, "seq", [(2, 6), (3, 7)]))
+        own, other = small_call(
+            last_kernel, "last", [state] * 2, me, mine, got, before, near, far
         )
-
-    def hop(step, state):
-        return lax.ppermute(
-            compose(end, state), "seq", route("seq", lambda i: i + 1 if i + 1 < size else None)
-        )
-
-    return lax.fori_loop(0, size - 1, hop, jnp.zeros((heads, DK, DV), BF16))
+        return own, work(lax.ppermute(other, "seq", swap))
+
+    onward = route("seq", lambda i: i + 1 if i + 1 < size else None)
+    parts = jnp.zeros((half, DK, DV), BF16), jnp.zeros((half, DK, DV), BF16)
+    odd = me[0] % 2 == 1
+
+    def hop(step, states):
+        ends = [step_call(end, held) for end, held in zip((mine, theirs), states)]
+        low, high = jnp.where(odd, ends[1], ends[0]), jnp.where(odd, ends[0], ends[1])
+        low, high = lax.ppermute((low, high), "seq", onward)
+        return jnp.where(odd, high, low), jnp.where(odd, low, high)
+
+    return lax.fori_loop(0, size - 1, hop, parts)
 
 
 def local(
@@ -446,36 +532,52 @@
     per_key = heads_here // keys_here
     groups = lax.axis_size("head")
     starts = doc_start.reshape(tokens_here // BLK, BLK)
-    wu, zc, rows, end = shard_pass(
-        log_gate, write_rate, starts, key_rows, value_rows, per_key
+    seq_me = lax.axis_index("seq").reshape(1).astype(jnp.int32)
+    head_me = lax.axis_index("head").reshape(1).astype(jnp.int32)
+    wu, zc, rows, mine, theirs = shard_pass(
+        seq_me, log_gate, write_rate, starts, key_rows, value_rows, per_key
     )
     outs, carries = [], []
 
-    def work(ready, coming):
+    def work(coming):
         key = len(outs)
-        if key < keys_here:
-            held, ready = lax.optimization_barrier((rows, ready))
-            out, carry = local_pass(key, held, queries, key_rows, wu, zc, per_key)
-            outs.append(out)
-            carries.append(carry)
-        return ready, coming
-
-    start = start_states(end, work)
+        if key == keys_here:
+            return coming
+        out, carry = local_pass(key, rows, queries, key_rows, wu, zc, per_key)
+        coming, out, carry = lax.optimization_barrier((coming, out, carry))
+        outs.append(out)
+        carries.append(carry)
+        return coming
+
+    own, back = start_states(seq_me, mine, theirs, work)
     while len(outs) < keys_here:
-        work(start, start)
-
-    me = lax.axis_index("head").reshape(1).astype(jnp.int32)
+        back = work(back)
+
+    me = jnp.concatenate([head_me, seq_me])
     chunks = 4
     rows_each = tokens_here // chunks
+    gain = norm_gain.reshape(1, DV)
+
+    def project(index, ready):
+        nonlocal back
+        if ready is not None:
+            back, ready = lax.optimization_barrier((back, ready))
+        pair = finish_pass(
+            index, rows_each, me, outs, carries, own, back, out_gate, gain, out_weight, per_key, groups
+        )
+        return ready, pair
+
     pieces = []
+    ready, (send, keep) = project(0, None)
     for index in range(chunks):
-        send, keep = finish_pass(
-            index, rows_each, me, outs, carries, start, out_gate,
-            norm_gain.reshape(1, DV), out_weight, per_key, groups,
-        )
+        following = None
         bit = 1
         while bit < groups:
             got = lax.ppermute(send, "head", route("head", lambda i: i ^ bit))
+            if bit == 1 and index + 1 < chunks:
+                following = project(index + 1, send)[1]
+                got, held = lax.optimization_barrier((got, following[0]))
+                following = (held, following[1])
             total = keep.astype(F32) + got.astype(F32)
             bit *= 2
             if bit < groups:
@@ -485,6 +587,8 @@
             else:
                 keep = total
         pieces.append(keep.astype(BF16))
+        if following is not None:
+            send, keep = following
     return jnp.concatenate(pieces, axis=0)
 
 

time: 121 us -> 111 us (0.917); the launches traced: 120 us -> 109 us
  waiting for transfers between devices: 32.3 us -> 23.5 us
  local copies, waits for them, and re-layouts: 16.6 us -> 22.3 us
  other arithmetic: 5.5 us -> 2.1 us
  Pallas kernels: 46.6 us -> 43.3 us
  starting transfers between devices: 19.2 us -> 17.6 us
    pallas_call x4 -> x3, Pallas kernels: 7.38 us -> 0.92 us  [the longest x2 0.73 us: small_call(): pl.pallas_call(kernel, grid=(1,), in_specs=[ONE] * len(scalars) + [plain(...]
    unnamed x34 -> x50, local copies, waits for them, and re-layouts: 15.7 us -> 22.1 us
    ppermute x3, waiting for transfers between devices: 6.56 us -> 0.91 us  [the longest x1 0.9 us: start_states(): return (own, work(lax.ppermute(other, 'seq', swap)))]
    select_n x5 -> x0, other arithmetic: 3.46 us -> none  [the longest x1 1.58 us: start_states(): here = jnp.where(pair == 2, near, compose(before, far))]
    pallas_call x4, Pallas kernels: 12.7 us -> 14.9 us  [finish_pass(): pl.pallas_call(functools.partial(finish_kernel, per_key, keys_here, half,...]
    ppermute x1, waiting for transfers between devices: 5.78 us -> 3.51 us  [start_states(): lax.ppermute(both, 'seq', route('seq', lambda i: i + 2 if i < 6 else None))]
    ppermute x3, starting transfers between devices: 8.26 us -> 6.67 us  [the longest x1 4.49 us: start_states(): far = work(lax.ppermute(third, 'seq', [(2, 6), (3, 7)]))]
    ppermute x8, waiting for transfers between devices: 20 us -> 18.6 us  [local(): got = lax.ppermute(send, 'head', route('head', lambda i: i ^ bit))]
  transfers between devices with their start and end apart: 13 -> 13, of which waited for: 6 -> 7; matrix products, arithmetic and copies ran while one was open for 1% -> 1% of each run, Pallas kernels for 15% -> 16%
where the time goes in v2:
time: 111 us; the launch traced here: 109 us
  Pallas kernels  43.3 us (39%)
  waiting for transfers between devices  23.5 us (21%)
  local copies, waits for them, and re-layouts  22.3 us (20%)
  starting transfers between devices  17.6 us (16%)
  other arithmetic  2.1 us (2%)
    unnamed x50, local copies, waits for them, and re-layouts  22.1 us
    pallas_call x1, Pallas kernels, shard_pass(): pl.pallas_call(functools.partial(shard_kernel, per_key, blocks, keys_here...  21 us
    ppermute x8, waiting for transfers between devices, local(): got = lax.ppermute(send, 'head', route('head', lambda i: i ^ bit))  18.6 us
    pallas_call x4, Pallas kernels, finish_pass(): pl.pallas_call(functools.partial(finish_kernel, per_key, keys_here, half,...  14.9 us
    pallas_call x4, Pallas kernels, local_pass(): pl.pallas_call(functools.partial(local_kernel, per_key, blocks), grid=(1,...  6.53 us
    ppermute x8, starting transfers between devices, local(): got = lax.ppermute(send, 'head', route('head', lambda i: i ^ bit))  6.09 us
    ppermute x1, starting transfers between devices, start_states(): far = work(lax.ppermute(third, 'seq', [(2, 6), (3, 7)]))  4.49 us
    ppermute x1, waiting for transfers between devices, start_states(): lax.ppermute(both, 'seq', route('seq', lambda i: i + 2 if i < 6 else None))  3.51 us
  transfers between devices with their start and end apart: 13, of which 7 were waited for; matrix products, arithmetic and copies ran while one was open for 1% of the time, Pallas kernels for 16%

profile of v2, /device:TPU:8, one launch (start us, length us, event | category | flops | bytes accessed | tf_op | source)
XLA Modules:
  0.0 109.2 jit_solution(1172339275152864292)
XLA Ops:
  0.0 21.0 %shard_pass.1 = (bf16[64,128,256]{2,1,0:T(8,128)(2,1)}, bf16[8,8,128,256]{3,2,1,0:T(8,128)(2,1)}, f32[4,40,128]{2,1,0:T(8,128)}, bf16[4,128,256]{2,1,0:T(8,128)(2,1)}, bf16[4,128,256]{2,1,0:T(8,128)(2,1)}) custom-call(s32[1]{0:T(128)} %bitcast.1.me_ref, f32[8,1024]{1,0:T(8,128)} %log_ref.1, f32[8,1024]{1,0:T(8,128)} %rate_ref.1, s32[8,128]{1,0:T(8,128)} %bitcast.8, ...), custom_call_target="tpu_custom_call" | custom-call | flops 4831838208 | bytes 12582912 | tf_op jit(solution)/shard_map/shard_pass/pallas_call | solution.py:188
  21.0 1.6 %collective-permute-start = (bf16[4,128,256]{2,1,0:T(8,128)(2,1)}, bf16[4,128,256]{2,1,0:T(8,128)(2,1)S(1)}, u32[]{:S(2)}, u32[]{:S(2)}) collective-permute-start(bf16[4,128,256]{2,1,0:T(8,128)(2,1)} %get-tuple-element.49), channel_id=1, source_target_pairs={{0,4},{4,0},{8,12},{12,8},{16,20},{20,16},{24,28},{28,24},{1,5},{5... | collective-permute-start | bytes 786440 | tf_op jit(solution)/shard_map/ppermute | solution.py:498
  22.5 2.2 %copy-done.1 = bf16[64,128,256]{2,1,0:T(8,128)(2,1)S(1)} copy-done((bf16[64,128,256]{2,1,0:T(8,128)(2,1)S(1)}, bf16[64,128,256]{2,1,0:T(8,128)(2,1)}, u32[]{:S(2)}) %copy-start.1) | copy-done | bytes 4194328
  24.7 2.2 %copy-done.2 = bf16[8,8,128,256]{3,2,1,0:T(8,128)(2,1)S(1)} copy-done((bf16[8,8,128,256]{3,2,1,0:T(8,128)(2,1)S(1)}, bf16[8,8,128,256]{3,2,1,0:T(8,128)(2,1)}, u32[]{:S(2)}) %copy-start.2) | copy-done | bytes 4194328
  26.9 1.2 %copy-done.5 = bf16[1024,512]{1,0:T(8,128)(2,1)S(1)} copy-done((bf16[1024,512]{1,0:T(8,128)(2,1)S(1)}, bf16[1024,512]{1,0:T(8,128)(2,1)}, u32[]{:S(2)}) %copy-start.5) | copy-done | bytes 1048600
  28.1 0.9 copy-done.22
  29.0 1.6 %local_pass.4 = (f32[1024,256]{1,0:T(8,128)S(1)}, bf16[1024,256]{1,0:T(8,128)(2,1)S(1)}) custom-call(f32[4,40,128]{2,1,0:T(8,128)S(1)} %copy-done.22, bf16[1024,512]{1,0:T(8,128)(2,1)S(1)} %copy-done.5, bf16[1024,512]{1,0:T(8,128)(2,1)S(1)} %copy-done.4, bf16[64,128,256]{2,1,0:T(8,128)(2,1)S(1)} %copy-done.1, bf16[8,8,128,256]{3,2,1,0:T(8,128)(2,1)S(1)} %copy-done.2), custom_call_target="tpu_custom_call" | custom-call | flops 536870912 | bytes 4194304 | tf_op jit(solution)/shard_map/local_pass/pallas_call | solution.py:267
  30.7 0.8 copy-done.14
  31.5 0.2 pair.1.later_ref
  31.7 3.5 %collective-permute-start.1 = (bf16[4,128,256]{2,1,0:T(8,128)(2,1)S(1)}, bf16[4,128,256]{2,1,0:T(8,128)(2,1)S(1)}, u32[]{:S(2)}, u32[]{:S(2)}) collective-permute-start(bf16[4,128,256]{2,1,0:T(8,128)(2,1)S(1)} %pair.1.later_ref), channel_id=1, source_target_pairs={{0,8},{4,12},{8,16},{12,20},{16,24},{20,28},{1,9},{5,13},{9,17},{1... | collective-permute-start | bytes 786440 | tf_op jit(solution)/shard_map/ppermute | solution.py:503
  35.2 1.6 %local_pass.5 = (f32[1024,256]{1,0:T(8,128)S(1)}, bf16[1024,256]{1,0:T(8,128)(2,1)S(1)}) custom-call(f32[4,40,128]{2,1,0:T(8,128)S(1)} %copy-done.22, bf16[1024,512]{1,0:T(8,128)(2,1)S(1)} %copy-done.5, bf16[1024,512]{1,0:T(8,128)(2,1)S(1)} %copy-done.4, bf16[64,128,256]{2,1,0:T(8,128)(2,1)S(1)} %copy-done.1, bf16[8,8,128,256]{3,2,1,0:T(8,128)(2,1)S(1)} %copy-done.2), custom_call_target="tpu_custom_call" | custom-call | flops 536870912 | bytes 4194304 | tf_op jit(solution)/shard_map/local_pass/pallas_call | solution.py:267
  36.8 1.0 copy-done.8
  37.8 3.5 %collective-permute-done.1.earlier_ref.before_ref = bf16[4,128,256]{2,1,0:T(8,128)(2,1)S(1)} collective-permute-done((bf16[4,128,256]{2,1,0:T(8,128)(2,1)S(1)}, bf16[4,128,256]{2,1,0:T(8,128)(2,1)S(1)}, u32[]{:S(2)}, u32[]{:S(2)}) %collective-permute-start.1) | collective-permute-done | bytes 262176 | tf_op jit(solution)/shard_map/ppermute | solution.py:503
  41.4 0.2 step.1
  41.6 4.5 %collective-permute-start.2 = (bf16[4,128,128]{2,1,0:T(8,128)(2,1)S(1)}, bf16[4,128,128]{2,1,0:T(8,128)(2,1)S(1)}, u32[]{:S(2)}, u32[]{:S(2)}) collective-permute-start(bf16[4,128,128]{2,1,0:T(8,128)(2,1)S(1)} %step.1), channel_id=1, source_target_pairs={{8,24},{12,28},{9,25},{13,29},{10,26},{14,30},{11,27},{15,31}} | collective-permute-start | bytes 393224 | tf_op jit(solution)/shard_map/ppermute | solution.py:507
  46.1 1.3 %collective-permute-start.3 = (bf16[4,128,128]{2,1,0:T(8,128)(2,1)S(1)}, bf16[4,128,128]{2,1,0:T(8,128)(2,1)S(1)}, u32[]{:S(2)}, u32[]{:S(2)}) collective-permute-start(bf16[4,128,128]{2,1,0:T(8,128)(2,1)S(1)} %step.1), channel_id=1, source_target_pairs={{8,16},{12,20},{9,17},{13,21},{10,18},{14,22},{11,19},{15,23}} | collective-permute-start | bytes 393224 | tf_op jit(solution)/shard_map/ppermute | solution.py:506
  47.4 1.6 %local_pass.6 = (f32[1024,256]{1,0:T(8,128)S(1)}, bf16[1024,256]{1,0:T(8,128)(2,1)S(1)}) custom-call(f32[4,40,128]{2,1,0:T(8,128)S(1)} %copy-done.22, bf16[1024,512]{1,0:T(8,128)(2,1)S(1)} %copy-done.5, bf16[1024,512]{1,0:T(8,128)(2,1)S(1)} %copy-done.4, bf16[64,128,256]{2,1,0:T(8,128)(2,1)S(1)} %copy-done.1, bf16[8,8,128,256]{3,2,1,0:T(8,128)(2,1)S(1)} %copy-done.2), custom_call_target="tpu_custom_call" | custom-call | flops 536870912 | bytes 4194304 | tf_op jit(solution)/shard_map/local_pass/pallas_call | solution.py:267
  49.0 0.8 copy-done.18
  49.8 0.6 collective-permute-done.3.near_ref
  50.4 0.5 last.1
  50.9 0.0 copy-start.3
  50.9 0.0 copy-start.24
  50.9 0.6 collective-permute-start.4
  51.6 1.6 %local_pass.7 = (f32[1024,256]{1,0:T(8,128)S(1)}, bf16[1024,256]{1,0:T(8,128)(2,1)S(1)}) custom-call(f32[4,40,128]{2,1,0:T(8,128)S(1)} %copy-done.22, bf16[1024,512]{1,0:T(8,128)(2,1)S(1)} %copy-done.5, bf16[1024,512]{1,0:T(8,128)(2,1)S(1)} %copy-done.4, bf16[64,128,256]{2,1,0:T(8,128)(2,1)S(1)} %copy-done.1, bf16[8,8,128,256]{3,2,1,0:T(8,128)(2,1)S(1)} %copy-done.2), custom_call_target="tpu_custom_call" | custom-call | flops 536870912 | bytes 4194304 | tf_op jit(solution)/shard_map/local_pass/pallas_call | solution.py:267
  53.2 1.0 copy-done.12
  54.2 0.8 copy-done.20
  55.0 0.1 pad_add_fusion.me_ref
  55.1 0.9 collective-permute-done.4.refs_9_
  56.0 2.2 %copy-done = bf16[1024,2048]{1,0:T(8,128)(2,1)S(1)} copy-done((bf16[1024,2048]{1,0:T(8,128)(2,1)S(1)}, bf16[1024,2048]{1,0:T(8,128)(2,1)}, u32[]{:S(2)}) %copy-start) | copy-done | bytes 4194328
  58.2 1.2 %copy-done.7 = f32[1024,256]{1,0:T(8,128)S(1)} copy-done((f32[1024,256]{1,0:T(8,128)S(1)}, f32[1024,256]{1,0:T(8,128)}, u32[]{:S(2)}) %copy-start.7) | copy-done | bytes 1048600
  59.4 1.2 %copy-done.9 = f32[1024,256]{1,0:T(8,128)S(1)} copy-done((f32[1024,256]{1,0:T(8,128)S(1)}, f32[1024,256]{1,0:T(8,128)}, u32[]{:S(2)}) %copy-start.9) | copy-done | bytes 1048600
  60.6 1.2 %copy-done.11 = f32[1024,256]{1,0:T(8,128)S(1)} copy-done((f32[1024,256]{1,0:T(8,128)S(1)}, f32[1024,256]{1,0:T(8,128)}, u32[]{:S(2)}) %copy-start.11) | copy-done | bytes 1048600
  61.9 1.2 %copy-done.13 = f32[1024,256]{1,0:T(8,128)S(1)} copy-done((f32[1024,256]{1,0:T(8,128)S(1)}, f32[1024,256]{1,0:T(8,128)}, u32[]{:S(2)}) %copy-start.13) | copy-done | bytes 1048600
  63.1 1.0 copy-done.15
  64.1 1.0 copy-done.17
  65.2 1.0 copy-done.19
  66.2 1.0 copy-done.21
  67.2 3.7 %finish_pass.4 = (bf16[256,1024]{1,0:T(8,128)(2,1)S(1)}, bf16[256,1024]{1,0:T(8,128)(2,1)S(1)}) custom-call(s32[2]{0:T(128)S(1)} %pad_add_fusion.me_ref, f32[1024,256]{1,0:T(8,128)S(1)} %copy-done.7, f32[1024,256]{1,0:T(8,128)S(1)} %copy-done.9, f32[1024,256]{1,0:T(8,128)S(1)} %copy-done.11, f32[1024,256]{1,0:T(8,128)S(1)} %copy-done.13, ...), custom_call_target="tpu_custom_call" | custom-call | flops 1073741824 | bytes 8388608 | tf_op jit(solution)/shard_map/finish_pass/pallas_call | solution.py:381
  71.0 0.1 collective-permute-start.5
  71.1 3.7 %finish_pass.5 = (bf16[256,1024]{1,0:T(8,128)(2,1)S(1)}, bf16[256,1024]{1,0:T(8,128)(2,1)S(1)}) custom-call(s32[2]{0:T(128)S(1)} %pad_add_fusion.me_ref, f32[1024,256]{1,0:T(8,128)S(1)} %copy-done.7, f32[1024,256]{1,0:T(8,128)S(1)} %copy-done.9, f32[1024,256]{1,0:T(8,128)S(1)} %copy-done.11, f32[1024,256]{1,0:T(8,128)S(1)} %copy-done.13, ...), custom_call_target="tpu_custom_call" | custom-call | flops 1073741824 | bytes 8388608 | tf_op jit(solution)/shard_map/finish_pass/pallas_call | solution.py:381
  74.8 0.0 collective-permute-done.5
  74.8 0.6 collective-permute-start.7
  75.4 0.2 convert_add_fusion.3
  75.6 1.6 %collective-permute-start.6 = (bf16[256,512]{1,0:T(8,128)(2,1)S(1)}, bf16[256,512]{1,0:T(8,128)(2,1)S(1)}, u32[]{:S(2)}, u32[]{:S(2)}) collective-permute-start(bf16[256,512]{1,0:T(8,128)(2,1)S(1)} %slice.63), channel_id=1, source_target_pairs={{0,2},{1,3},{2,0},{3,1},{4,6},{5,7},{6,4},{7,5},{8,10},{9,11},{10,... | collective-permute-start | bytes 786440 | tf_op jit(solution)/shard_map/ppermute | solution.py:576
  77.2 3.7 %finish_pass.6 = (bf16[256,1024]{1,0:T(8,128)(2,1)S(1)}, bf16[256,1024]{1,0:T(8,128)(2,1)S(1)}) custom-call(s32[2]{0:T(128)S(1)} %pad_add_fusion.me_ref, f32[1024,256]{1,0:T(8,128)S(1)} %copy-done.7, f32[1024,256]{1,0:T(8,128)S(1)} %copy-done.9, f32[1024,256]{1,0:T(8,128)S(1)} %copy-done.11, f32[1024,256]{1,0:T(8,128)S(1)} %copy-done.13, ...), custom_call_target="tpu_custom_call" | custom-call | flops 1073741824 | bytes 8388608 | tf_op jit(solution)/shard_map/finish_pass/pallas_call | solution.py:381
  80.9 0.0 collective-permute-done.7
  80.9 0.1 collective-permute-start.9
  81.0 2.9 %collective-permute-done.6 = bf16[256,512]{1,0:T(8,128)(2,1)S(1)} collective-permute-done((bf16[256,512]{1,0:T(8,128)(2,1)S(1)}, bf16[256,512]{1,0:T(8,128)(2,1)S(1)}, u32[]{:S(2)}, u32[]{:S(2)}) %collective-permute-start.6) | collective-permute-done | bytes 262176 | tf_op jit(solution)/shard_map/ppermute | solution.py:576
  83.9 0.1 fusion.3
  84.0 3.7 %finish_pass.7 = (bf16[256,1024]{1,0:T(8,128)(2,1)S(1)}, bf16[256,1024]{1,0:T(8,128)(2,1)S(1)}) custom-call(s32[2]{0:T(128)S(1)} %pad_add_fusion.me_ref, f32[1024,256]{1,0:T(8,128)S(1)} %copy-done.7, f32[1024,256]{1,0:T(8,128)S(1)} %copy-done.9, f32[1024,256]{1,0:T(8,128)S(1)} %copy-done.11, f32[1024,256]{1,0:T(8,128)S(1)} %copy-done.13, ...), custom_call_target="tpu_custom_call" | custom-call | flops 1073741824 | bytes 8388608 | tf_op jit(solution)/shard_map/finish_pass/pallas_call | solution.py:381
  87.7 0.1 collective-permute-start.11
  87.8 0.2 convert_add_fusion.2
  88.0 1.6 %collective-permute-start.8 = (bf16[256,512]{1,0:T(8,128)(2,1)S(1)}, bf16[256,512]{1,0:T(8,128)(2,1)S(1)}, u32[]{:S(2)}, u32[]{:S(2)}) collective-permute-start(bf16[256,512]{1,0:T(8,128)(2,1)S(1)} %slice.62), channel_id=1, source_target_pairs={{0,2},{1,3},{2,0},{3,1},{4,6},{5,7},{6,4},{7,5},{8,10},{9,11},{10,... | collective-permute-start | bytes 786440 | tf_op jit(solution)/shard_map/ppermute | solution.py:576
  89.6 0.2 convert_add_fusion.1
  89.8 0.6 collective-permute-start.10
  90.4 0.2 convert_add_fusion
  90.6 1.6 %collective-permute-start.12 = (bf16[256,512]{1,0:T(8,128)(2,1)S(1)}, bf16[256,512]{1,0:T(8,128)(2,1)S(1)}, u32[]{:S(2)}, u32[]{:S(2)}) collective-permute-start(bf16[256,512]{1,0:T(8,128)(2,1)S(1)} %slice.60), channel_id=1, source_target_pairs={{0,2},{1,3},{2,0},{3,1},{4,6},{5,7},{6,4},{7,5},{8,10},{9,11},{10,... | collective-permute-start | bytes 786440 | tf_op jit(solution)/shard_map/ppermute | solution.py:576
  92.2 5.0 %collective-permute-done.8 = bf16[256,512]{1,0:T(8,128)(2,1)S(1)} collective-permute-done((bf16[256,512]{1,0:T(8,128)(2,1)S(1)}, bf16[256,512]{1,0:T(8,128)(2,1)S(1)}, u32[]{:S(2)}, u32[]{:S(2)}) %collective-permute-start.8) | collective-permute-done | bytes 262176 | tf_op jit(solution)/shard_map/ppermute | solution.py:576
  97.2 0.1 fusion.2
  97.3 5.5 %collective-permute-done.10 = bf16[256,512]{1,0:T(8,128)(2,1)S(1)} collective-permute-done((bf16[256,512]{1,0:T(8,128)(2,1)S(1)}, bf16[256,512]{1,0:T(8,128)(2,1)S(1)}, u32[]{:S(2)}, u32[]{:S(2)}) %collective-permute-start.10) | collective-permute-done | bytes 262176 | tf_op jit(solution)/shard_map/ppermute | solution.py:576
  102.8 0.1 fusion.1
  102.9 5.1 %collective-permute-done.12 = bf16[256,512]{1,0:T(8,128)(2,1)S(1)} collective-permute-done((bf16[256,512]{1,0:T(8,128)(2,1)S(1)}, bf16[256,512]{1,0:T(8,128)(2,1)S(1)}, u32[]{:S(2)}, u32[]{:S(2)}) %collective-permute-start.12) | collective-permute-done | bytes 262176 | tf_op jit(solution)/shard_map/ppermute | solution.py:576
  108.0 0.1 fusion
  108.1 1.0 pad_maximum_fusion
  (38 shorter events, 0.2 us)
Async XLA Ops:
  0.0 22.5 %copy-start.4 = (bf16[1024,512]{1,0:T(8,128)(2,1)S(1)}, bf16[1024,512]{1,0:T(8,128)(2,1)}, u32[]{:S(2)}) copy-start(bf16[1024,512]{1,0:T(8,128)(2,1)} %k_ref.9) | copy-start | bytes 3145732
  21.0 10.5 %collective-permute-start = (bf16[4,128,256]{2,1,0:T(8,128)(2,1)}, bf16[4,128,256]{2,1,0:T(8,128)(2,1)S(1)}, u32[]{:S(2)}, u32[]{:S(2)}) collective-permute-start(bf16[4,128,256]{2,1,0:T(8,128)(2,1)} %get-tuple-element.49), channel_id=1, source_target_pairs={{0,4},{4,0},{8,12},{12,8},{16,20},{20,16},{24,28},{28,24},{1,5},{5... | collective-permute-start | bytes 786440 | tf_op jit(solution)/shard_map/ppermute | solution.py:498
  22.5 2.2 %copy-start.1 = (bf16[64,128,256]{2,1,0:T(8,128)(2,1)S(1)}, bf16[64,128,256]{2,1,0:T(8,128)(2,1)}, u32[]{:S(2)}) copy-start(bf16[64,128,256]{2,1,0:T(8,128)(2,1)} %get-tuple-element.51.wu_ref) | copy-start | bytes 12582916
  24.7 2.2 %copy-start.2 = (bf16[8,8,128,256]{3,2,1,0:T(8,128)(2,1)S(1)}, bf16[8,8,128,256]{3,2,1,0:T(8,128)(2,1)}, u32[]{:S(2)}) copy-start(bf16[8,8,128,256]{3,2,1,0:T(8,128)(2,1)} %get-tuple-element.52.zc_ref) | copy-start | bytes 12582916
  26.9 1.2 %copy-start.5 = (bf16[1024,512]{1,0:T(8,128)(2,1)S(1)}, bf16[1024,512]{1,0:T(8,128)(2,1)}, u32[]{:S(2)}) copy-start(bf16[1024,512]{1,0:T(8,128)(2,1)} %q_ref.7) | copy-start | bytes 3145732
  28.1 0.9 copy-start.22
  29.0 2.4 %copy-start.23 = (bf16[4,128,256]{2,1,0:T(8,128)(2,1)S(1)}, bf16[4,128,256]{2,1,0:T(8,128)(2,1)}, u32[]{:S(2)}) copy-start(bf16[4,128,256]{2,1,0:T(8,128)(2,1)} %get-tuple-element.56.mine_ref) | copy-start | bytes 786436
  30.7 0.8 copy-start.14
  31.5 5.4 %copy-start.6 = (f32[1024,256]{1,0:T(8,128)}, f32[1024,256]{1,0:T(8,128)S(1)}, u32[]{:S(2)}) copy-start(f32[1024,256]{1,0:T(8,128)S(1)} %get-tuple-element.55.refs_0_) | copy-start | bytes 3145732
  31.7 9.7 %collective-permute-start.1 = (bf16[4,128,256]{2,1,0:T(8,128)(2,1)S(1)}, bf16[4,128,256]{2,1,0:T(8,128)(2,1)S(1)}, u32[]{:S(2)}, u32[]{:S(2)}) collective-permute-start(bf16[4,128,256]{2,1,0:T(8,128)(2,1)S(1)} %pair.1.later_ref), channel_id=1, source_target_pairs={{0,8},{4,12},{8,16},{12,20},{16,24},{20,28},{1,9},{5,13},{9,17},{1... | collective-permute-start | bytes 786440 | tf_op jit(solution)/shard_map/ppermute | solution.py:503
  36.8 1.0 copy-start.8
  37.8 8.2 %copy-start.16 = (bf16[1024,256]{1,0:T(8,128)(2,1)}, bf16[1024,256]{1,0:T(8,128)(2,1)S(1)}, u32[]{:S(2)}) copy-start(bf16[1024,256]{1,0:T(8,128)(2,1)S(1)} %get-tuple-element.71.refs_5_) | copy-start | bytes 1572868
  41.6 8.3 %collective-permute-start.2 = (bf16[4,128,128]{2,1,0:T(8,128)(2,1)S(1)}, bf16[4,128,128]{2,1,0:T(8,128)(2,1)S(1)}, u32[]{:S(2)}, u32[]{:S(2)}) collective-permute-start(bf16[4,128,128]{2,1,0:T(8,128)(2,1)S(1)} %step.1), channel_id=1, source_target_pairs={{8,24},{12,28},{9,25},{13,29},{10,26},{14,30},{11,27},{15,31}} | collective-permute-start | bytes 393224 | tf_op jit(solution)/shard_map/ppermute | solution.py:507
  46.1 4.3 %collective-permute-start.3 = (bf16[4,128,128]{2,1,0:T(8,128)(2,1)S(1)}, bf16[4,128,128]{2,1,0:T(8,128)(2,1)S(1)}, u32[]{:S(2)}, u32[]{:S(2)}) collective-permute-start(bf16[4,128,128]{2,1,0:T(8,128)(2,1)S(1)} %step.1), channel_id=1, source_target_pairs={{8,16},{12,20},{9,17},{13,21},{10,18},{14,22},{11,19},{15,23}} | collective-permute-start | bytes 393224 | tf_op jit(solution)/shard_map/ppermute | solution.py:506
  49.0 0.8 copy-start.18
  49.8 1.1 %copy-start.10 = (f32[1024,256]{1,0:T(8,128)}, f32[1024,256]{1,0:T(8,128)S(1)}, u32[]{:S(2)}) copy-start(f32[1024,256]{1,0:T(8,128)S(1)} %get-tuple-element.64.refs_2_) | copy-start | bytes 3145732
  50.9 5.1 %copy-start.3 = (bf16[1024,1024]{1,0:T(8,128)(2,1)S(1)}, bf16[1024,1024]{1,0:T(8,128)(2,1)}, u32[]{:S(2)}) copy-start(bf16[1024,1024]{1,0:T(8,128)(2,1)} %refs_10_.7) | copy-start | bytes 6291460
  50.9 5.1 %copy-start.24 = (f32[128]{0:T(128)S(1)}, f32[128]{0:T(128)}, u32[]{:S(2)}) copy-start(f32[128]{0:T(128)} %param.16) | copy-start | bytes 1540
  50.9 5.0 %collective-permute-start.4 = (bf16[4,128,128]{2,1,0:T(8,128)(2,1)S(1)}, bf16[4,128,128]{2,1,0:T(8,128)(2,1)S(1)}, u32[]{:S(2)}, u32[]{:S(2)}) collective-permute-start(bf16[4,128,128]{2,1,0:T(8,128)(2,1)S(1)} %get-tuple-element.66), channel_id=1, source_target_pairs={{0,4},{4,0},{8,12},{12,8},{16,20},{20,16},{24,28},{28,24},{1,5},{5... | collective-permute-start | bytes 393224 | tf_op jit(solution)/shard_map/ppermute | solution.py:511
  53.2 1.0 copy-start.12
  54.2 0.8 copy-start.20
  56.0 2.2 %copy-start = (bf16[1024,2048]{1,0:T(8,128)(2,1)S(1)}, bf16[1024,2048]{1,0:T(8,128)(2,1)}, u32[]{:S(2)}) copy-start(bf16[1024,2048]{1,0:T(8,128)(2,1)} %refs_12_.7) | copy-start | bytes 12582916
  58.2 1.2 %copy-start.7 = (f32[1024,256]{1,0:T(8,128)S(1)}, f32[1024,256]{1,0:T(8,128)}, u32[]{:S(2)}) copy-start(f32[1024,256]{1,0:T(8,128)} %copy-done.6) | copy-start | bytes 3145732
  59.4 1.2 %copy-start.9 = (f32[1024,256]{1,0:T(8,128)S(1)}, f32[1024,256]{1,0:T(8,128)}, u32[]{:S(2)}) copy-start(f32[1024,256]{1,0:T(8,128)} %copy-done.8) | copy-start | bytes 3145732
  60.6 1.2 %copy-start.11 = (f32[1024,256]{1,0:T(8,128)S(1)}, f32[1024,256]{1,0:T(8,128)}, u32[]{:S(2)}) copy-start(f32[1024,256]{1,0:T(8,128)} %copy-done.10) | copy-start | bytes 3145732
  61.9 1.2 %copy-start.13 = (f32[1024,256]{1,0:T(8,128)S(1)}, f32[1024,256]{1,0:T(8,128)}, u32[]{:S(2)}) copy-start(f32[1024,256]{1,0:T(8,128)} %copy-done.12) | copy-start | bytes 3145732
  63.1 1.0 copy-start.15
  64.1 1.0 copy-start.17
  65.2 1.0 copy-start.19
  66.2 1.0 copy-start.21
  71.0 3.8 %collective-permute-start.5 = (bf16[256,1024]{1,0:T(8,128)(2,1)S(1)}, bf16[256,1024]{1,0:T(8,128)(2,1)S(1)}, u32[]{:S(2)}, u32[]{:S(2)}) collective-permute-start(bf16[256,1024]{1,0:T(8,128)(2,1)S(1)} %get-tuple-element.77), channel_id=1, source_target_pairs={{0,1},{1,0},{2,3},{3,2},{4,5},{5,4},{6,7},{7,6},{8,9},{9,8},{10,11... | collective-permute-start | bytes 1572872 | tf_op jit(solution)/shard_map/ppermute | solution.py:576
  74.8 6.1 %collective-permute-start.7 = (bf16[256,1024]{1,0:T(8,128)(2,1)S(1)}, bf16[256,1024]{1,0:T(8,128)(2,1)S(1)}, u32[]{:S(2)}, u32[]{:S(2)}) collective-permute-start(bf16[256,1024]{1,0:T(8,128)(2,1)S(1)} %get-tuple-element.82), channel_id=1, source_target_pairs={{0,1},{1,0},{2,3},{3,2},{4,5},{5,4},{6,7},{7,6},{8,9},{9,8},{10,11... | collective-permute-start | bytes 1572872 | tf_op jit(solution)/shard_map/ppermute | solution.py:576
  75.6 8.3 %collective-permute-start.6 = (bf16[256,512]{1,0:T(8,128)(2,1)S(1)}, bf16[256,512]{1,0:T(8,128)(2,1)S(1)}, u32[]{:S(2)}, u32[]{:S(2)}) collective-permute-start(bf16[256,512]{1,0:T(8,128)(2,1)S(1)} %slice.63), channel_id=1, source_target_pairs={{0,2},{1,3},{2,0},{3,1},{4,6},{5,7},{6,4},{7,5},{8,10},{9,11},{10,... | collective-permute-start | bytes 786440 | tf_op jit(solution)/shard_map/ppermute | solution.py:576
  80.9 6.8 %collective-permute-start.9 = (bf16[256,1024]{1,0:T(8,128)(2,1)S(1)}, bf16[256,1024]{1,0:T(8,128)(2,1)S(1)}, u32[]{:S(2)}, u32[]{:S(2)}) collective-permute-start(bf16[256,1024]{1,0:T(8,128)(2,1)S(1)} %get-tuple-element.87), channel_id=1, source_target_pairs={{0,1},{1,0},{2,3},{3,2},{4,5},{5,4},{6,7},{7,6},{8,9},{9,8},{10,11... | collective-permute-start | bytes 1572872 | tf_op jit(solution)/shard_map/ppermute | solution.py:576
  87.7 2.7 %collective-permute-start.11 = (bf16[256,1024]{1,0:T(8,128)(2,1)S(1)}, bf16[256,1024]{1,0:T(8,128)(2,1)S(1)}, u32[]{:S(2)}, u32[]{:S(2)}) collective-permute-start(bf16[256,1024]{1,0:T(8,128)(2,1)S(1)} %get-tuple-element.92), channel_id=1, source_target_pairs={{0,1},{1,0},{2,3},{3,2},{4,5},{5,4},{6,7},{7,6},{8,9},{9,8},{10,11... | collective-permute-start | bytes 1572872 | tf_op jit(solution)/shard_map/ppermute | solution.py:576
  88.0 9.2 %collective-permute-start.8 = (bf16[256,512]{1,0:T(8,128)(2,1)S(1)}, bf16[256,512]{1,0:T(8,128)(2,1)S(1)}, u32[]{:S(2)}, u32[]{:S(2)}) collective-permute-start(bf16[256,512]{1,0:T(8,128)(2,1)S(1)} %slice.62), channel_id=1, source_target_pairs={{0,2},{1,3},{2,0},{3,1},{4,6},{5,7},{6,4},{7,5},{8,10},{9,11},{10,... | collective-permute-start | bytes 786440 | tf_op jit(solution)/shard_map/ppermute | solution.py:576
  89.8 13.0 %collective-permute-start.10 = (bf16[256,512]{1,0:T(8,128)(2,1)S(1)}, bf16[256,512]{1,0:T(8,128)(2,1)S(1)}, u32[]{:S(2)}, u32[]{:S(2)}) collective-permute-start(bf16[256,512]{1,0:T(8,128)(2,1)S(1)} %slice.61), channel_id=1, source_target_pairs={{0,2},{1,3},{2,0},{3,1},{4,6},{5,7},{6,4},{7,5},{8,10},{9,11},{10,... | collective-permute-start | bytes 786440 | tf_op jit(solution)/shard_map/ppermute | solution.py:576
  90.6 17.4 %collective-permute-start.12 = (bf16[256,512]{1,0:T(8,128)(2,1)S(1)}, bf16[256,512]{1,0:T(8,128)(2,1)S(1)}, u32[]{:S(2)}, u32[]{:S(2)}) collective-permute-start(bf16[256,512]{1,0:T(8,128)(2,1)S(1)} %slice.60), channel_id=1, source_target_pairs={{0,2},{1,3},{2,0},{3,1},{4,6},{5,7},{6,4},{7,5},{8,10},{9,11},{10,... | collective-permute-start | bytes 786440 | tf_op jit(solution)/shard_map/ppermute | solution.py:576

commit v3 on v2

v3 whole, which is shorter than its diff:
```python
import functools

import jax
import jax.numpy as jnp
from jax import lax
from jax.experimental import pallas as pl
from jax.experimental.pallas import tpu as pltpu
from jax.sharding import PartitionSpec as P

DK = 128
DV = 128
BLK = 128
SUB = 16
EPS = 1e-06
FAR = -1e30
F32 = jnp.float32
BF16 = jnp.bfloat16
MIB = 1024 * 1024


def dot(a, b):
    return jnp.dot(a, b, preferred_element_type=F32)


def dot_t(a, b):
    return lax.dot_general(a, b, (((1,), (1,)), ((), ())), preferred_element_type=F32)


def running_sum(values):
    lane = lax.broadcasted_iota(jnp.int32, values.shape, 1)
    step = 1
    while step < BLK:
        values = values + jnp.where(lane >= step, pltpu.roll(values, step, 1), 0.0)
        step *= 2
    return values


def columns_of(rows):
    pad = BLK - rows.shape[0]
    return jnp.transpose(jnp.concatenate([rows, jnp.zeros((pad, BLK), F32)], axis=0))


def doc_mask(reset_col, reset_row, strict):
    i = lax.broadcasted_iota(jnp.int32, (BLK, BLK), 0)
    j = lax.broadcasted_iota(jnp.int32, (BLK, BLK), 1)
    below = (i > j) if strict else (i >= j)
    return jnp.where(below & (reset_col == reset_row), 0.0, FAR)


def small_inverses(lower, count):
    lane = lax.broadcasted_iota(jnp.int32, (SUB, BLK), 1)
    packed = []
    for m in lower:
        kept = m[:SUB]
        for b in range(1, BLK // SUB):
            kept = jnp.where(lane // SUB == b, m[b * SUB : (b + 1) * SUB], kept)
        packed.append(kept.astype(BF16))
    packed = jnp.concatenate(packed, axis=0)
    i = lax.broadcasted_iota(jnp.int32, (BLK, BLK), 0)
    j = lax.broadcasted_iota(jnp.int32, (BLK, BLK), 1)
    same = i // SUB == j // SUB
    place = lax.broadcasted_iota(jnp.int32, (count, SUB, BLK), 1)
    lanes = lax.broadcasted_iota(jnp.int32, (count, SUB, BLK), 2)
    found = jnp.where(place == lanes % SUB, 1.0, 0.0)
    for m in range(0, SUB, 2):
        spread = [jnp.where(same & (i % SUB == m + d), 1.0, 0.0).astype(BF16) for d in range(2)]
        pair = dot(packed, jnp.concatenate(spread, axis=1)).reshape(count, SUB, 2 * BLK)
        for d in range(2):
            if m + d < SUB - 1:
                found = found - pair[:, :, d * BLK : (d + 1) * BLK] * found[:, m + d : m + d + 1, :]
    return found.astype(BF16)


def odd_rows(matrix, size):
    return jnp.concatenate(
        [matrix[p : p + size] for p in range(size, BLK, 2 * size)], axis=0
    )


def with_odd_rows(matrix, rows, size):
    parts = []
    for p in range(0, BLK, 2 * size):
        parts.append(matrix[p : p + size])
        parts.append(rows[p // 2 : p // 2 + size])
    return jnp.concatenate(parts, axis=0)


def shard_kernel(
    first, per_key, blocks, keys,
    me_ref, log_ref, rate_ref, start_ref, k_ref, v_ref,
    wu_ref, zc_ref, rows_ref, mine_ref, theirs_ref,
    logs, rates, norms, kt, db, keep, state,
):
    heads = keys * per_key
    count = heads * blocks
    for h in range(heads):
        head = first * per_key + h
        for c in range(blocks):
            at = h * blocks + c
            span = slice(c * BLK, (c + 1) * BLK)
            logs[at : at + 1, :] = log_ref[head : head + 1, span]
            rates[at : at + 1, :] = rate_ref[head : head + 1, span]

    starts = start_ref[...].astype(F32)
    sums = running_sum(jnp.concatenate([logs[...], starts], axis=0))
    cum, reset = sums[:count], sums[count:]
    inner = []
    for key in range(keys):
        for c in range(blocks):
            rows = k_ref[c * BLK : (c + 1) * BLK, key * DK : (key + 1) * DK]
            flipped = jnp.transpose(rows.astype(F32))
            turned = flipped.astype(BF16)
            kt[key * blocks + c] = turned
            norms[key * blocks + c : key * blocks + c + 1, :] = jnp.sum(
                flipped * flipped, axis=0, keepdims=True
            )
            inner.append(dot(rows, turned))
    reset_cols = columns_of(reset)
    masks = [doc_mask(reset_cols[:, c : c + 1], reset[c : c + 1, :], True) for c in range(blocks)]

    squares = norms[...] + EPS
    squares = jnp.concatenate(
        [squares[(h // per_key) * blocks : (h // per_key + 1) * blocks] for h in range(heads)], axis=0
    )
    scale = lax.rsqrt(squares)
    log_scale = -0.5 * jnp.log(squares)
    resets = jnp.concatenate([reset] * heads, axis=0)
    rate = rates[...]
    last = cum[:, BLK - 1 :]
    last_reset = resets[:, BLK - 1 :]
    left_cols = columns_of(cum + jnp.log(rate) + log_scale)
    right = cum - log_scale
    head_keep = jnp.where(resets == 0.0, jnp.exp(cum), 0.0)
    tail = jnp.where(resets == last_reset, jnp.exp(last - cum), 0.0) * scale
    erase_row = rate * head_keep * scale
    keep[...] = jnp.broadcast_to(jnp.where(last_reset == 0.0, jnp.exp(last), 0.0), (count, BLK))
    rows_ref[0:count, :] = cum
    rows_ref[count : 2 * count, :] = right
    rows_ref[2 * count :, :] = reset

    lower = []
    for at in range(count):
        c = at % blocks
        gap = left_cols[:, at : at + 1] - right[at : at + 1, :] + masks[c]
        lower.append(inner[at // (per_key * blocks) * blocks + c] * jnp.exp(gap))
    packed = small_inverses(lower, count)
    lower = [m.astype(BF16) for m in lower]
    lane = lax.broadcasted_iota(jnp.int32, (SUB, BLK), 1)
    zero = jnp.zeros((SUB, BLK), BF16)
    ones = [jnp.where(lane // SUB == b, 1.0, 0.0).astype(BF16) for b in range(BLK // SUB)]
    inverse = [
        jnp.concatenate([packed[at] * ones[b] for b in range(BLK // SUB)], axis=0)
        for at in range(count)
    ]
    size = SUB
    while size < BLK:
        i = lax.broadcasted_iota(jnp.int32, (BLK // 2, BLK), 0)
        j = lax.broadcasted_iota(jnp.int32, (BLK // 2, BLK), 1)
        reach = jnp.where(j // size == 2 * (i // size), 1.0, 0.0).astype(BF16)
        odd = [odd_rows(t, size) for t in inverse]
        half = [dot(o, m).astype(BF16) * reach for o, m in zip(odd, lower)]
        fresh = [o - dot(f, t).astype(BF16) for o, f, t in zip(odd, half, inverse)]
        inverse = [with_odd_rows(t, f, size) for t, f in zip(inverse, fresh)]
        size *= 2
    for at in range(count):
        c, h = at % blocks, at // blocks
        key = h // per_key
        span = slice(c * BLK, (c + 1) * BLK)
        t = inverse[at].astype(F32)
        erase = dot(
            (t * erase_row[at : at + 1, :]).astype(BF16), k_ref[span, key * DK : (key + 1) * DK]
        )
        write = dot((t * rate[at : at + 1, :]).astype(BF16), v_ref[span, h * DV : (h + 1) * DV])
        wu_ref[at, :, :DK] = erase.astype(BF16)
        wu_ref[at, :, DK:] = write.astype(BF16)
    for at in range(count):
        c, key = at % blocks, at // (per_key * blocks)
        tailed = (kt[key * blocks + c].astype(F32) * tail[at : at + 1, :]).astype(BF16)
        db[at] = dot(tailed, wu_ref[at]).astype(BF16)

    i = lax.broadcasted_iota(jnp.int32, (DK, DK), 0)
    j = lax.broadcasted_iota(jnp.int32, (DK, DK), 1)
    for h in range(heads):
        state[h, :, :DV] = jnp.zeros((DK, DV), F32)
        state[h, :, DV:] = jnp.where(i == j, 1.0, 0.0)
    for c in range(blocks):
        for h in range(heads):
            now = state[h]
            low = now.astype(BF16)
            at = h * blocks + c
            zc_ref[at] = low
            moved = dot(db[at, :, :DK], low)
            g = keep[at : at + 1, :]
            state[h, :, :DV] = g * now[:, :DV] - moved[:, :DV] + db[at, :, DK:].astype(F32)
            state[h, :, DV:] = g * now[:, DV:] - moved[:, DV:]
    half = heads // 2
    odd = lax.rem(me_ref[0], 2) == 1
    for h in range(heads):
        ends = state[h].astype(BF16)
        ours = odd if h >= half else jnp.logical_not(odd)

        @pl.when(ours)
        def _():
            mine_ref[h % half] = ends

        @pl.when(jnp.logical_not(ours))
        def _():
            theirs_ref[h % half] = ends


def vmem(shape, dtype):
    return pltpu.VMEM(shape, dtype)


def in_hbm(array):
    return pltpu.with_memory_space_constraint(array, pltpu.HBM)


def in_vmem():
    return pl.BlockSpec(memory_space=pltpu.VMEM)


def shard_pass(group, groups, me, log_gate, write_rate, starts, key_rows, value_rows, per_key):
    tokens_here = key_rows.shape[0]
    keys = key_rows.shape[1] // DK // groups
    heads = keys * per_key
    heads_here = heads * groups
    blocks = tokens_here // BLK
    count = heads * blocks
    wide = DK + DV
    whole = lambda *shape: pl.BlockSpec(shape, lambda i: (0,) * len(shape))
    return pl.pallas_call(
        functools.partial(shard_kernel, group * keys, per_key, blocks, keys),
        grid=(1,),
        in_specs=[
            pl.BlockSpec(memory_space=pltpu.SMEM),
            whole(heads_here, tokens_here),
            whole(heads_here, tokens_here),
            whole(blocks, BLK),
            pl.BlockSpec((tokens_here, keys * DK), lambda i: (0, group)),
            pl.BlockSpec((tokens_here, heads * DV), lambda i: (0, group)),
        ],
        out_specs=[in_vmem()] * 5,
        out_shape=[
            vmem((count, BLK, wide), BF16),
            vmem((count, DK, wide), BF16),
            vmem((2 * count + blocks, BLK), F32),
            vmem((heads // 2, DK, wide), BF16),
            vmem((heads // 2, DK, wide), BF16),
        ],
        scratch_shapes=[
            pltpu.VMEM((count, BLK), F32),
            pltpu.VMEM((count, BLK), F32),
            pltpu.VMEM((keys * blocks, BLK), F32),
            pltpu.VMEM((keys * blocks, DK, BLK), BF16),
            pltpu.VMEM((count, DK, wide), BF16),
            pltpu.VMEM((count, BLK), F32),
            pltpu.VMEM((heads, DK, wide), F32),
        ],
        compiler_params=pltpu.CompilerParams(vmem_limit_bytes=24 * MIB),
        cost_estimate=pl.CostEstimate(
            flops=count * 18 * 2 * BLK**3, bytes_accessed=4 * MIB, transcendentals=0
        ),
        name="shard_pass",
    )(me, *(in_hbm(a) for a in (log_gate, write_rate, starts, key_rows, value_rows)))


def local_kernel(
    per_key, blocks, at_key, rows_ref, q_ref, k_ref, gate_ref, gain_ref, wu_ref, zc_ref,
    out_ref, carry_ref, gated_ref,
):
    count = per_key * blocks
    total = (rows_ref.shape[0] - blocks) // 2
    base = at_key * count
    cum = rows_ref[base : base + count, :]
    right = rows_ref[total + base : total + base + count, :]
    reset = rows_ref[2 * total :, :]
    cols = columns_of(jnp.concatenate([cum, reset], axis=0))
    units, inner, masks = [], [], []
    for c in range(blocks):
        span = slice(c * BLK, (c + 1) * BLK)
        query = q_ref[span, :].astype(F32)
        units.append(jnp.sum(query * query, axis=1, keepdims=True) + EPS)
        inner.append(dot_t(q_ref[span, :], k_ref[span, :]))
        masks.append(doc_mask(cols[:, count + c : count + c + 1], reset[c : c + 1, :], False))
    scores = []
    for at in range(count):
        c = at % blocks
        left = cols[:, at : at + 1] - 0.5 * jnp.log(units[c])
        gap = left - right[at : at + 1, :] + masks[c]
        scores.append((inner[c] * jnp.exp(gap)).astype(BF16))
    seen = [dot(scores[at], wu_ref[base + at]) for at in range(count)]
    for at in range(count):
        c, h = at % blocks, at // blocks
        span = slice(c * BLK, (c + 1) * BLK)
        wide = slice(h * DV, (h + 1) * DV)
        reset_col = cols[:, count + c : count + c + 1]
        keep = jnp.where(reset_col == 0.0, jnp.exp(cols[:, at : at + 1]), 0.0) * lax.rsqrt(units[c])
        g = (keep * q_ref[span, :].astype(F32) - seen[at][:, :DK]).astype(BF16)
        both = dot(g, zc_ref[base + at])
        out_ref[span, wide] = both[:, :DV] + seen[at][:, DK:]
        carry_ref[span, wide] = both[:, DV:].astype(BF16)
        gate = gate_ref[span, wide].astype(F32)
        gated_ref[span, wide] = gain_ref[...] * (gate / (1.0 + jnp.exp(-gate)))


def local_pass(key, at_key, rows, queries, key_rows, out_gate, gain, wu, zc, per_key):
    tokens_here = queries.shape[0]
    blocks = tokens_here // BLK
    count = per_key * blocks
    wide = per_key * DV
    return pl.pallas_call(
        functools.partial(local_kernel, per_key, blocks, at_key),
        grid=(1,),
        in_specs=[
            in_vmem(),
            pl.BlockSpec((tokens_here, DK), lambda i: (0, key)),
            pl.BlockSpec((tokens_here, DK), lambda i: (0, key)),
            pl.BlockSpec((tokens_here, wide), lambda i: (0, key)),
            pl.BlockSpec((1, DV), lambda i: (0, 0)),
            in_vmem(),
            in_vmem(),
        ],
        out_specs=[in_vmem()] * 3,
        out_shape=[
            vmem((tokens_here, wide), F32),
            vmem((tokens_here, wide), BF16),
            vmem((tokens_here, wide), F32),
        ],
        compiler_params=pltpu.CompilerParams(vmem_limit_bytes=16 * MIB),
        cost_estimate=pl.CostEstimate(
            flops=count * 8 * 2 * BLK**3, bytes_accessed=4 * MIB, transcendentals=0
        ),
        name="local_pass",
    )(rows, queries, key_rows, out_gate, gain, wu, zc)


def finish_kernel(row, per_key, keys_here, group_heads, order, me_ref, *refs):
    outs = refs[:keys_here]
    carries = refs[keys_here : 2 * keys_here]
    gates = refs[2 * keys_here : 3 * keys_here]
    refs = refs[3 * keys_here :]
    groups = keys_here * per_key // group_heads
    starts = refs[: 2 * groups]
    weight_ref, send_ref, keep_ref = refs[2 * groups :]
    rows = slice(row, row + send_ref.shape[0])
    half = group_heads // 2
    odd = lax.rem(me_ref[0], 2) == 1
    parts = []
    for head in range(keys_here * per_key):
        key, h = head // per_key, head % per_key
        span = slice(h * DV, (h + 1) * DV)
        own_ref, back_ref = starts[2 * (head // group_heads) : 2 * (head // group_heads) + 2]
        own, back = own_ref[head % half], back_ref[head % half]
        start = jnp.where(odd, own, back) if head % group_heads >= half else jnp.where(odd, back, own)
        seen = outs[key][rows, span] + dot(carries[key][rows, span], start)
        spread = jnp.mean(seen * seen, axis=1, keepdims=True)
        parts.append((seen * lax.rsqrt(spread + EPS) * gates[key][rows, span]).astype(BF16))
    normed = jnp.concatenate(parts, axis=1)
    columns = weight_ref.shape[1] // len(order)
    sends = len(order) // 2
    for at, place in enumerate(order):
        first = pl.multiple_of((me_ref[1] ^ place) * columns, columns)
        part = dot(normed, weight_ref[:, pl.ds(first, columns)]).astype(BF16)
        to, slot = (send_ref, at - sends) if at >= sends else (keep_ref, at)
        to[:, slot * columns : (slot + 1) * columns] = part


def halving_order(size):
    def split(group, bit):
        if len(group) == 1:
            return group
        kept = [p for p in group if not p & bit]
        return split(kept, 2 * bit) + split([p for p in group if p & bit], 2 * bit)

    return split(list(range(size)), 1)


def finish_pass(row, rows, me, outs, carries, gates, starts, weight, per_key, group_heads, devices):
    keys_here = len(outs)
    half = weight.shape[1] // 2
    return pl.pallas_call(
        functools.partial(
            finish_kernel, row, per_key, keys_here, group_heads, halving_order(devices)
        ),
        grid=(1,),
        in_specs=[pl.BlockSpec(memory_space=pltpu.SMEM)]
        + [in_vmem()] * (3 * keys_here + len(starts) + 1),
        out_specs=[in_vmem()] * 2,
        out_shape=[vmem((rows, half), BF16)] * 2,
        compiler_params=pltpu.CompilerParams(vmem_limit_bytes=16 * MIB),
        cost_estimate=pl.CostEstimate(
            flops=2 * rows * weight.shape[0] * weight.shape[1],
            bytes_accessed=8 * MIB,
            transcendentals=0,
        ),
        name="finish_pass",
    )(me, *outs, *carries, *gates, *starts, weight)


def composed(later, earlier, h):
    return dot(later[h, :, DV:], earlier[h]) + later[h, :, :DV].astype(F32)


def pair_kernel(me_ref, mine_ref, got_ref, both_ref):
    odd = lax.rem(me_ref[0], 2) == 1

    def join(second, first):
        for h in range(both_ref.shape[0]):
            moved = dot(second[h, :, DV:], first[h])
            both_ref[h, :, :DV] = (moved[:, :DV] + second[h, :, :DV].astype(F32)).astype(BF16)
            both_ref[h, :, DV:] = moved[:, DV:].astype(BF16)

    @pl.when(odd)
    def _():
        join(mine_ref, got_ref)

    @pl.when(jnp.logical_not(odd))
    def _():
        join(got_ref, mine_ref)


def step_kernel(later_ref, earlier_ref, out_ref):
    for h in range(out_ref.shape[0]):
        out_ref[h] = composed(later_ref, earlier_ref, h).astype(BF16)


def last_kernel(me_ref, mine_ref, got_ref, before_ref, near_ref, far_ref, own_ref, other_ref):
    odd = lax.rem(me_ref[0], 2) == 1
    third = lax.div(me_ref[0], 2) == 2

    def fill(first, here_ref, then_ref):
        for h in range(own_ref.shape[0]):
            here = composed(before_ref, far_ref, h).astype(BF16)
            here_ref[h] = jnp.where(third, near_ref[h], here)
        for h in range(own_ref.shape[0]):
            then_ref[h] = composed(first, here_ref, h).astype(BF16)

    @pl.when(odd)
    def _():
        fill(got_ref, other_ref, own_ref)

    @pl.when(jnp.logical_not(odd))
    def _():
        fill(mine_ref, own_ref, other_ref)


SMALL = pltpu.CompilerParams(vmem_limit_bytes=8 * MIB)
ONE = pl.BlockSpec(memory_space=pltpu.SMEM)


def plain(array):
    return pl.BlockSpec(array.shape, lambda i: (0,) * array.ndim)


def small_call(kernel, name, outs, me, *arrays):
    heads = arrays[0].shape[0]
    state = jax.ShapeDtypeStruct((heads, DK, DV), BF16)
    scalars = [] if me is None else [me]
    return pl.pallas_call(
        kernel,
        grid=(1,),
        in_specs=[ONE] * len(scalars) + [plain(a) for a in arrays],
        out_specs=[plain(a) for a in outs],
        out_shape=outs,
        compiler_params=SMALL,
        cost_estimate=pl.CostEstimate(
            flops=heads * 4 * DK**3, bytes_accessed=MIB, transcendentals=0
        ),
        name=name,
    )(*scalars, *arrays)


def step_call(later, earlier):
    heads = later.shape[0]
    return pl.pallas_call(
        step_kernel,
        grid=(1,),
        in_specs=[
            pl.BlockSpec((heads, DK, DK + DV), lambda i: (0, 0, 0)),
            pl.BlockSpec((heads, DK, DV), lambda i: (0, 0, 0)),
        ],
        out_specs=pl.BlockSpec((heads, DK, DV), lambda i: (0, 0, 0)),
        out_shape=jax.ShapeDtypeStruct((heads, DK, DV), BF16),
        compiler_params=SMALL,
        cost_estimate=pl.CostEstimate(
            flops=heads * 2 * DK**3, bytes_accessed=MIB, transcendentals=0
        ),
        name="step",
    )(later, earlier)


def route(axis, target):
    size = lax.axis_size(axis)
    return [(i, target(i)) for i in range(size) if target(i) is not None]


def start_states(me, mine, theirs, work):
    size = lax.axis_size("seq")
    half = mine.shape[0]
    state = jax.ShapeDtypeStruct((half, DK, DV), BF16)
    swap = route("seq", lambda i: i ^ 1)
    if size == 8:
        got = work(lax.ppermute(theirs, "seq", swap))
        both, = small_call(
            pair_kernel, "pair", [jax.ShapeDtypeStruct(mine.shape, BF16)], me, mine, got
        )
        before = work(
            lax.ppermute(both, "seq", route("seq", lambda i: i + 2 if i < 6 else None))
        )
        third = step_call(both, before)
        near = lax.ppermute(third, "seq", [(2, 4), (3, 5)])
        far = work(lax.ppermute(third, "seq", [(2, 6), (3, 7)]))
        own, other = small_call(
            last_kernel, "last", [state] * 2, me, mine, got, before, near, far
        )
        return own, work(lax.ppermute(other, "seq", swap))

    onward = route("seq", lambda i: i + 1 if i + 1 < size else None)
    parts = jnp.zeros((half, DK, DV), BF16), jnp.zeros((half, DK, DV), BF16)
    odd = me[0] % 2 == 1

    def hop(step, states):
        ends = [step_call(end, held) for end, held in zip((mine, theirs), states)]
        low, high = jnp.where(odd, ends[1], ends[0]), jnp.where(odd, ends[0], ends[1])
        low, high = lax.ppermute((low, high), "seq", onward)
        return jnp.where(odd, high, low), jnp.where(odd, low, high)

    return lax.fori_loop(0, size - 1, hop, parts)


def local(
    queries, key_rows, value_rows, out_gate, write_rate, log_gate, doc_start, norm_gain, out_weight
):
    tokens_here = queries.shape[0]
    heads_here = value_rows.shape[1] // DV
    keys_here = key_rows.shape[1] // DK
    per_key = heads_here // keys_here
    devices = lax.axis_size("head")
    starts = doc_start.reshape(tokens_here // BLK, BLK)
    me = jnp.stack([lax.axis_index("seq"), lax.axis_index("head")]).astype(jnp.int32)
    gain = norm_gain.reshape(1, DV)
    groups = 1
    keys = keys_here // groups
    outs, carries, gates, states = [], [], [], []
    for group in range(groups):
        wu, zc, rows, mine, theirs = shard_pass(
            group, groups, me, log_gate, write_rate, starts, key_rows, value_rows, per_key
        )

        def work(coming):
            key = len(outs)
            if key == (group + 1) * keys:
                return coming
            out, carry, gate = local_pass(
                key, key - group * keys, rows, queries, key_rows, out_gate, gain, wu, zc, per_key
            )
            coming, out, carry, gate = lax.optimization_barrier((coming, out, carry, gate))
            outs.append(out)
            carries.append(carry)
            gates.append(gate)
            return coming

        own, back = start_states(me, mine, theirs, work)
        while len(outs) < (group + 1) * keys:
            back = work(back)
        states += [own, back]

    weight = pltpu.with_memory_space_constraint(out_weight, pltpu.VMEM)

    def project(row, rows, ready):
        if ready is not None:
            states[-1], ready = lax.optimization_barrier((states[-1], ready))
        pair = finish_pass(
            row, rows, me, outs, carries, gates, states, weight, per_key, keys * per_key, devices
        )
        return ready, pair

    sizes = [tokens_here // 8, tokens_here // 4, tokens_here // 4, tokens_here // 4, tokens_here // 8]
    places = [sum(sizes[:index]) for index in range(len(sizes))]
    mixed = jnp.zeros((tokens_here, out_weight.shape[1] // devices), BF16)
    send, keep = project(places[0], sizes[0], None)[1]
    for index, place in enumerate(places):
        following = None
        bit = 1
        while bit < devices:
            got = lax.ppermute(send, "head", route("head", lambda i: i ^ bit))
            if bit == 1 and index + 1 < len(sizes):
                following = project(places[index + 1], sizes[index + 1], send)[1]
                got, *following = lax.optimization_barrier((got, *following))
            total = keep.astype(F32) + got.astype(F32)
            bit *= 2
            if bit < devices:
                width = total.shape[1] // 2
                keep = total[:, :width]
                send = total[:, width:].astype(BF16)
                if bit == 2 and following is not None:
                    states[-1], send = lax.optimization_barrier((states[-1], send))
            else:
                keep = total
        mixed = lax.dynamic_update_slice(mixed, keep.astype(BF16), (place, 0))
        if following is not None:
            send, keep = following
    return mixed


def solution(mesh):
    placed = (
        P("seq", "head"),
        P("seq", "head"),
        P("seq", "head"),
        P("seq", "head"),
        P("head", "seq"),
        P("head", "seq"),
        P("seq"),
        P(),
        P("head", None),
    )
    return jax.shard_map(
        local, mesh=mesh, in_specs=placed, out_specs=P("seq", "head"), check_vma=False
    )
```

time: 111 us -> 81.1 us (0.73)
  local copies, waits for them, and re-layouts: 22.3 us -> 0.24 us
  Pallas kernels: 43.3 us -> 31.4 us
  waiting for transfers between devices: 23.5 us -> 28.3 us
    unnamed x50 -> x12, local copies, waits for them, and re-layouts: 22.1 us -> 0.03 us
    pallas_call x9 -> x10, Pallas kernels: 42.4 us -> 29.6 us  [the longest x1 12.9 us: shard_pass(): pl.pallas_call(functools.partial(shard_kernel, group * keys, per_key, blo...]
    ppermute x1, waiting for transfers between devices: 0.01 us -> 4.72 us  [start_states(): got = work(lax.ppermute(theirs, 'seq', swap))]
    concatenate x2 -> x0, other arithmetic: 1.11 us -> none  [the longest x1 1.04 us: local(): return jnp.concatenate(pieces, axis=0)]
    ppermute x8 -> x10, waiting for transfers between devices: 18.6 us -> 17.5 us  [local(): got = lax.ppermute(send, 'head', route('head', lambda i: i ^ bit))]
    ppermute x8 -> x10, starting transfers between devices: 6.09 us -> 5.7 us  [local(): got = lax.ppermute(send, 'head', route('head', lambda i: i ^ bit))]
  transfers between devices with their start and end apart: 13 -> 15, of which waited for: 7 -> 9; matrix products, arithmetic and copies ran while one was open for 1% -> 1% of each run, Pallas kernels for 16% -> 19%
where the time goes in v3:
time: 81.1 us; the launch traced here: 80 us
  Pallas kernels  31.4 us (39%)
  waiting for transfers between devices  28.3 us (35%)
  starting transfers between devices  18.1 us (22%)
  other arithmetic  1.64 us (2%)
    ppermute x10, waiting for transfers between devices, local(): got = lax.ppermute(send, 'head', route('head', lambda i: i ^ bit))  17.5 us
    pallas_call x1, Pallas kernels, shard_pass(): pl.pallas_call(functools.partial(shard_kernel, group * keys, per_key, blo...  12.9 us
    pallas_call x5, Pallas kernels, finish_pass(): pl.pallas_call(functools.partial(finish_kernel, row, per_key, keys_here,...  9.38 us
    pallas_call x4, Pallas kernels, local_pass(): pl.pallas_call(functools.partial(local_kernel, per_key, blocks, at_key),...  7.31 us
    ppermute x10, starting transfers between devices, local(): got = lax.ppermute(send, 'head', route('head', lambda i: i ^ bit))  5.7 us
    ppermute x1, waiting for transfers between devices, start_states(): got = work(lax.ppermute(theirs, 'seq', swap))  4.72 us
    ppermute x1, starting transfers between devices, start_states(): far = work(lax.ppermute(third, 'seq', [(2, 6), (3, 7)]))  4.48 us
    ppermute x1, waiting for transfers between devices, start_states(): lax.ppermute(both, 'seq', route('seq', lambda i: i + 2 if i < 6 else None))  3.75 us
  transfers between devices with their start and end apart: 15, of which 9 were waited for; matrix products, arithmetic and copies ran while one was open for 1% of the time, Pallas kernels for 19%

profile of v3, /device:TPU:8, one launch (start us, length us, event | category | flops | bytes accessed | tf_op | source)
XLA Modules:
  0.0 80.0 jit_solution(9630366618677040737)
XLA Ops:
  0.0 0.1 pad_add_fusion.me_ref
  0.1 0.0 copy-start.1
  0.1 0.0 copy-start.2
  0.1 12.9 %shard_pass.1 = (bf16[64,128,256]{2,1,0:T(8,128)(2,1)S(1)}, bf16[64,128,256]{2,1,0:T(8,128)(2,1)S(1)}, f32[136,128]{1,0:T(8,128)S(1)}, bf16[4,128,256]{2,1,0:T(8,128)(2,1)S(1)}, bf16[4,128,256]{2,1,0:T(8,128)(2,1)S(1)}) custom-call(s32[2]{0:T(128)S(1)} %pad_add_fusion.me_ref, f32[8,1024]{1,0:T(8,128)} %log_ref.1, f32[8,1024]{1,0:T(8,128)} %rate_ref.1, ...), custom_call_target="tpu_custom_call" | custom-call | flops 4831838208 | bytes 4194304 | tf_op jit(solution)/shard_map/shard_pass/pallas_call | solution.py:232
  13.0 1.6 %collective-permute-start = (bf16[4,128,256]{2,1,0:T(8,128)(2,1)S(1)}, bf16[4,128,256]{2,1,0:T(8,128)(2,1)S(1)}, u32[]{:S(2)}, u32[]{:S(2)}) collective-permute-start(bf16[4,128,256]{2,1,0:T(8,128)(2,1)S(1)} %get-tuple-element.73), channel_id=1, source_target_pairs={{0,4},{4,0},{8,12},{12,8},{16,20},{20,16},{24,28},{28,24},{1,5},{5... | collective-permute-start | bytes 786440 | tf_op jit(solution)/shard_map/ppermute | solution.py:504
  14.5 0.0 copy-done.1
  14.5 0.0 copy-done.2
  14.5 0.0 copy-done.3
  14.5 0.0 copy-done.4
  14.5 1.8 %local_pass.4 = (f32[1024,256]{1,0:T(8,128)S(1)}, bf16[1024,256]{1,0:T(8,128)(2,1)S(1)}, f32[1024,256]{1,0:T(8,128)S(1)}) custom-call(f32[136,128]{1,0:T(8,128)S(1)} %get-tuple-element.74.rows_ref, bf16[1024,512]{1,0:T(8,128)(2,1)S(1)} %copy-done.3, bf16[1024,512]{1,0:T(8,128)(2,1)S(1)} %copy-done.2, bf16[1024,1024]{1,0:T(8,128)(2,1)S(1)} %copy-done.1, ...), custom_call_target="tpu_custom_call" | custom-call | flops 536870912 | bytes 4194304 | tf_op jit(solution)/shard_map/local_pass/pallas_call | solution.py:312
  16.4 4.7 %collective-permute-done.got_ref = bf16[4,128,256]{2,1,0:T(8,128)(2,1)S(1)} collective-permute-done((bf16[4,128,256]{2,1,0:T(8,128)(2,1)S(1)}, bf16[4,128,256]{2,1,0:T(8,128)(2,1)S(1)}, u32[]{:S(2)}, u32[]{:S(2)}) %collective-permute-start) | collective-permute-done | bytes 262176 | tf_op jit(solution)/shard_map/ppermute | solution.py:504
  21.1 0.8 pair.1.later_ref
  21.9 3.5 %collective-permute-start.1 = (bf16[4,128,256]{2,1,0:T(8,128)(2,1)S(1)}, bf16[4,128,256]{2,1,0:T(8,128)(2,1)S(1)}, u32[]{:S(2)}, u32[]{:S(2)}) collective-permute-start(bf16[4,128,256]{2,1,0:T(8,128)(2,1)S(1)} %pair.1.later_ref), channel_id=1, source_target_pairs={{0,8},{4,12},{8,16},{12,20},{16,24},{20,28},{1,9},{5,13},{9,17},{1... | collective-permute-start | bytes 786440 | tf_op jit(solution)/shard_map/ppermute | solution.py:509
  25.3 1.8 %local_pass.5 = (f32[1024,256]{1,0:T(8,128)S(1)}, bf16[1024,256]{1,0:T(8,128)(2,1)S(1)}, f32[1024,256]{1,0:T(8,128)S(1)}) custom-call(f32[136,128]{1,0:T(8,128)S(1)} %get-tuple-element.74.rows_ref, bf16[1024,512]{1,0:T(8,128)(2,1)S(1)} %copy-done.3, bf16[1024,512]{1,0:T(8,128)(2,1)S(1)} %copy-done.2, bf16[1024,1024]{1,0:T(8,128)(2,1)S(1)} %copy-done.1, ...), custom_call_target="tpu_custom_call" | custom-call | flops 536870912 | bytes 4194304 | tf_op jit(solution)/shard_map/local_pass/pallas_call | solution.py:312
  27.2 3.7 %collective-permute-done.1.earlier_ref.before_ref = bf16[4,128,256]{2,1,0:T(8,128)(2,1)S(1)} collective-permute-done((bf16[4,128,256]{2,1,0:T(8,128)(2,1)S(1)}, bf16[4,128,256]{2,1,0:T(8,128)(2,1)S(1)}, u32[]{:S(2)}, u32[]{:S(2)}) %collective-permute-start.1) | collective-permute-done | bytes 262176 | tf_op jit(solution)/shard_map/ppermute | solution.py:509
  30.9 0.2 step.1
  31.1 4.5 %collective-permute-start.2 = (bf16[4,128,128]{2,1,0:T(8,128)(2,1)S(1)}, bf16[4,128,128]{2,1,0:T(8,128)(2,1)S(1)}, u32[]{:S(2)}, u32[]{:S(2)}) collective-permute-start(bf16[4,128,128]{2,1,0:T(8,128)(2,1)S(1)} %step.1), channel_id=1, source_target_pairs={{8,24},{12,28},{9,25},{13,29},{10,26},{14,30},{11,27},{15,31}} | collective-permute-start | bytes 393224 | tf_op jit(solution)/shard_map/ppermute | solution.py:513
  35.6 1.3 %collective-permute-start.3 = (bf16[4,128,128]{2,1,0:T(8,128)(2,1)S(1)}, bf16[4,128,128]{2,1,0:T(8,128)(2,1)S(1)}, u32[]{:S(2)}, u32[]{:S(2)}) collective-permute-start(bf16[4,128,128]{2,1,0:T(8,128)(2,1)S(1)} %step.1), channel_id=1, source_target_pairs={{8,16},{12,20},{9,17},{13,21},{10,18},{14,22},{11,19},{15,23}} | collective-permute-start | bytes 393224 | tf_op jit(solution)/shard_map/ppermute | solution.py:512
  36.9 1.8 %local_pass.6 = (f32[1024,256]{1,0:T(8,128)S(1)}, bf16[1024,256]{1,0:T(8,128)(2,1)S(1)}, f32[1024,256]{1,0:T(8,128)S(1)}) custom-call(f32[136,128]{1,0:T(8,128)S(1)} %get-tuple-element.74.rows_ref, bf16[1024,512]{1,0:T(8,128)(2,1)S(1)} %copy-done.3, bf16[1024,512]{1,0:T(8,128)(2,1)S(1)} %copy-done.2, bf16[1024,1024]{1,0:T(8,128)(2,1)S(1)} %copy-done.1, ...), custom_call_target="tpu_custom_call" | custom-call | flops 536870912 | bytes 4194304 | tf_op jit(solution)/shard_map/local_pass/pallas_call | solution.py:312
  38.8 0.0 collective-permute-done.2.far_ref
  38.8 0.7 collective-permute-done.3.near_ref
  39.5 0.9 %last.1 = (bf16[4,128,128]{2,1,0:T(8,128)(2,1)S(1)}, bf16[4,128,128]{2,1,0:T(8,128)(2,1)S(1)}) custom-call(s32[2]{0:T(128)S(1)} %pad_add_fusion.me_ref, bf16[4,128,256]{2,1,0:T(8,128)(2,1)S(1)} %get-tuple-element.81.mine_ref, bf16[4,128,256]{2,1,0:T(8,128)(2,1)S(1)} %collective-permute-done.got_ref, ...), custom_call_target="tpu_custom_call" | custom-call | flops 33554432 | bytes 1048576 | tf_op jit(solution)/shard_map/last/pallas_call | solution.py:460
  40.4 0.0 copy-start
  40.4 1.6 %collective-permute-start.4 = (bf16[4,128,128]{2,1,0:T(8,128)(2,1)S(1)}, bf16[4,128,128]{2,1,0:T(8,128)(2,1)S(1)}, u32[]{:S(2)}, u32[]{:S(2)}) collective-permute-start(bf16[4,128,128]{2,1,0:T(8,128)(2,1)S(1)} %get-tuple-element.93), channel_id=1, source_target_pairs={{0,4},{4,0},{8,12},{12,8},{16,20},{20,16},{24,28},{28,24},{1,5},{5... | collective-permute-start | bytes 393224 | tf_op jit(solution)/shard_map/ppermute | solution.py:517
  42.0 1.8 %local_pass.7 = (f32[1024,256]{1,0:T(8,128)S(1)}, bf16[1024,256]{1,0:T(8,128)(2,1)S(1)}, f32[1024,256]{1,0:T(8,128)S(1)}) custom-call(f32[136,128]{1,0:T(8,128)S(1)} %get-tuple-element.74.rows_ref, bf16[1024,512]{1,0:T(8,128)(2,1)S(1)} %copy-done.3, bf16[1024,512]{1,0:T(8,128)(2,1)S(1)} %copy-done.2, bf16[1024,1024]{1,0:T(8,128)(2,1)S(1)} %copy-done.1, ...), custom_call_target="tpu_custom_call" | custom-call | flops 536870912 | bytes 4194304 | tf_op jit(solution)/shard_map/local_pass/pallas_call | solution.py:312
  43.8 1.6 %collective-permute-done.4.refs_13_ = bf16[4,128,128]{2,1,0:T(8,128)(2,1)S(1)} collective-permute-done((bf16[4,128,128]{2,1,0:T(8,128)(2,1)S(1)}, bf16[4,128,128]{2,1,0:T(8,128)(2,1)S(1)}, u32[]{:S(2)}, u32[]{:S(2)}) %collective-permute-start.4) | collective-permute-done | bytes 131104 | tf_op jit(solution)/shard_map/ppermute | solution.py:517
  45.4 0.0 copy-done
  45.4 1.5 %finish_pass.5 = (bf16[128,1024]{1,0:T(8,128)(2,1)S(1)}, bf16[128,1024]{1,0:T(8,128)(2,1)S(1)}) custom-call(s32[2]{0:T(128)S(1)} %pad_add_fusion.me_ref, f32[1024,256]{1,0:T(8,128)S(1)} %get-tuple-element.80.refs_0_, f32[1024,256]{1,0:T(8,128)S(1)} %get-tuple-element.86.refs_1_, f32[1024,256]{1,0:T(8,128)S(1)} %get-tuple-element.91.refs_2_, ...), custom_call_target="tpu_custom_call" | custom-call | flops 536870912 | bytes 8388608 | tf_op jit(solution)/shard_map/finish_pass/pallas_call | solution.py:382
  46.9 0.1 collective-permute-start.5
  47.0 2.1 %finish_pass.6 = (bf16[256,1024]{1,0:T(8,128)(2,1)S(1)}, bf16[256,1024]{1,0:T(8,128)(2,1)S(1)}) custom-call(s32[2]{0:T(128)S(1)} %pad_add_fusion.me_ref, f32[1024,256]{1,0:T(8,128)S(1)} %get-tuple-element.80.refs_0_, f32[1024,256]{1,0:T(8,128)S(1)} %get-tuple-element.86.refs_1_, f32[1024,256]{1,0:T(8,128)S(1)} %get-tuple-element.91.refs_2_, ...), custom_call_target="tpu_custom_call" | custom-call | flops 1073741824 | bytes 8388608 | tf_op jit(solution)/shard_map/finish_pass/pallas_call | solution.py:382
  49.2 0.0 collective-permute-done.5
  49.2 0.6 collective-permute-start.7
  49.7 0.1 convert_add_fusion.4
  49.8 1.6 %collective-permute-start.6 = (bf16[128,512]{1,0:T(8,128)(2,1)S(1)}, bf16[128,512]{1,0:T(8,128)(2,1)S(1)}, u32[]{:S(2)}, u32[]{:S(2)}) collective-permute-start(bf16[128,512]{1,0:T(8,128)(2,1)S(1)} %slice.87), channel_id=1, source_target_pairs={{0,2},{1,3},{2,0},{3,1},{4,6},{5,7},{6,4},{7,5},{8,10},{9,11},{10,... | collective-permute-start | bytes 393224 | tf_op jit(solution)/shard_map/ppermute | solution.py:587
  51.4 2.1 %finish_pass.7 = (bf16[256,1024]{1,0:T(8,128)(2,1)S(1)}, bf16[256,1024]{1,0:T(8,128)(2,1)S(1)}) custom-call(s32[2]{0:T(128)S(1)} %pad_add_fusion.me_ref, f32[1024,256]{1,0:T(8,128)S(1)} %get-tuple-element.80.refs_0_, f32[1024,256]{1,0:T(8,128)S(1)} %get-tuple-element.86.refs_1_, f32[1024,256]{1,0:T(8,128)S(1)} %get-tuple-element.91.refs_2_, ...), custom_call_target="tpu_custom_call" | custom-call | flops 1073741824 | bytes 8388608 | tf_op jit(solution)/shard_map/finish_pass/pallas_call | solution.py:382
  53.5 0.0 collective-permute-done.7
  53.5 0.1 collective-permute-start.9
  53.6 0.2 convert_add_fusion.2
  53.8 0.6 collective-permute-start.8
  54.4 0.9 %collective-permute-done.6 = bf16[128,512]{1,0:T(8,128)(2,1)S(1)} collective-permute-done((bf16[128,512]{1,0:T(8,128)(2,1)S(1)}, bf16[128,512]{1,0:T(8,128)(2,1)S(1)}, u32[]{:S(2)}, u32[]{:S(2)}) %collective-permute-start.6) | collective-permute-done | bytes 131104 | tf_op jit(solution)/shard_map/ppermute | solution.py:587
  55.3 0.1 dynamic_update_slice.15
  55.4 2.1 %finish_pass.8 = (bf16[256,1024]{1,0:T(8,128)(2,1)S(1)}, bf16[256,1024]{1,0:T(8,128)(2,1)S(1)}) custom-call(s32[2]{0:T(128)S(1)} %pad_add_fusion.me_ref, f32[1024,256]{1,0:T(8,128)S(1)} %get-tuple-element.80.refs_0_, f32[1024,256]{1,0:T(8,128)S(1)} %get-tuple-element.86.refs_1_, f32[1024,256]{1,0:T(8,128)S(1)} %get-tuple-element.91.refs_2_, ...), custom_call_target="tpu_custom_call" | custom-call | flops 1073741824 | bytes 8388608 | tf_op jit(solution)/shard_map/finish_pass/pallas_call | solution.py:382
  57.5 0.0 collective-permute-done.9
  57.6 0.1 collective-permute-start.11
  57.6 5.0 %collective-permute-done.8 = bf16[256,512]{1,0:T(8,128)(2,1)S(1)} collective-permute-done((bf16[256,512]{1,0:T(8,128)(2,1)S(1)}, bf16[256,512]{1,0:T(8,128)(2,1)S(1)}, u32[]{:S(2)}, u32[]{:S(2)}) %collective-permute-start.8) | collective-permute-done | bytes 262176 | tf_op jit(solution)/shard_map/ppermute | solution.py:587
  62.6 0.1 fusion.3
  62.7 0.2 convert_add_fusion.1
  62.9 0.6 collective-permute-start.10
  63.5 1.5 %finish_pass.9 = (bf16[128,1024]{1,0:T(8,128)(2,1)S(1)}, bf16[128,1024]{1,0:T(8,128)(2,1)S(1)}) custom-call(s32[2]{0:T(128)S(1)} %pad_add_fusion.me_ref, f32[1024,256]{1,0:T(8,128)S(1)} %get-tuple-element.80.refs_0_, f32[1024,256]{1,0:T(8,128)S(1)} %get-tuple-element.86.refs_1_, f32[1024,256]{1,0:T(8,128)S(1)} %get-tuple-element.91.refs_2_, ...), custom_call_target="tpu_custom_call" | custom-call | flops 536870912 | bytes 8388608 | tf_op jit(solution)/shard_map/finish_pass/pallas_call | solution.py:382
  65.0 0.0 collective-permute-done.11
  65.0 0.1 collective-permute-start.13
  65.1 0.2 convert_add_fusion
  65.3 1.6 %collective-permute-start.12 = (bf16[256,512]{1,0:T(8,128)(2,1)S(1)}, bf16[256,512]{1,0:T(8,128)(2,1)S(1)}, u32[]{:S(2)}, u32[]{:S(2)}) collective-permute-start(bf16[256,512]{1,0:T(8,128)(2,1)S(1)} %slice.83), channel_id=1, source_target_pairs={{0,2},{1,3},{2,0},{3,1},{4,6},{5,7},{6,4},{7,5},{8,10},{9,11},{10,... | collective-permute-start | bytes 786440 | tf_op jit(solution)/shard_map/ppermute | solution.py:587
  66.9 5.3 %collective-permute-done.10 = bf16[256,512]{1,0:T(8,128)(2,1)S(1)} collective-permute-done((bf16[256,512]{1,0:T(8,128)(2,1)S(1)}, bf16[256,512]{1,0:T(8,128)(2,1)S(1)}, u32[]{:S(2)}, u32[]{:S(2)}) %collective-permute-start.10) | collective-permute-done | bytes 262176 | tf_op jit(solution)/shard_map/ppermute | solution.py:587
  72.2 0.1 fusion.4
  72.3 0.0 collective-permute-done.13
  72.3 0.1 convert_add_fusion.3
  72.4 0.6 collective-permute-start.14
  72.9 4.9 %collective-permute-done.12 = bf16[256,512]{1,0:T(8,128)(2,1)S(1)} collective-permute-done((bf16[256,512]{1,0:T(8,128)(2,1)S(1)}, bf16[256,512]{1,0:T(8,128)(2,1)S(1)}, u32[]{:S(2)}, u32[]{:S(2)}) %collective-permute-start.12) | collective-permute-done | bytes 262176 | tf_op jit(solution)/shard_map/ppermute | solution.py:587
  77.8 0.1 fusion.5
  77.9 0.0 copy-start.5
  77.9 1.4 %collective-permute-done.14 = bf16[128,512]{1,0:T(8,128)(2,1)S(1)} collective-permute-done((bf16[128,512]{1,0:T(8,128)(2,1)S(1)}, bf16[128,512]{1,0:T(8,128)(2,1)S(1)}, u32[]{:S(2)}, u32[]{:S(2)}) %collective-permute-start.14) | collective-permute-done | bytes 131104 | tf_op jit(solution)/shard_map/ppermute | solution.py:587
  79.3 0.0 copy-done.5
  79.3 0.7 fusion.8
  (8 shorter events, 0.2 us)
Async XLA Ops:
  0.1 14.4 %copy-start.1 = (bf16[1024,1024]{1,0:T(8,128)(2,1)S(1)}, bf16[1024,1024]{1,0:T(8,128)(2,1)}, u32[]{:S(2)}) copy-start(bf16[1024,1024]{1,0:T(8,128)(2,1)} %gate_ref.7) | copy-start | bytes 6291460
  0.1 14.4 %copy-start.2 = (bf16[1024,512]{1,0:T(8,128)(2,1)S(1)}, bf16[1024,512]{1,0:T(8,128)(2,1)}, u32[]{:S(2)}) copy-start(bf16[1024,512]{1,0:T(8,128)(2,1)} %k_ref.9) | copy-start | bytes 3145732
  0.1 14.4 %copy-start.3 = (bf16[1024,512]{1,0:T(8,128)(2,1)S(1)}, bf16[1024,512]{1,0:T(8,128)(2,1)}, u32[]{:S(2)}) copy-start(bf16[1024,512]{1,0:T(8,128)(2,1)} %q_ref.7) | copy-start | bytes 3145732
  0.1 14.4 %copy-start.4 = (f32[128]{0:T(128)S(1)}, f32[128]{0:T(128)}, u32[]{:S(2)}) copy-start(f32[128]{0:T(128)} %param.16) | copy-start | bytes 1540
  13.0 8.1 %collective-permute-start = (bf16[4,128,256]{2,1,0:T(8,128)(2,1)S(1)}, bf16[4,128,256]{2,1,0:T(8,128)(2,1)S(1)}, u32[]{:S(2)}, u32[]{:S(2)}) collective-permute-start(bf16[4,128,256]{2,1,0:T(8,128)(2,1)S(1)} %get-tuple-element.73), channel_id=1, source_target_pairs={{0,4},{4,0},{8,12},{12,8},{16,20},{20,16},{24,28},{28,24},{1,5},{5... | collective-permute-start | bytes 786440 | tf_op jit(solution)/shard_map/ppermute | solution.py:504
  21.9 9.1 %collective-permute-start.1 = (bf16[4,128,256]{2,1,0:T(8,128)(2,1)S(1)}, bf16[4,128,256]{2,1,0:T(8,128)(2,1)S(1)}, u32[]{:S(2)}, u32[]{:S(2)}) collective-permute-start(bf16[4,128,256]{2,1,0:T(8,128)(2,1)S(1)} %pair.1.later_ref), channel_id=1, source_target_pairs={{0,8},{4,12},{8,16},{12,20},{16,24},{20,28},{1,9},{5,13},{9,17},{1... | collective-permute-start | bytes 786440 | tf_op jit(solution)/shard_map/ppermute | solution.py:509
  31.1 7.6 %collective-permute-start.2 = (bf16[4,128,128]{2,1,0:T(8,128)(2,1)S(1)}, bf16[4,128,128]{2,1,0:T(8,128)(2,1)S(1)}, u32[]{:S(2)}, u32[]{:S(2)}) collective-permute-start(bf16[4,128,128]{2,1,0:T(8,128)(2,1)S(1)} %step.1), channel_id=1, source_target_pairs={{8,24},{12,28},{9,25},{13,29},{10,26},{14,30},{11,27},{15,31}} | collective-permute-start | bytes 393224 | tf_op jit(solution)/shard_map/ppermute | solution.py:513
  35.6 3.9 %collective-permute-start.3 = (bf16[4,128,128]{2,1,0:T(8,128)(2,1)S(1)}, bf16[4,128,128]{2,1,0:T(8,128)(2,1)S(1)}, u32[]{:S(2)}, u32[]{:S(2)}) collective-permute-start(bf16[4,128,128]{2,1,0:T(8,128)(2,1)S(1)} %step.1), channel_id=1, source_target_pairs={{8,16},{12,20},{9,17},{13,21},{10,18},{14,22},{11,19},{15,23}} | collective-permute-start | bytes 393224 | tf_op jit(solution)/shard_map/ppermute | solution.py:512
  40.4 5.0 %copy-start = (bf16[1024,2048]{1,0:T(8,128)(2,1)S(1)}, bf16[1024,2048]{1,0:T(8,128)(2,1)}, u32[]{:S(2)}) copy-start(bf16[1024,2048]{1,0:T(8,128)(2,1)} %refs_14_.9) | copy-start | bytes 12582916
  40.4 5.0 %collective-permute-start.4 = (bf16[4,128,128]{2,1,0:T(8,128)(2,1)S(1)}, bf16[4,128,128]{2,1,0:T(8,128)(2,1)S(1)}, u32[]{:S(2)}, u32[]{:S(2)}) collective-permute-start(bf16[4,128,128]{2,1,0:T(8,128)(2,1)S(1)} %get-tuple-element.93), channel_id=1, source_target_pairs={{0,4},{4,0},{8,12},{12,8},{16,20},{20,16},{24,28},{28,24},{1,5},{5... | collective-permute-start | bytes 393224 | tf_op jit(solution)/shard_map/ppermute | solution.py:517
  46.9 2.2 %collective-permute-start.5 = (bf16[128,1024]{1,0:T(8,128)(2,1)S(1)}, bf16[128,1024]{1,0:T(8,128)(2,1)S(1)}, u32[]{:S(2)}, u32[]{:S(2)}) collective-permute-start(bf16[128,1024]{1,0:T(8,128)(2,1)S(1)} %get-tuple-element.109), channel_id=1, source_target_pairs={{0,1},{1,0},{2,3},{3,2},{4,5},{5,4},{6,7},{7,6},{8,9},{9,8},{10,11... | collective-permute-start | bytes 786440 | tf_op jit(solution)/shard_map/ppermute | solution.py:587
  49.2 4.4 %collective-permute-start.7 = (bf16[256,1024]{1,0:T(8,128)(2,1)S(1)}, bf16[256,1024]{1,0:T(8,128)(2,1)S(1)}, u32[]{:S(2)}, u32[]{:S(2)}) collective-permute-start(bf16[256,1024]{1,0:T(8,128)(2,1)S(1)} %get-tuple-element.116), channel_id=1, source_target_pairs={{0,1},{1,0},{2,3},{3,2},{4,5},{5,4},{6,7},{7,6},{8,9},{9,8},{10,11... | collective-permute-start | bytes 1572872 | tf_op jit(solution)/shard_map/ppermute | solution.py:587
  49.8 5.5 %collective-permute-start.6 = (bf16[128,512]{1,0:T(8,128)(2,1)S(1)}, bf16[128,512]{1,0:T(8,128)(2,1)S(1)}, u32[]{:S(2)}, u32[]{:S(2)}) collective-permute-start(bf16[128,512]{1,0:T(8,128)(2,1)S(1)} %slice.87), channel_id=1, source_target_pairs={{0,2},{1,3},{2,0},{3,1},{4,6},{5,7},{6,4},{7,5},{8,10},{9,11},{10,... | collective-permute-start | bytes 393224 | tf_op jit(solution)/shard_map/ppermute | solution.py:587
  53.5 4.0 %collective-permute-start.9 = (bf16[256,1024]{1,0:T(8,128)(2,1)S(1)}, bf16[256,1024]{1,0:T(8,128)(2,1)S(1)}, u32[]{:S(2)}, u32[]{:S(2)}) collective-permute-start(bf16[256,1024]{1,0:T(8,128)(2,1)S(1)} %get-tuple-element.124), channel_id=1, source_target_pairs={{0,1},{1,0},{2,3},{3,2},{4,5},{5,4},{6,7},{7,6},{8,9},{9,8},{10,11... | collective-permute-start | bytes 1572872 | tf_op jit(solution)/shard_map/ppermute | solution.py:587
  53.8 8.8 %collective-permute-start.8 = (bf16[256,512]{1,0:T(8,128)(2,1)S(1)}, bf16[256,512]{1,0:T(8,128)(2,1)S(1)}, u32[]{:S(2)}, u32[]{:S(2)}) collective-permute-start(bf16[256,512]{1,0:T(8,128)(2,1)S(1)} %slice.85), channel_id=1, source_target_pairs={{0,2},{1,3},{2,0},{3,1},{4,6},{5,7},{6,4},{7,5},{8,10},{9,11},{10,... | collective-permute-start | bytes 786440 | tf_op jit(solution)/shard_map/ppermute | solution.py:587
  57.6 7.4 %collective-permute-start.11 = (bf16[256,1024]{1,0:T(8,128)(2,1)S(1)}, bf16[256,1024]{1,0:T(8,128)(2,1)S(1)}, u32[]{:S(2)}, u32[]{:S(2)}) collective-permute-start(bf16[256,1024]{1,0:T(8,128)(2,1)S(1)} %get-tuple-element.132), channel_id=1, source_target_pairs={{0,1},{1,0},{2,3},{3,2},{4,5},{5,4},{6,7},{7,6},{8,9},{9,8},{10,11... | collective-permute-start | bytes 1572872 | tf_op jit(solution)/shard_map/ppermute | solution.py:587
  62.9 9.3 %collective-permute-start.10 = (bf16[256,512]{1,0:T(8,128)(2,1)S(1)}, bf16[256,512]{1,0:T(8,128)(2,1)S(1)}, u32[]{:S(2)}, u32[]{:S(2)}) collective-permute-start(bf16[256,512]{1,0:T(8,128)(2,1)S(1)} %slice.84), channel_id=1, source_target_pairs={{0,2},{1,3},{2,0},{3,1},{4,6},{5,7},{6,4},{7,5},{8,10},{9,11},{10,... | collective-permute-start | bytes 786440 | tf_op jit(solution)/shard_map/ppermute | solution.py:587
  65.0 7.3 %collective-permute-start.13 = (bf16[128,1024]{1,0:T(8,128)(2,1)S(1)}, bf16[128,1024]{1,0:T(8,128)(2,1)S(1)}, u32[]{:S(2)}, u32[]{:S(2)}) collective-permute-start(bf16[128,1024]{1,0:T(8,128)(2,1)S(1)} %get-tuple-element.140), channel_id=1, source_target_pairs={{0,1},{1,0},{2,3},{3,2},{4,5},{5,4},{6,7},{7,6},{8,9},{9,8},{10,11... | collective-permute-start | bytes 786440 | tf_op jit(solution)/shard_map/ppermute | solution.py:587
  65.3 12.5 %collective-permute-start.12 = (bf16[256,512]{1,0:T(8,128)(2,1)S(1)}, bf16[256,512]{1,0:T(8,128)(2,1)S(1)}, u32[]{:S(2)}, u32[]{:S(2)}) collective-permute-start(bf16[256,512]{1,0:T(8,128)(2,1)S(1)} %slice.83), channel_id=1, source_target_pairs={{0,2},{1,3},{2,0},{3,1},{4,6},{5,7},{6,4},{7,5},{8,10},{9,11},{10,... | collective-permute-start | bytes 786440 | tf_op jit(solution)/shard_map/ppermute | solution.py:587
  72.4 7.0 %collective-permute-start.14 = (bf16[128,512]{1,0:T(8,128)(2,1)S(1)}, bf16[128,512]{1,0:T(8,128)(2,1)S(1)}, u32[]{:S(2)}, u32[]{:S(2)}) collective-permute-start(bf16[128,512]{1,0:T(8,128)(2,1)S(1)} %slice.86), channel_id=1, source_target_pairs={{0,2},{1,3},{2,0},{3,1},{4,6},{5,7},{6,4},{7,5},{8,10},{9,11},{10,... | collective-permute-start | bytes 393224 | tf_op jit(solution)/shard_map/ppermute | solution.py:587
  77.9 1.4 %copy-start.5 = (bf16[1024,512]{1,0:T(8,128)(2,1)}, bf16[1024,512]{1,0:T(8,128)(2,1)S(1)}, u32[]{:S(2)}) copy-start(bf16[1024,512]{1,0:T(8,128)(2,1)S(1)} %fusion.5) | copy-start | bytes 3145732

commit v4 on v3

v4 whole, which is shorter than its diff:
```python
import functools

import jax
import jax.numpy as jnp
from jax import lax
from jax.experimental import pallas as pl
from jax.experimental.pallas import tpu as pltpu
from jax.sharding import PartitionSpec as P

DK = 128
DV = 128
BLK = 128
SUB = 16
EPS = 1e-06
FAR = -1e30
F32 = jnp.float32
BF16 = jnp.bfloat16
MIB = 1024 * 1024


def dot(a, b):
    return jnp.dot(a, b, preferred_element_type=F32)


def dot_t(a, b):
    return lax.dot_general(a, b, (((1,), (1,)), ((), ())), preferred_element_type=F32)


def running_sum(values):
    lane = lax.broadcasted_iota(jnp.int32, values.shape, 1)
    step = 1
    while step < BLK:
        values = values + jnp.where(lane >= step, pltpu.roll(values, step, 1), 0.0)
        step *= 2
    return values


def columns_of(rows):
    pad = BLK - rows.shape[0]
    return jnp.transpose(jnp.concatenate([rows, jnp.zeros((pad, BLK), F32)], axis=0))


def doc_mask(reset_col, reset_row, strict):
    i = lax.broadcasted_iota(jnp.int32, (BLK, BLK), 0)
    j = lax.broadcasted_iota(jnp.int32, (BLK, BLK), 1)
    below = (i > j) if strict else (i >= j)
    return jnp.where(below & (reset_col == reset_row), 0.0, FAR)


def place_of(part, parts):
    if parts == 1:
        return 0
    odd = lax.rem(lax.axis_index("seq"), 2)
    return odd if part == 1 else 1 - odd


def small_inverses(lower, count):
    lane = lax.broadcasted_iota(jnp.int32, (SUB, BLK), 1)
    packed = []
    for m in lower:
        kept = m[:SUB]
        for b in range(1, BLK // SUB):
            kept = jnp.where(lane // SUB == b, m[b * SUB : (b + 1) * SUB], kept)
        packed.append(kept.astype(BF16))
    packed = jnp.concatenate(packed, axis=0)
    i = lax.broadcasted_iota(jnp.int32, (BLK, BLK), 0)
    j = lax.broadcasted_iota(jnp.int32, (BLK, BLK), 1)
    same = i // SUB == j // SUB
    place = lax.broadcasted_iota(jnp.int32, (count, SUB, BLK), 1)
    lanes = lax.broadcasted_iota(jnp.int32, (count, SUB, BLK), 2)
    found = jnp.where(place == lanes % SUB, 1.0, 0.0)
    for m in range(0, SUB, 2):
        spread = [jnp.where(same & (i % SUB == m + d), 1.0, 0.0).astype(BF16) for d in range(2)]
        pair = dot(packed, jnp.concatenate(spread, axis=1)).reshape(count, SUB, 2 * BLK)
        for d in range(2):
            if m + d < SUB - 1:
                found = found - pair[:, :, d * BLK : (d + 1) * BLK] * found[:, m + d : m + d + 1, :]
    return found.astype(BF16)


def odd_rows(matrix, size):
    return jnp.concatenate(
        [matrix[p : p + size] for p in range(size, BLK, 2 * size)], axis=0
    )


def with_odd_rows(matrix, rows, size):
    parts = []
    for p in range(0, BLK, 2 * size):
        parts.append(matrix[p : p + size])
        parts.append(rows[p // 2 : p // 2 + size])
    return jnp.concatenate(parts, axis=0)


def shard_kernel(
    part, parts, per_key, blocks, keys, *refs
):
    if part == 0:
        log_in, rate_in, start_in, k_in, v_in = refs[:5]
        wu_ref, zc_ref, rows_ref, end_ref, log_ref, rate_ref, start_ref, k_ref, v_ref = refs[5:14]
    else:
        log_ref, rate_ref, start_ref, k_ref, v_ref, wu_ref, zc_ref, rows_ref, end_ref = refs[:9]
    logs, rates, norms, kt, db, keep, state = refs[len(refs) - 7 :] if part else refs[14:21]
    mine = place_of(part, parts)
    small_copies, k_copies, v_copies = [], [], []
    if part == 0:
        small_sems, k_sems, v_sems = refs[21:]
        for at, (ref, here) in enumerate(
            ((log_in, log_ref), (rate_in, rate_ref), (start_in, start_ref))
        ):
            small_copies.append(pltpu.make_async_copy(ref, here, small_sems.at[at]))
        for copies, ref, here, sems in (
            (k_copies, k_in, k_ref, k_sems),
            (v_copies, v_in, v_ref, v_sems),
        ):
            for c in range(blocks):
                span = slice(c * BLK, (c + 1) * BLK)
                copies.append(pltpu.make_async_copy(ref.at[span], here.at[span], sems.at[c]))
        for copy in small_copies + k_copies + v_copies:
            copy.start()
        for copy in small_copies:
            copy.wait()
    key_lanes = lambda key: pl.ds(pl.multiple_of((mine * keys + key) * DK, DK), DK)
    head_lanes = lambda h: pl.ds(pl.multiple_of((mine * keys * per_key + h) * DV, DV), DV)
    heads = keys * per_key
    count = heads * blocks
    for place in range(parts):

        @pl.when(mine == place)
        def _():
            for h in range(heads):
                head = place * heads + h
                for c in range(blocks):
                    at = h * blocks + c
                    span = slice(c * BLK, (c + 1) * BLK)
                    logs[at : at + 1, :] = log_ref[head : head + 1, span]
                    rates[at : at + 1, :] = rate_ref[head : head + 1, span]

    starts = start_ref[...].astype(F32)
    sums = running_sum(jnp.concatenate([logs[...], starts], axis=0))
    cum, reset = sums[:count], sums[count:]
    inner = []
    for copy in k_copies:
        copy.wait()
    for key in range(keys):
        for c in range(blocks):
            rows = k_ref[c * BLK : (c + 1) * BLK, key_lanes(key)]
            flipped = jnp.transpose(rows.astype(F32))
            turned = flipped.astype(BF16)
            kt[key * blocks + c] = turned
            norms[key * blocks + c : key * blocks + c + 1, :] = jnp.sum(
                flipped * flipped, axis=0, keepdims=True
            )
            inner.append(dot(rows, turned))
    reset_cols = columns_of(reset)
    masks = [doc_mask(reset_cols[:, c : c + 1], reset[c : c + 1, :], True) for c in range(blocks)]

    squares = norms[...] + EPS
    squares = jnp.concatenate(
        [squares[(h // per_key) * blocks : (h // per_key + 1) * blocks] for h in range(heads)], axis=0
    )
    scale = lax.rsqrt(squares)
    log_scale = -0.5 * jnp.log(squares)
    resets = jnp.concatenate([reset] * heads, axis=0)
    rate = rates[...]
    last = cum[:, BLK - 1 :]
    last_reset = resets[:, BLK - 1 :]
    left_cols = columns_of(cum + jnp.log(rate) + log_scale)
    right = cum - log_scale
    head_keep = jnp.where(resets == 0.0, jnp.exp(cum), 0.0)
    tail = jnp.where(resets == last_reset, jnp.exp(last - cum), 0.0) * scale
    erase_row = rate * head_keep * scale
    keep[...] = jnp.broadcast_to(jnp.where(last_reset == 0.0, jnp.exp(last), 0.0), (count, BLK))
    rows_ref[0:count, :] = cum
    rows_ref[count : 2 * count, :] = right
    rows_ref[2 * count :, :] = reset

    lower = []
    for at in range(count):
        c = at % blocks
        gap = left_cols[:, at : at + 1] - right[at : at + 1, :] + masks[c]
        lower.append(inner[at // (per_key * blocks) * blocks + c] * jnp.exp(gap))
    packed = small_inverses(lower, count)
    lower = [m.astype(BF16) for m in lower]
    lane = lax.broadcasted_iota(jnp.int32, (SUB, BLK), 1)
    zero = jnp.zeros((SUB, BLK), BF16)
    ones = [jnp.where(lane // SUB == b, 1.0, 0.0).astype(BF16) for b in range(BLK // SUB)]
    inverse = [
        jnp.concatenate([packed[at] * ones[b] for b in range(BLK // SUB)], axis=0)
        for at in range(count)
    ]
    size = SUB
    while size < BLK:
        i = lax.broadcasted_iota(jnp.int32, (BLK // 2, BLK), 0)
        j = lax.broadcasted_iota(jnp.int32, (BLK // 2, BLK), 1)
        reach = jnp.where(j // size == 2 * (i // size), 1.0, 0.0).astype(BF16)
        odd = [odd_rows(t, size) for t in inverse]
        half = [dot(o, m).astype(BF16) * reach for o, m in zip(odd, lower)]
        fresh = [o - dot(f, t).astype(BF16) for o, f, t in zip(odd, half, inverse)]
        inverse = [with_odd_rows(t, f, size) for t, f in zip(inverse, fresh)]
        size *= 2
    for copy in v_copies:
        copy.wait()
    for at in range(count):
        c, h = at % blocks, at // blocks
        key = h // per_key
        span = slice(c * BLK, (c + 1) * BLK)
        t = inverse[at].astype(F32)
        erase = dot(
            (t * erase_row[at : at + 1, :]).astype(BF16), k_ref[span, key_lanes(key)]
        )
        write = dot((t * rate[at : at + 1, :]).astype(BF16), v_ref[span, head_lanes(h)])
        wu_ref[at, :, :DK] = erase.astype(BF16)
        wu_ref[at, :, DK:] = write.astype(BF16)
    for at in range(count):
        c, key = at % blocks, at // (per_key * blocks)
        tailed = (kt[key * blocks + c].astype(F32) * tail[at : at + 1, :]).astype(BF16)
        db[at] = dot(tailed, wu_ref[at]).astype(BF16)

    i = lax.broadcasted_iota(jnp.int32, (DK, DK), 0)
    j = lax.broadcasted_iota(jnp.int32, (DK, DK), 1)
    for h in range(heads):
        state[h, :, :DV] = jnp.zeros((DK, DV), F32)
        state[h, :, DV:] = jnp.where(i == j, 1.0, 0.0)
    for c in range(blocks):
        for h in range(heads):
            now = state[h]
            low = now.astype(BF16)
            at = h * blocks + c
            zc_ref[at] = low
            moved = dot(db[at, :, :DK], low)
            g = keep[at : at + 1, :]
            state[h, :, :DV] = g * now[:, :DV] - moved[:, :DV] + db[at, :, DK:].astype(F32)
            state[h, :, DV:] = g * now[:, DV:] - moved[:, DV:]
    for h in range(heads):
        end_ref[h] = state[h].astype(BF16)


def vmem(shape, dtype):
    return pltpu.VMEM(shape, dtype)


def in_hbm(array):
    return pltpu.with_memory_space_constraint(array, pltpu.HBM)


def in_vmem():
    return pl.BlockSpec(memory_space=pltpu.VMEM)


def shard_pass(part, parts, arrays, heads_here, per_key):
    tokens_here = arrays[3].shape[0]
    heads = heads_here // parts
    keys = heads // per_key
    blocks = tokens_here // BLK
    count = heads * blocks
    wide = DK + DV
    shapes = [
        vmem((count, BLK, wide), BF16),
        vmem((count, DK, wide), BF16),
        vmem((2 * count + blocks, BLK), F32),
        vmem((heads, DK, wide), BF16),
    ]
    scratch = [
        pltpu.VMEM((count, BLK), F32),
        pltpu.VMEM((count, BLK), F32),
        pltpu.VMEM((keys * blocks, BLK), F32),
        pltpu.VMEM((keys * blocks, DK, BLK), BF16),
        pltpu.VMEM((count, DK, wide), BF16),
        pltpu.VMEM((count, BLK), F32),
        pltpu.VMEM((heads, DK, wide), F32),
    ]
    if part == 0:
        shapes += [vmem(a.shape, a.dtype) for a in arrays]
        scratch += [pltpu.SemaphoreType.DMA((n,)) for n in (3, blocks, blocks)]
        arrays = [in_hbm(a) for a in arrays]
        space = pltpu.HBM
    else:
        space = pltpu.VMEM
    outs = pl.pallas_call(
        functools.partial(shard_kernel, part, parts, per_key, blocks, keys),
        in_specs=[pl.BlockSpec(memory_space=space)] * 5,
        out_specs=[in_vmem()] * len(shapes),
        out_shape=shapes,
        scratch_shapes=scratch,
        compiler_params=pltpu.CompilerParams(vmem_limit_bytes=24 * MIB),
        cost_estimate=pl.CostEstimate(
            flops=count * 18 * 2 * BLK**3, bytes_accessed=4 * MIB, transcendentals=0
        ),
        name="shard_pass",
    )(*arrays)
    return list(outs[:4]), outs[4:]


def local_kernel(
    part, parts, per_key, blocks, at_key, rows_ref, q_ref, k_ref, gate_ref, gain_ref, wu_ref, zc_ref,
    out_ref, carry_ref, gated_ref,
):
    count = per_key * blocks
    keys = wu_ref.shape[0] // count
    key = place_of(part, parts) * keys + at_key
    narrow = pl.ds(pl.multiple_of(key * DK, DK), DK)
    total = (rows_ref.shape[0] - blocks) // 2
    base = at_key * count
    cum = rows_ref[base : base + count, :]
    right = rows_ref[total + base : total + base + count, :]
    reset = rows_ref[2 * total :, :]
    cols = columns_of(jnp.concatenate([cum, reset], axis=0))
    units, inner, masks = [], [], []
    for c in range(blocks):
        span = slice(c * BLK, (c + 1) * BLK)
        query = q_ref[span, narrow].astype(F32)
        units.append(jnp.sum(query * query, axis=1, keepdims=True) + EPS)
        inner.append(dot_t(q_ref[span, narrow], k_ref[span, narrow]))
        masks.append(doc_mask(cols[:, count + c : count + c + 1], reset[c : c + 1, :], False))
    scores = []
    for at in range(count):
        c = at % blocks
        left = cols[:, at : at + 1] - 0.5 * jnp.log(units[c])
        gap = left - right[at : at + 1, :] + masks[c]
        scores.append((inner[c] * jnp.exp(gap)).astype(BF16))
    seen = [dot(scores[at], wu_ref[base + at]) for at in range(count)]
    for at in range(count):
        c, h = at % blocks, at // blocks
        span = slice(c * BLK, (c + 1) * BLK)
        wide = slice(h * DV, (h + 1) * DV)
        reset_col = cols[:, count + c : count + c + 1]
        keep = jnp.where(reset_col == 0.0, jnp.exp(cols[:, at : at + 1]), 0.0) * lax.rsqrt(units[c])
        g = (keep * q_ref[span, narrow].astype(F32) - seen[at][:, :DK]).astype(BF16)
        both = dot(g, zc_ref[base + at])
        out_ref[span, wide] = both[:, :DV] + seen[at][:, DK:]
        carry_ref[span, wide] = both[:, DV:].astype(BF16)
        first = pl.multiple_of((key * per_key + h) * DV, DV)
        gate = gate_ref[span, pl.ds(first, DV)].astype(F32)
        gated_ref[span, wide] = gain_ref[...] * (gate / (1.0 + jnp.exp(-gate)))


def local_pass(part, parts, at_key, rows, queries, key_rows, out_gate, gain, wu, zc, per_key):
    tokens_here = queries.shape[0]
    blocks = tokens_here // BLK
    count = per_key * blocks
    wide = per_key * DV
    return pl.pallas_call(
        functools.partial(local_kernel, part, parts, per_key, blocks, at_key),
        in_specs=[in_vmem()] * 7,
        out_specs=[in_vmem()] * 3,
        out_shape=[
            vmem((tokens_here, wide), F32),
            vmem((tokens_here, wide), BF16),
            vmem((tokens_here, wide), F32),
        ],
        compiler_params=pltpu.CompilerParams(vmem_limit_bytes=16 * MIB),
        cost_estimate=pl.CostEstimate(
            flops=count * 8 * 2 * BLK**3, bytes_accessed=4 * MIB, transcendentals=0
        ),
        name="local_pass",
    )(rows, queries, key_rows, out_gate, gain, wu, zc)


def finish_kernel(row, per_key, parts, order, *refs):
    me = lax.axis_index("head")
    keys_here = (len(refs) - parts - 3) // 3
    outs = refs[:keys_here]
    carries = refs[keys_here : 2 * keys_here]
    gates = refs[2 * keys_here : 3 * keys_here]
    starts = refs[3 * keys_here : 3 * keys_here + parts]
    weight_ref, send_ref, keep_ref = refs[3 * keys_here + parts :]
    rows = slice(row, row + send_ref.shape[0])
    heads = keys_here * per_key // parts
    normed = []
    for part in range(parts):
        pieces = []
        for head in range(heads):
            key, h = part * (keys_here // parts) + head // per_key, head % per_key
            span = slice(h * DV, (h + 1) * DV)
            seen = outs[key][rows, span] + dot(carries[key][rows, span], starts[part][head])
            spread = jnp.mean(seen * seen, axis=1, keepdims=True)
            pieces.append((seen * lax.rsqrt(spread + EPS) * gates[key][rows, span]).astype(BF16))
        normed.append(jnp.concatenate(pieces, axis=1))
    columns = weight_ref.shape[1] // len(order)
    sends = len(order) // 2
    for at, place in enumerate(order):
        first = pl.multiple_of((me ^ place) * columns, columns)
        total = None
        for part in range(parts):
            top = pl.multiple_of(place_of(part, parts) * (heads * DV), heads * DV)
            term = dot(normed[part], weight_ref[pl.ds(top, heads * DV), pl.ds(first, columns)])
            total = term if total is None else total + term
        to, slot = (send_ref, at - sends) if at >= sends else (keep_ref, at)
        to[:, slot * columns : (slot + 1) * columns] = total.astype(BF16)


def halving_order(size):
    def split(group, bit):
        if len(group) == 1:
            return group
        kept = [p for p in group if not p & bit]
        return split(kept, 2 * bit) + split([p for p in group if p & bit], 2 * bit)

    return split(list(range(size)), 1)


def finish_pass(row, rows, outs, carries, gates, starts, weight, per_key, devices):
    keys_here = len(outs)
    half = weight.shape[1] // 2
    return pl.pallas_call(
        functools.partial(
            finish_kernel, row, per_key, len(starts), halving_order(devices)
        ),
        in_specs=[in_vmem()] * (3 * keys_here + len(starts) + 1),
        out_specs=[in_vmem()] * 2,
        out_shape=[vmem((rows, half), BF16)] * 2,
        compiler_params=pltpu.CompilerParams(vmem_limit_bytes=16 * MIB),
        cost_estimate=pl.CostEstimate(
            flops=rows, bytes_accessed=rows, transcendentals=0
        ),
        name="finish_pass",
    )(*outs, *carries, *gates, *starts, weight)


def composed(later, earlier, h):
    return dot(later[h, :, DV:], earlier[h]) + later[h, :, :DV].astype(F32)


def pair_kernel(mine_ref, got_ref, both_ref, begun_ref):
    odd = lax.rem(lax.axis_index("seq"), 2) == 1

    def join(second, first):
        for h in range(both_ref.shape[0]):
            moved = dot(second[h, :, DV:], first[h])
            begun = (moved[:, :DV] + second[h, :, :DV].astype(F32)).astype(BF16)
            begun_ref[h] = begun
            both_ref[h, :, :DV] = begun
            both_ref[h, :, DV:] = moved[:, DV:].astype(BF16)

    @pl.when(odd)
    def _():
        join(mine_ref, got_ref)

    @pl.when(jnp.logical_not(odd))
    def _():
        join(got_ref, mine_ref)


def step_kernel(later_ref, earlier_ref, out_ref):
    for h in range(out_ref.shape[0]):
        out_ref[h] = composed(later_ref, earlier_ref, h).astype(BF16)


def last_kernel(
    mine_ref, got_ref, first_ref, before_ref, near_ref, far_ref, own_ref, other_ref
):
    odd = lax.rem(lax.axis_index("seq"), 2) == 1
    pair = lax.div(lax.axis_index("seq"), 2)

    def fill(first, here_ref, then_ref):
        for h in range(own_ref.shape[0]):
            here = composed(before_ref, far_ref, h).astype(BF16)
            here = jnp.where(pair == 2, near_ref[h], here)
            here_ref[h] = jnp.where(pair == 1, first_ref[h], here)
        for h in range(own_ref.shape[0]):
            then_ref[h] = composed(first, here_ref, h).astype(BF16)

    @pl.when(odd)
    def _():
        fill(got_ref, other_ref, own_ref)

    @pl.when(jnp.logical_not(odd))
    def _():
        fill(mine_ref, own_ref, other_ref)


def small_call(kernel, name, outs, *arrays):
    heads = arrays[0].shape[0]
    return pl.pallas_call(
        kernel,
        in_specs=[in_vmem()] * len(arrays),
        out_specs=[in_vmem()] * len(outs),
        out_shape=[vmem(a.shape, a.dtype) for a in outs],
        compiler_params=pltpu.CompilerParams(vmem_limit_bytes=4 * MIB),
        cost_estimate=pl.CostEstimate(
            flops=heads * 4 * DK**3, bytes_accessed=MIB, transcendentals=0
        ),
        name=name,
    )(*arrays)


def step_call(later, earlier):
    return small_call(
        step_kernel, "step", [jax.ShapeDtypeStruct(earlier.shape, BF16)], later, earlier
    )[0]


def route(axis, target):
    size = lax.axis_size(axis)
    return [(i, target(i)) for i in range(size) if target(i) is not None]


def exchanged(mine, got, work):
    state = jax.ShapeDtypeStruct(mine.shape[:2] + (DV,), BF16)
    both, begun = small_call(
        pair_kernel, "pair", [jax.ShapeDtypeStruct(mine.shape, BF16), state], mine, got
    )
    first = lax.ppermute(begun, "seq", [(0, 2), (1, 3)])
    before = lax.ppermute(both, "seq", [(4, 6), (5, 7)])
    first = work(work(first))
    third = step_call(both, first)
    near = lax.ppermute(third, "seq", [(2, 4), (3, 5)])
    far = work(lax.ppermute(third, "seq", [(2, 6), (3, 7)]))
    own, other = small_call(
        last_kernel, "last", [state] * 2, mine, got, first, before, near, far
    )
    return own, work(lax.ppermute(other, "seq", route("seq", lambda i: i ^ 1)))


def handed_on(end):
    size = lax.axis_size("seq")
    onward = route("seq", lambda i: i + 1 if i + 1 < size else None)

    def hop(step, state):
        return lax.ppermute(step_call(end, state), "seq", onward)

    return lax.fori_loop(0, size - 1, hop, jnp.zeros(end.shape[:2] + (DV,), BF16))


def assemble_kernel(pieces, *refs):
    kept, got, out_ref = refs[:pieces], refs[pieces : 2 * pieces], refs[2 * pieces]
    row = 0
    for keep_ref, got_ref in zip(kept, got):
        rows, columns = got_ref.shape
        total = keep_ref[:, :columns].astype(F32) + got_ref[...].astype(F32)
        out_ref[row : row + rows, :] = total.astype(BF16)
        row += rows


def assemble(kept, got):
    shape = (sum(piece.shape[0] for piece in got), got[0].shape[1])
    return pl.pallas_call(
        functools.partial(assemble_kernel, len(got)),
        grid=(1,),
        in_specs=[in_vmem()] * (2 * len(got)),
        out_specs=pl.BlockSpec(shape, lambda i: (0, 0)),
        out_shape=jax.ShapeDtypeStruct(shape, BF16),
        compiler_params=pltpu.CompilerParams(vmem_limit_bytes=8 * MIB),
        name="assemble",
    )(*kept, *got)


def local(
    queries, key_rows, value_rows, out_gate, write_rate, log_gate, doc_start, norm_gain, out_weight
):
    tokens_here = queries.shape[0]
    heads_here = value_rows.shape[1] // DV
    keys_here = key_rows.shape[1] // DK
    per_key = heads_here // keys_here
    devices = lax.axis_size("head")
    parts = 2 if lax.axis_size("seq") == 8 and keys_here % 2 == 0 else 1
    keys = keys_here // parts
    starts = doc_start.reshape(tokens_here // BLK, BLK)
    gain = norm_gain.reshape(1, DV)
    queries, out_gate, weight, gain = (
        pltpu.with_memory_space_constraint(a, pltpu.VMEM)
        for a in (queries, out_gate, out_weight, gain)
    )
    shards, got = [], None
    held = [log_gate, write_rate, starts, key_rows, value_rows]
    for part in range(parts):
        shard, here = shard_pass(part, parts, held, heads_here, per_key)
        shards.append(shard)
        if part == 0:
            held = here
            nearby_keys = held[3]
            if parts == 2:
                got = lax.ppermute(shard[3], "seq", route("seq", lambda i: i ^ 1))
    outs, carries, gates = [], [], []

    def work(coming):
        at = len(outs)
        if at == keys_here:
            return coming
        wu, zc, rows, _ = shards[at // keys]
        out, carry, gate = local_pass(
            at // keys, parts, at % keys, rows, queries, nearby_keys, out_gate, gain, wu, zc, per_key
        )
        coming, out, carry, gate = lax.optimization_barrier((coming, out, carry, gate))
        outs.append(out)
        carries.append(carry)
        gates.append(gate)
        return coming

    if parts == 2:
        mine = shards[1][3]
        rows, mine = lax.optimization_barrier((shards[0][2], mine))
        shards[0][2] = rows
        own, back = exchanged(mine, got, work)
        states = [back, own]
    else:
        states = [handed_on(shards[0][3])]
    while len(outs) < keys_here:
        states[0] = work(states[0])

    unit = tokens_here // 16
    sizes = [unit * share for share in (4, 4, 4, 4)]
    firsts = [sum(sizes[:index]) for index in range(len(sizes))]
    kept, arrived = [], []
    for first, rows in zip(firsts, sizes):
        send, keep = finish_pass(
            first, rows, outs, carries, gates, states, weight, per_key, devices
        )
        bit = 1
        while bit < devices:
            got = lax.ppermute(send, "head", route("head", lambda i: i ^ bit))
            bit *= 2
            if bit < devices:
                keep = keep.astype(F32) + got.astype(F32)
                width = keep.shape[1] // 2
                send = keep[:, width:].astype(BF16)
                keep = keep[:, :width] if 2 * bit < devices else keep
        kept.append(keep)
        arrived.append(got)
    return assemble(kept, arrived)


def solution(mesh):
    placed = (
        P("seq", "head"),
        P("seq", "head"),
        P("seq", "head"),
        P("seq", "head"),
        P("head", "seq"),
        P("head", "seq"),
        P("seq"),
        P(),
        P("head", None),
    )
    return jax.shard_map(
        local, mesh=mesh, in_specs=placed, out_specs=P("seq", "head"), check_vma=False
    )
```

time: 81.1 us -> 73.3 us (0.904)
  waiting for transfers between devices: 28.3 us -> 24.8 us
  starting transfers between devices: 18.1 us -> 16 us
  Pallas kernels: 31.4 us -> 30.4 us
  other arithmetic: 1.64 us -> 0.68 us
    ppermute x5 -> x6, waiting for transfers between devices: 10.8 us -> 4.51 us  [the longest x1 2.03 us: exchanged(): lax.ppermute(other, 'seq', route('seq', lambda i: i ^ 1))]
    ppermute x10 -> x8, waiting for transfers between devices: 17.5 us -> 20.2 us  [local(): got = lax.ppermute(send, 'head', route('head', lambda i: i ^ bit))]
    ppermute x5 -> x6, starting transfers between devices: 12.4 us -> 10.4 us  [the longest x1 3.75 us: exchanged(): far = work(lax.ppermute(third, 'seq', [(2, 6), (3, 7)]))]
    pallas_call x13 -> x14, Pallas kernels: 31.4 us -> 30.4 us  [the longest x2 14.6 us: shard_pass(): pl.pallas_call(functools.partial(shard_kernel, part, parts, per_key, bloc...]
    dynamic_update_slice x4 -> x0, other arithmetic: 0.91 us -> none  [local(): mixed = lax.dynamic_update_slice(mixed, keep.astype(BF16), (place, 0))]
    ppermute x10 -> x8, starting transfers between devices: 5.7 us -> 5.54 us  [local(): got = lax.ppermute(send, 'head', route('head', lambda i: i ^ bit))]
  transfers between devices with their start and end apart: 15 -> 14, of which waited for: 9 -> 9; matrix products, arithmetic and copies ran while one was open for 1% -> 1% of each run, Pallas kernels for 19% -> 26%
where the time goes in v4:
time: 73.3 us; the launch traced here: 72.2 us
  Pallas kernels  30.4 us (41%)
  waiting for transfers between devices  24.8 us (34%)
  starting transfers between devices  16 us (22%)
    ppermute x8, waiting for transfers between devices, local(): got = lax.ppermute(send, 'head', route('head', lambda i: i ^ bit))  20.2 us
    pallas_call x2, Pallas kernels, shard_pass(): pl.pallas_call(functools.partial(shard_kernel, part, parts, per_key, bloc...  14.6 us
    pallas_call x4, Pallas kernels, local_pass(): pl.pallas_call(functools.partial(local_kernel, part, parts, per_key, bloc...  7.66 us
    pallas_call x4, Pallas kernels, finish_pass(): pl.pallas_call(functools.partial(finish_kernel, row, per_key, len(starts)...  6.3 us
    ppermute x8, starting transfers between devices, local(): got = lax.ppermute(send, 'head', route('head', lambda i: i ^ bit))  5.54 us
    ppermute x1, starting transfers between devices, exchanged(): far = work(lax.ppermute(third, 'seq', [(2, 6), (3, 7)]))  3.75 us
    ppermute x1, waiting for transfers between devices, exchanged(): lax.ppermute(other, 'seq', route('seq', lambda i: i ^ 1))  2.03 us
    ppermute x1, starting transfers between devices, exchanged(): near = lax.ppermute(third, 'seq', [(2, 4), (3, 5)])  1.86 us
  transfers between devices with their start and end apart: 14, of which 9 were waited for; matrix products, arithmetic and copies ran while one was open for 1% of the time, Pallas kernels for 26%

profile of v4, /device:TPU:8, one launch (start us, length us, event | category | flops | bytes accessed | tf_op | source)
XLA Modules:
  0.0 72.2 jit_solution(11469157016791480420)
XLA Ops:
  0.0 8.3 %shard_pass.2 = (bf16[32,128,256]{2,1,0:T(8,128)(2,1)S(1)}, bf16[32,128,256]{2,1,0:T(8,128)(2,1)S(1)}, f32[72,128]{1,0:T(8,128)S(1)}, bf16[4,128,256]{2,1,0:T(8,...) custom-call(f32[8,1024]{1,0:T(8,128)} %refs_0_.1, ...), custom_call_target="tpu_custom_call" | custom-call | flops 2415919104 | bytes 4194304 | tf_op jit(solution)/shard_map/shard_pass/pallas_call | solution.py:280
  8.3 1.5 %collective-permute-start = (bf16[4,128,256]{2,1,0:T(8,128)(2,1)S(1)}, bf16[4,128,256]{2,1,0:T(8,128)(2,1)S(1)}, u32[]{:S(2)}, u32[]{:S(2)}) collective-permute-start(bf16[4,128,256]{2,1,0:T(8,128)(2,1)S(1)} %get-tuple-element.68), channel_id=1, source_target_pairs={{0,4},{4,0},{8,12},{12,8},{16,20},{20,16},{24,28},{28,24},{1,5},{5... | collective-permute-start | bytes 786440 | tf_op jit(solution)/shard_map/ppermute | solution.py:574
  9.8 0.0 copy-start.1
  9.8 0.0 copy-start.2
  9.8 0.0 copy-start.3
  9.8 6.3 %shard_pass.3 = (bf16[32,128,256]{2,1,0:T(8,128)(2,1)S(1)}, bf16[32,128,256]{2,1,0:T(8,128)(2,1)S(1)}, f32[72,128]{1,0:T(8,128)S(1)}, bf16[4,128,256]{2,1,0:T(8,128)(2,1)S(1)}) custom-call(f32[8,1024]{1,0:T(8,128)S(1)} %get-tuple-element.61.refs_0_, f32[8,1024]{1,0:T(8,128)S(1)} %get-tuple-element.62.refs_1_, s32[8,128]{1,0:T(8,128)S(1)} %get-tuple-element.63.refs_2_, ...), custom_call_target="tpu_custom_call" | custom-call | flops 2415919104 | bytes 4194304 | tf_op jit(solution)/shard_map/shard_pass/pallas_call | solution.py:280
  16.2 0.2 collective-permute-done.got_ref
  16.4 0.2 pair.1
  16.6 1.3 %collective-permute-start.1 = (bf16[4,128,128]{2,1,0:T(8,128)(2,1)S(1)}, bf16[4,128,128]{2,1,0:T(8,128)(2,1)S(1)}, u32[]{:S(2)}, u32[]{:S(2)}) collective-permute-start(bf16[4,128,128]{2,1,0:T(8,128)(2,1)S(1)} %get-tuple-element.69), channel_id=1, source_target_pairs={{0,8},{4,12},{1,9},{5,13},{2,10},{6,14},{3,11},{7,15}} | collective-permute-start | bytes 393224 | tf_op jit(solution)/shard_map/ppermute | solution.py:504
  17.9 0.9 %collective-permute-start.3 = (bf16[4,128,256]{2,1,0:T(8,128)(2,1)S(1)}, bf16[4,128,256]{2,1,0:T(8,128)(2,1)S(1)}, u32[]{:S(2)}, u32[]{:S(2)}) collective-permute-start(bf16[4,128,256]{2,1,0:T(8,128)(2,1)S(1)} %get-tuple-element.82.later_ref), channel_id=1, source_target_pairs={{16,24},{20,28},{17,25},{21,29},{18,26},{22,30},{19,27},{23,31}} | collective-permute-start | bytes 786440 | tf_op jit(solution)/shard_map/ppermute | solution.py:505
  18.8 0.0 copy-done.1
  18.8 0.0 copy-done.2
  18.8 0.0 copy-done.3
  18.8 1.9 %local_pass.4 = (f32[1024,256]{1,0:T(8,128)S(1)}, bf16[1024,256]{1,0:T(8,128)(2,1)S(1)}, f32[1024,256]{1,0:T(8,128)S(1)}) custom-call(f32[72,128]{1,0:T(8,128)S(1)} %get-tuple-element.70.rows_ref, bf16[1024,512]{1,0:T(8,128)(2,1)S(1)} %copy-done.2, bf16[1024,512]{1,0:T(8,128)(2,1)S(1)} %get-tuple-element.64.refs_3_.k_ref, bf16[1024,1024]{1,0:T(8,128)(2,1)S(1)} %copy-done.1, ...), custom_call_target="tpu_custom_call" | custom-call | flops 536870912 | bytes 4194304 | tf_op jit(solution)/shard_map/local_pass/pallas_call | solution.py:343
  20.8 2.0 %local_pass.5 = (f32[1024,256]{1,0:T(8,128)S(1)}, bf16[1024,256]{1,0:T(8,128)(2,1)S(1)}, f32[1024,256]{1,0:T(8,128)S(1)}) custom-call(f32[72,128]{1,0:T(8,128)S(1)} %get-tuple-element.70.rows_ref, bf16[1024,512]{1,0:T(8,128)(2,1)S(1)} %copy-done.2, bf16[1024,512]{1,0:T(8,128)(2,1)S(1)} %get-tuple-element.64.refs_3_.k_ref, bf16[1024,1024]{1,0:T(8,128)(2,1)S(1)} %copy-done.1, ...), custom_call_target="tpu_custom_call" | custom-call | flops 536870912 | bytes 4194304 | tf_op jit(solution)/shard_map/local_pass/pallas_call | solution.py:343
  22.7 0.8 %collective-permute-done.1.earlier_ref.first_ref = bf16[4,128,128]{2,1,0:T(8,128)(2,1)S(1)} collective-permute-done((bf16[4,128,128]{2,1,0:T(8,128)(2,1)S(1)}, bf16[4,128,128]{2,1,0:T(8,128)(2,1)S(1)}, u32[]{:S(2)}, u32[]{:S(2)}) %collective-permute-start.1) | collective-permute-done | bytes 131104 | tf_op jit(solution)/shard_map/ppermute | solution.py:504
  23.5 0.2 step.1
  23.7 3.7 %collective-permute-start.2 = (bf16[4,128,128]{2,1,0:T(8,128)(2,1)S(1)}, bf16[4,128,128]{2,1,0:T(8,128)(2,1)S(1)}, u32[]{:S(2)}, u32[]{:S(2)}) collective-permute-start(bf16[4,128,128]{2,1,0:T(8,128)(2,1)S(1)} %step.1), channel_id=1, source_target_pairs={{8,24},{12,28},{9,25},{13,29},{10,26},{14,30},{11,27},{15,31}} | collective-permute-start | bytes 393224 | tf_op jit(solution)/shard_map/ppermute | solution.py:509
  27.4 1.9 %collective-permute-start.4 = (bf16[4,128,128]{2,1,0:T(8,128)(2,1)S(1)}, bf16[4,128,128]{2,1,0:T(8,128)(2,1)S(1)}, u32[]{:S(2)}, u32[]{:S(2)}) collective-permute-start(bf16[4,128,128]{2,1,0:T(8,128)(2,1)S(1)} %step.1), channel_id=1, source_target_pairs={{8,16},{12,20},{9,17},{13,21},{10,18},{14,22},{11,19},{15,23}} | collective-permute-start | bytes 393224 | tf_op jit(solution)/shard_map/ppermute | solution.py:508
  29.3 1.9 %local_pass.6 = (f32[1024,256]{1,0:T(8,128)S(1)}, bf16[1024,256]{1,0:T(8,128)(2,1)S(1)}, f32[1024,256]{1,0:T(8,128)S(1)}) custom-call(f32[72,128]{1,0:T(8,128)S(1)} %get-tuple-element.84.rows_ref, bf16[1024,512]{1,0:T(8,128)(2,1)S(1)} %copy-done.2, bf16[1024,512]{1,0:T(8,128)(2,1)S(1)} %get-tuple-element.64.refs_3_.k_ref, bf16[1024,1024]{1,0:T(8,128)(2,1)S(1)} %copy-done.1, ...), custom_call_target="tpu_custom_call" | custom-call | flops 536870912 | bytes 4194304 | tf_op jit(solution)/shard_map/local_pass/pallas_call | solution.py:343
  31.2 0.1 collective-permute-done.2.far_ref
  31.3 0.0 collective-permute-done.3.before_ref
  31.3 1.4 %collective-permute-done.4.near_ref = bf16[4,128,128]{2,1,0:T(8,128)(2,1)S(1)} collective-permute-done((bf16[4,128,128]{2,1,0:T(8,128)(2,1)S(1)}, bf16[4,128,128]{2,1,0:T(8,128)(2,1)S(1)}, u32[]{:S(2)}, u32[]{:S(2)}) %collective-permute-start.4) | collective-permute-done | bytes 131104 | tf_op jit(solution)/shard_map/ppermute | solution.py:508
  32.7 0.3 last.1
  33.0 1.1 %collective-permute-start.5 = (bf16[4,128,128]{2,1,0:T(8,128)(2,1)S(1)}, bf16[4,128,128]{2,1,0:T(8,128)(2,1)S(1)}, u32[]{:S(2)}, u32[]{:S(2)}) collective-permute-start(bf16[4,128,128]{2,1,0:T(8,128)(2,1)S(1)} %get-tuple-element.92), channel_id=1, source_target_pairs={{0,4},{4,0},{8,12},{12,8},{16,20},{20,16},{24,28},{28,24},{1,5},{5... | collective-permute-start | bytes 393224 | tf_op jit(solution)/shard_map/ppermute | solution.py:513
  34.1 0.0 copy-start
  34.1 1.9 %local_pass.7 = (f32[1024,256]{1,0:T(8,128)S(1)}, bf16[1024,256]{1,0:T(8,128)(2,1)S(1)}, f32[1024,256]{1,0:T(8,128)S(1)}) custom-call(f32[72,128]{1,0:T(8,128)S(1)} %get-tuple-element.84.rows_ref, bf16[1024,512]{1,0:T(8,128)(2,1)S(1)} %copy-done.2, bf16[1024,512]{1,0:T(8,128)(2,1)S(1)} %get-tuple-element.64.refs_3_.k_ref, bf16[1024,1024]{1,0:T(8,128)(2,1)S(1)} %copy-done.1, ...), custom_call_target="tpu_custom_call" | custom-call | flops 536870912 | bytes 4194304 | tf_op jit(solution)/shard_map/local_pass/pallas_call | solution.py:343
  36.0 2.0 %collective-permute-done.5.refs_12_ = bf16[4,128,128]{2,1,0:T(8,128)(2,1)S(1)} collective-permute-done((bf16[4,128,128]{2,1,0:T(8,128)(2,1)S(1)}, bf16[4,128,128]{2,1,0:T(8,128)(2,1)S(1)}, u32[]{:S(2)}, u32[]{:S(2)}) %collective-permute-start.5) | collective-permute-done | bytes 131104 | tf_op jit(solution)/shard_map/ppermute | solution.py:513
  38.0 0.0 copy-done
  38.1 1.6 %finish_pass.4 = (bf16[256,1024]{1,0:T(8,128)(2,1)S(1)}, bf16[256,1024]{1,0:T(8,128)(2,1)S(1)}) custom-call(f32[1024,256]{1,0:T(8,128)S(1)} %get-tuple-element.76.refs_0_, f32[1024,256]{1,0:T(8,128)S(1)} %get-tuple-element.81.refs_1_, f32[1024,256]{1,0:T(8,128)S(1)} %get-tuple-element.90.refs_2_, f32[1024,256]{1,0:T(8,128)S(1)} %get-tuple-element.96.refs_3_, ...), custom_call_target="tpu_custom_call" | custom-call | flops 256 | bytes 256 | tf_op jit(solution)/shard_map/finish_pass/pallas_call | solution.py:406
  39.6 0.1 collective-permute-start.6
  39.7 1.6 %finish_pass.5 = (bf16[256,1024]{1,0:T(8,128)(2,1)S(1)}, bf16[256,1024]{1,0:T(8,128)(2,1)S(1)}) custom-call(f32[1024,256]{1,0:T(8,128)S(1)} %get-tuple-element.76.refs_0_, f32[1024,256]{1,0:T(8,128)S(1)} %get-tuple-element.81.refs_1_, f32[1024,256]{1,0:T(8,128)S(1)} %get-tuple-element.90.refs_2_, f32[1024,256]{1,0:T(8,128)S(1)} %get-tuple-element.96.refs_3_, ...), custom_call_target="tpu_custom_call" | custom-call | flops 256 | bytes 256 | tf_op jit(solution)/shard_map/finish_pass/pallas_call | solution.py:406
  41.3 0.6 collective-permute-start.7
  41.9 1.6 %finish_pass.6 = (bf16[256,1024]{1,0:T(8,128)(2,1)S(1)}, bf16[256,1024]{1,0:T(8,128)(2,1)S(1)}) custom-call(f32[1024,256]{1,0:T(8,128)S(1)} %get-tuple-element.76.refs_0_, f32[1024,256]{1,0:T(8,128)S(1)} %get-tuple-element.81.refs_1_, f32[1024,256]{1,0:T(8,128)S(1)} %get-tuple-element.90.refs_2_, f32[1024,256]{1,0:T(8,128)S(1)} %get-tuple-element.96.refs_3_, ...), custom_call_target="tpu_custom_call" | custom-call | flops 256 | bytes 256 | tf_op jit(solution)/shard_map/finish_pass/pallas_call | solution.py:406
  43.5 1.6 %finish_pass.7 = (bf16[256,1024]{1,0:T(8,128)(2,1)S(1)}, bf16[256,1024]{1,0:T(8,128)(2,1)S(1)}) custom-call(f32[1024,256]{1,0:T(8,128)S(1)} %get-tuple-element.76.refs_0_, f32[1024,256]{1,0:T(8,128)S(1)} %get-tuple-element.81.refs_1_, f32[1024,256]{1,0:T(8,128)S(1)} %get-tuple-element.90.refs_2_, f32[1024,256]{1,0:T(8,128)S(1)} %get-tuple-element.96.refs_3_, ...), custom_call_target="tpu_custom_call" | custom-call | flops 256 | bytes 256 | tf_op jit(solution)/shard_map/finish_pass/pallas_call | solution.py:406
  45.1 0.2 collective-permute-start.8
  45.2 0.4 collective-permute-start.9
  45.6 0.0 collective-permute-done.6
  45.6 0.2 convert_add_fusion.3.refs_0_
  45.8 1.6 %collective-permute-start.10 = (bf16[256,512]{1,0:T(8,128)(2,1)S(1)}, bf16[256,512]{1,0:T(8,128)(2,1)S(1)}, u32[]{:S(2)}, u32[]{:S(2)}) collective-permute-start(bf16[256,512]{1,0:T(8,128)(2,1)S(1)} %slice.31), channel_id=1, source_target_pairs={{0,2},{1,3},{2,0},{3,1},{4,6},{5,7},{6,4},{7,5},{8,10},{9,11},{10,... | collective-permute-start | bytes 786440 | tf_op jit(solution)/shard_map/ppermute | solution.py:612
  47.4 0.0 collective-permute-done.7
  47.4 0.2 convert_add_fusion.2.refs_1_
  47.6 0.6 collective-permute-start.11
  48.2 0.0 collective-permute-done.8
  48.2 0.2 convert_add_fusion.1.refs_2_
  48.4 1.6 %collective-permute-start.12 = (bf16[256,512]{1,0:T(8,128)(2,1)S(1)}, bf16[256,512]{1,0:T(8,128)(2,1)S(1)}, u32[]{:S(2)}, u32[]{:S(2)}) collective-permute-start(bf16[256,512]{1,0:T(8,128)(2,1)S(1)} %slice.29), channel_id=1, source_target_pairs={{0,2},{1,3},{2,0},{3,1},{4,6},{5,7},{6,4},{7,5},{8,10},{9,11},{10,... | collective-permute-start | bytes 786440 | tf_op jit(solution)/shard_map/ppermute | solution.py:612
  50.0 0.0 collective-permute-done.9
  50.0 0.2 convert_add_fusion.refs_3_
  50.2 0.6 collective-permute-start.13
  50.8 4.2 %collective-permute-done.10.refs_4_ = bf16[256,512]{1,0:T(8,128)(2,1)S(1)} collective-permute-done((bf16[256,512]{1,0:T(8,128)(2,1)S(1)}, bf16[256,512]{1,0:T(8,128)(2,1)S(1)}, u32[]{:S(2)}, u32[]{:S(2)}) %collective-permute-start.10) | collective-permute-done | bytes 262176 | tf_op jit(solution)/shard_map/ppermute | solution.py:612
  55.1 5.6 %collective-permute-done.11.refs_5_ = bf16[256,512]{1,0:T(8,128)(2,1)S(1)} collective-permute-done((bf16[256,512]{1,0:T(8,128)(2,1)S(1)}, bf16[256,512]{1,0:T(8,128)(2,1)S(1)}, u32[]{:S(2)}, u32[]{:S(2)}) %collective-permute-start.11) | collective-permute-done | bytes 262176 | tf_op jit(solution)/shard_map/ppermute | solution.py:612
  60.7 5.6 %collective-permute-done.12.refs_6_ = bf16[256,512]{1,0:T(8,128)(2,1)S(1)} collective-permute-done((bf16[256,512]{1,0:T(8,128)(2,1)S(1)}, bf16[256,512]{1,0:T(8,128)(2,1)S(1)}, u32[]{:S(2)}, u32[]{:S(2)}) %collective-permute-start.12) | collective-permute-done | bytes 262176 | tf_op jit(solution)/shard_map/ppermute | solution.py:612
  66.3 4.8 %collective-permute-done.13.refs_7_ = bf16[256,512]{1,0:T(8,128)(2,1)S(1)} collective-permute-done((bf16[256,512]{1,0:T(8,128)(2,1)S(1)}, bf16[256,512]{1,0:T(8,128)(2,1)S(1)}, u32[]{:S(2)}, u32[]{:S(2)}) %collective-permute-start.13) | collective-permute-done | bytes 262176 | tf_op jit(solution)/shard_map/ppermute | solution.py:612
  71.1 1.1 %assemble.1 = bf16[1024,512]{1,0:T(8,128)(2,1)} custom-call(f32[256,1024]{1,0:T(8,128)S(1)} %convert_add_fusion.3.refs_0_, f32[256,1024]{1,0:T(8,128)S(1)} %convert_add_fusion.2.refs_1_, f32[256,1024]{1,0:T(8,128)S(1)} %convert_add_fusion.1.refs_2_, f32[256,1024]{1,0:T(8,128)S(1)} %convert_add_fusion.refs_3_, ...), custom_call_target="tpu_custom_call" | custom-call | tf_op jit(solution)/shard_map/assemble/pallas_call | solution.py:538
  (4 shorter events, 0.1 us)
Async XLA Ops:
  8.3 8.1 %collective-permute-start = (bf16[4,128,256]{2,1,0:T(8,128)(2,1)S(1)}, bf16[4,128,256]{2,1,0:T(8,128)(2,1)S(1)}, u32[]{:S(2)}, u32[]{:S(2)}) collective-permute-start(bf16[4,128,256]{2,1,0:T(8,128)(2,1)S(1)} %get-tuple-element.68), channel_id=1, source_target_pairs={{0,4},{4,0},{8,12},{12,8},{16,20},{20,16},{24,28},{28,24},{1,5},{5... | collective-permute-start | bytes 786440 | tf_op jit(solution)/shard_map/ppermute | solution.py:574
  9.8 9.0 %copy-start.1 = (bf16[1024,1024]{1,0:T(8,128)(2,1)S(1)}, bf16[1024,1024]{1,0:T(8,128)(2,1)}, u32[]{:S(2)}) copy-start(bf16[1024,1024]{1,0:T(8,128)(2,1)} %gate_ref.7) | copy-start | bytes 6291460
  9.8 9.0 %copy-start.2 = (bf16[1024,512]{1,0:T(8,128)(2,1)S(1)}, bf16[1024,512]{1,0:T(8,128)(2,1)}, u32[]{:S(2)}) copy-start(bf16[1024,512]{1,0:T(8,128)(2,1)} %q_ref.7) | copy-start | bytes 3145732
  9.8 9.0 %copy-start.3 = (f32[128]{0:T(128)S(1)}, f32[128]{0:T(128)}, u32[]{:S(2)}) copy-start(f32[128]{0:T(128)} %param.16) | copy-start | bytes 1540
  16.6 6.9 %collective-permute-start.1 = (bf16[4,128,128]{2,1,0:T(8,128)(2,1)S(1)}, bf16[4,128,128]{2,1,0:T(8,128)(2,1)S(1)}, u32[]{:S(2)}, u32[]{:S(2)}) collective-permute-start(bf16[4,128,128]{2,1,0:T(8,128)(2,1)S(1)} %get-tuple-element.69), channel_id=1, source_target_pairs={{0,8},{4,12},{1,9},{5,13},{2,10},{6,14},{3,11},{7,15}} | collective-permute-start | bytes 393224 | tf_op jit(solution)/shard_map/ppermute | solution.py:504
  17.9 13.4 %collective-permute-start.3 = (bf16[4,128,256]{2,1,0:T(8,128)(2,1)S(1)}, bf16[4,128,256]{2,1,0:T(8,128)(2,1)S(1)}, u32[]{:S(2)}, u32[]{:S(2)}) collective-permute-start(bf16[4,128,256]{2,1,0:T(8,128)(2,1)S(1)} %get-tuple-element.82.later_ref), channel_id=1, source_target_pairs={{16,24},{20,28},{17,25},{21,29},{18,26},{22,30},{19,27},{23,31}} | collective-permute-start | bytes 786440 | tf_op jit(solution)/shard_map/ppermute | solution.py:505
  23.7 7.6 %collective-permute-start.2 = (bf16[4,128,128]{2,1,0:T(8,128)(2,1)S(1)}, bf16[4,128,128]{2,1,0:T(8,128)(2,1)S(1)}, u32[]{:S(2)}, u32[]{:S(2)}) collective-permute-start(bf16[4,128,128]{2,1,0:T(8,128)(2,1)S(1)} %step.1), channel_id=1, source_target_pairs={{8,24},{12,28},{9,25},{13,29},{10,26},{14,30},{11,27},{15,31}} | collective-permute-start | bytes 393224 | tf_op jit(solution)/shard_map/ppermute | solution.py:509
  27.4 5.3 %collective-permute-start.4 = (bf16[4,128,128]{2,1,0:T(8,128)(2,1)S(1)}, bf16[4,128,128]{2,1,0:T(8,128)(2,1)S(1)}, u32[]{:S(2)}, u32[]{:S(2)}) collective-permute-start(bf16[4,128,128]{2,1,0:T(8,128)(2,1)S(1)} %step.1), channel_id=1, source_target_pairs={{8,16},{12,20},{9,17},{13,21},{10,18},{14,22},{11,19},{15,23}} | collective-permute-start | bytes 393224 | tf_op jit(solution)/shard_map/ppermute | solution.py:508
  33.0 5.0 %collective-permute-start.5 = (bf16[4,128,128]{2,1,0:T(8,128)(2,1)S(1)}, bf16[4,128,128]{2,1,0:T(8,128)(2,1)S(1)}, u32[]{:S(2)}, u32[]{:S(2)}) collective-permute-start(bf16[4,128,128]{2,1,0:T(8,128)(2,1)S(1)} %get-tuple-element.92), channel_id=1, source_target_pairs={{0,4},{4,0},{8,12},{12,8},{16,20},{20,16},{24,28},{28,24},{1,5},{5... | collective-permute-start | bytes 393224 | tf_op jit(solution)/shard_map/ppermute | solution.py:513
  34.1 3.9 %copy-start = (bf16[1024,2048]{1,0:T(8,128)(2,1)S(1)}, bf16[1024,2048]{1,0:T(8,128)(2,1)}, u32[]{:S(2)}) copy-start(bf16[1024,2048]{1,0:T(8,128)(2,1)} %refs_14_.7) | copy-start | bytes 12582916
  39.6 6.0 %collective-permute-start.6 = (bf16[256,1024]{1,0:T(8,128)(2,1)S(1)}, bf16[256,1024]{1,0:T(8,128)(2,1)S(1)}, u32[]{:S(2)}, u32[]{:S(2)}) collective-permute-start(bf16[256,1024]{1,0:T(8,128)(2,1)S(1)} %get-tuple-element.108), channel_id=1, source_target_pairs={{0,1},{1,0},{2,3},{3,2},{4,5},{5,4},{6,7},{7,6},{8,9},{9,8},{10,11... | collective-permute-start | bytes 1572872 | tf_op jit(solution)/shard_map/ppermute | solution.py:612
  41.3 6.1 %collective-permute-start.7 = (bf16[256,1024]{1,0:T(8,128)(2,1)S(1)}, bf16[256,1024]{1,0:T(8,128)(2,1)S(1)}, u32[]{:S(2)}, u32[]{:S(2)}) collective-permute-start(bf16[256,1024]{1,0:T(8,128)(2,1)S(1)} %get-tuple-element.110), channel_id=1, source_target_pairs={{0,1},{1,0},{2,3},{3,2},{4,5},{5,4},{6,7},{7,6},{8,9},{9,8},{10,11... | collective-permute-start | bytes 1572872 | tf_op jit(solution)/shard_map/ppermute | solution.py:612
  45.1 3.2 %collective-permute-start.8 = (bf16[256,1024]{1,0:T(8,128)(2,1)S(1)}, bf16[256,1024]{1,0:T(8,128)(2,1)S(1)}, u32[]{:S(2)}, u32[]{:S(2)}) collective-permute-start(bf16[256,1024]{1,0:T(8,128)(2,1)S(1)} %get-tuple-element.112), channel_id=1, source_target_pairs={{0,1},{1,0},{2,3},{3,2},{4,5},{5,4},{6,7},{7,6},{8,9},{9,8},{10,11... | collective-permute-start | bytes 1572872 | tf_op jit(solution)/shard_map/ppermute | solution.py:612
  45.2 4.8 %collective-permute-start.9 = (bf16[256,1024]{1,0:T(8,128)(2,1)S(1)}, bf16[256,1024]{1,0:T(8,128)(2,1)S(1)}, u32[]{:S(2)}, u32[]{:S(2)}) collective-permute-start(bf16[256,1024]{1,0:T(8,128)(2,1)S(1)} %get-tuple-element.114), channel_id=1, source_target_pairs={{0,1},{1,0},{2,3},{3,2},{4,5},{5,4},{6,7},{7,6},{8,9},{9,8},{10,11... | collective-permute-start | bytes 1572872 | tf_op jit(solution)/shard_map/ppermute | solution.py:612
  45.8 9.2 %collective-permute-start.10 = (bf16[256,512]{1,0:T(8,128)(2,1)S(1)}, bf16[256,512]{1,0:T(8,128)(2,1)S(1)}, u32[]{:S(2)}, u32[]{:S(2)}) collective-permute-start(bf16[256,512]{1,0:T(8,128)(2,1)S(1)} %slice.31), channel_id=1, source_target_pairs={{0,2},{1,3},{2,0},{3,1},{4,6},{5,7},{6,4},{7,5},{8,10},{9,11},{10,... | collective-permute-start | bytes 786440 | tf_op jit(solution)/shard_map/ppermute | solution.py:612
  47.6 13.0 %collective-permute-start.11 = (bf16[256,512]{1,0:T(8,128)(2,1)S(1)}, bf16[256,512]{1,0:T(8,128)(2,1)S(1)}, u32[]{:S(2)}, u32[]{:S(2)}) collective-permute-start(bf16[256,512]{1,0:T(8,128)(2,1)S(1)} %slice.30), channel_id=1, source_target_pairs={{0,2},{1,3},{2,0},{3,1},{4,6},{5,7},{6,4},{7,5},{8,10},{9,11},{10,... | collective-permute-start | bytes 786440 | tf_op jit(solution)/shard_map/ppermute | solution.py:612
  48.4 17.9 %collective-permute-start.12 = (bf16[256,512]{1,0:T(8,128)(2,1)S(1)}, bf16[256,512]{1,0:T(8,128)(2,1)S(1)}, u32[]{:S(2)}, u32[]{:S(2)}) collective-permute-start(bf16[256,512]{1,0:T(8,128)(2,1)S(1)} %slice.29), channel_id=1, source_target_pairs={{0,2},{1,3},{2,0},{3,1},{4,6},{5,7},{6,4},{7,5},{8,10},{9,11},{10,... | collective-permute-start | bytes 786440 | tf_op jit(solution)/shard_map/ppermute | solution.py:612
  50.2 20.8 %collective-permute-start.13 = (bf16[256,512]{1,0:T(8,128)(2,1)S(1)}, bf16[256,512]{1,0:T(8,128)(2,1)S(1)}, u32[]{:S(2)}, u32[]{:S(2)}) collective-permute-start(bf16[256,512]{1,0:T(8,128)(2,1)S(1)} %slice.28), channel_id=1, source_target_pairs={{0,2},{1,3},{2,0},{3,1},{4,6},{5,7},{6,4},{7,5},{8,10},{9,11},{10,... | collective-permute-start | bytes 786440 | tf_op jit(solution)/shard_map/ppermute | solution.py:612

commit v5 on v4

--- a/solution.py
+++ b/solution.py
@@ -93,30 +93,48 @@
 
 
 def shard_kernel(
-    part, parts, per_key, blocks, keys, *refs
+    part, parts, per_key, blocks, keys, devices, *refs
 ):
     if part == 0:
-        log_in, rate_in, start_in, k_in, v_in = refs[:5]
-        wu_ref, zc_ref, rows_ref, end_ref, log_ref, rate_ref, start_ref, k_ref, v_ref = refs[5:14]
+        log_in, rate_in, start_in, k_in, v_in, w_in = refs[:6]
+        wu_ref, zc_ref, rows_ref, end_ref, log_ref, rate_ref, start_ref, k_ref, v_ref = refs[6:15]
+        w_keep, w_give = refs[15:17]
     else:
         log_ref, rate_ref, start_ref, k_ref, v_ref, wu_ref, zc_ref, rows_ref, end_ref = refs[:9]
-    logs, rates, norms, kt, db, keep, state = refs[len(refs) - 7 :] if part else refs[14:21]
+    logs, rates, norms, kt, db, keep, state = refs[len(refs) - 7 :] if part else refs[17:24]
     mine = place_of(part, parts)
     small_copies, k_copies, v_copies = [], [], []
     if part == 0:
-        small_sems, k_sems, v_sems = refs[21:]
+        small_sems, k_sems, other_sems, v_sems, w_sems = refs[24:]
         for at, (ref, here) in enumerate(
             ((log_in, log_ref), (rate_in, rate_ref), (start_in, start_ref))
         ):
             small_copies.append(pltpu.make_async_copy(ref, here, small_sems.at[at]))
-        for copies, ref, here, sems in (
-            (k_copies, k_in, k_ref, k_sems),
-            (v_copies, v_in, v_ref, v_sems),
-        ):
+        width = keys * DK
+        for place, copies, sems in ((mine, k_copies, k_sems), (1 - mine, v_copies, other_sems)):
+            if parts == 1 and copies is v_copies:
+                continue
+            lanes = pl.ds(pl.multiple_of(place * width, width), width)
             for c in range(blocks):
-                span = slice(c * BLK, (c + 1) * BLK)
-                copies.append(pltpu.make_async_copy(ref.at[span], here.at[span], sems.at[c]))
-        for copy in small_copies + k_copies + v_copies:
+                at = (slice(c * BLK, (c + 1) * BLK), lanes)
+                copies.append(pltpu.make_async_copy(k_in.at[at], k_ref.at[at], sems.at[c]))
+        for c in range(blocks):
+            span = slice(c * BLK, (c + 1) * BLK)
+            v_copies.append(pltpu.make_async_copy(v_in.at[span], v_ref.at[span], v_sems.at[c]))
+        w_copies = []
+        order = halving_order(devices)
+        columns = w_in.shape[1] // devices
+        for at, place in enumerate(order):
+            first = pl.multiple_of((lax.axis_index("head") ^ place) * columns, columns)
+            to, slot = (w_keep, at) if at < devices // 2 else (w_give, at - devices // 2)
+            w_copies.append(
+                pltpu.make_async_copy(
+                    w_in.at[:, pl.ds(first, columns)],
+                    to.at[:, slot * columns : (slot + 1) * columns],
+                    w_sems.at[at],
+                )
+            )
+        for copy in small_copies + k_copies:
             copy.start()
         for copy in small_copies:
             copy.wait()
@@ -142,6 +160,11 @@
     inner = []
     for copy in k_copies:
         copy.wait()
+    for copy in v_copies:
+        copy.start()
+    if part == 0:
+        for copy in w_copies:
+            copy.start()
     for key in range(keys):
         for c in range(blocks):
             rows = k_ref[c * BLK : (c + 1) * BLK, key_lanes(key)]
@@ -234,6 +257,9 @@
             state[h, :, DV:] = g * now[:, DV:] - moved[:, DV:]
     for h in range(heads):
         end_ref[h] = state[h].astype(BF16)
+    if part == 0:
+        for copy in w_copies:
+            copy.wait()
 
 
 def vmem(shape, dtype):
@@ -248,7 +274,7 @@
     return pl.BlockSpec(memory_space=pltpu.VMEM)
 
 
-def shard_pass(part, parts, arrays, heads_here, per_key):
+def shard_pass(part, parts, arrays, heads_here, per_key, devices):
     tokens_here = arrays[3].shape[0]
     heads = heads_here // parts
     keys = heads // per_key
@@ -271,15 +297,16 @@
         pltpu.VMEM((heads, DK, wide), F32),
     ]
     if part == 0:
-        shapes += [vmem(a.shape, a.dtype) for a in arrays]
-        scratch += [pltpu.SemaphoreType.DMA((n,)) for n in (3, blocks, blocks)]
+        depth, wide = arrays[5].shape
+        shapes += [vmem(a.shape, a.dtype) for a in arrays[:5]] + [vmem((depth, wide // 2), BF16)] * 2
+        scratch += [pltpu.SemaphoreType.DMA((n,)) for n in (3, blocks, blocks, blocks, devices)]
         arrays = [in_hbm(a) for a in arrays]
         space = pltpu.HBM
     else:
         space = pltpu.VMEM
     outs = pl.pallas_call(
-        functools.partial(shard_kernel, part, parts, per_key, blocks, keys),
-        in_specs=[pl.BlockSpec(memory_space=space)] * 5,
+        functools.partial(shard_kernel, part, parts, per_key, blocks, keys, devices),
+        in_specs=[pl.BlockSpec(memory_space=space)] * len(arrays),
         out_specs=[in_vmem()] * len(shapes),
         out_shape=shapes,
         scratch_shapes=scratch,
@@ -357,37 +384,65 @@
     )(rows, queries, key_rows, out_gate, gain, wu, zc)
 
 
-def finish_kernel(row, per_key, parts, order, *refs):
-    me = lax.axis_index("head")
-    keys_here = (len(refs) - parts - 3) // 3
+def norm_kernel(row, per_key, parts, *refs):
+    keys_here = (len(refs) - parts - 1) // 3
     outs = refs[:keys_here]
     carries = refs[keys_here : 2 * keys_here]
     gates = refs[2 * keys_here : 3 * keys_here]
-    starts = refs[3 * keys_here : 3 * keys_here + parts]
-    weight_ref, send_ref, keep_ref = refs[3 * keys_here + parts :]
-    rows = slice(row, row + send_ref.shape[0])
+    starts, normed_ref = refs[3 * keys_here : -1], refs[-1]
+    rows = slice(row, row + normed_ref.shape[0])
     heads = keys_here * per_key // parts
-    normed = []
-    for part in range(parts):
-        pieces = []
-        for head in range(heads):
-            key, h = part * (keys_here // parts) + head // per_key, head % per_key
+    for key in range(keys_here):
+        for h in range(per_key):
+            head = key * per_key + h
             span = slice(h * DV, (h + 1) * DV)
-            seen = outs[key][rows, span] + dot(carries[key][rows, span], starts[part][head])
+            start = starts[head // heads][head % heads]
+            seen = outs[key][rows, span] + dot(carries[key][rows, span], start)
             spread = jnp.mean(seen * seen, axis=1, keepdims=True)
-            pieces.append((seen * lax.rsqrt(spread + EPS) * gates[key][rows, span]).astype(BF16))
-        normed.append(jnp.concatenate(pieces, axis=1))
-    columns = weight_ref.shape[1] // len(order)
-    sends = len(order) // 2
-    for at, place in enumerate(order):
-        first = pl.multiple_of((me ^ place) * columns, columns)
+            normed = seen * lax.rsqrt(spread + EPS) * gates[key][rows, span]
+            normed_ref[:, head * DV : (head + 1) * DV] = normed.astype(BF16)
+
+
+def norm_pass(row, rows, outs, carries, gates, starts, per_key):
+    arrays = (*outs, *carries, *gates, *starts)
+    return pl.pallas_call(
+        functools.partial(norm_kernel, row, per_key, len(starts)),
+        in_specs=[in_vmem()] * len(arrays),
+        out_specs=in_vmem(),
+        out_shape=vmem((rows, len(outs) * per_key * DV), BF16),
+        compiler_params=pltpu.CompilerParams(vmem_limit_bytes=8 * MIB),
+        cost_estimate=pl.CostEstimate(flops=rows, bytes_accessed=rows, transcendentals=0),
+        name="norm_pass",
+    )(*arrays)
+
+
+def project_kernel(parts, own_ref, got_ref, kept_ref, given_ref, keep_ref, send_ref):
+    heads_wide = own_ref.shape[1] // parts
+    width = keep_ref.shape[1]
+    for to, columns in ((send_ref, slice(width, 2 * width)), (keep_ref, slice(0, width))):
         total = None
-        for part in range(parts):
-            top = pl.multiple_of(place_of(part, parts) * (heads * DV), heads * DV)
-            term = dot(normed[part], weight_ref[pl.ds(top, heads * DV), pl.ds(first, columns)])
-            total = term if total is None else total + term
-        to, slot = (send_ref, at - sends) if at >= sends else (keep_ref, at)
-        to[:, slot * columns : (slot + 1) * columns] = total.astype(BF16)
+        for normed, weight in ((own_ref, kept_ref), (got_ref, given_ref)):
+            for part in range(parts):
+                top = pl.multiple_of(place_of(part, parts) * heads_wide, heads_wide)
+                term = dot(
+                    normed[:, part * heads_wide : (part + 1) * heads_wide],
+                    weight[pl.ds(top, heads_wide), columns],
+                )
+                total = term if total is None else total + term
+        to[...] = total.astype(to.dtype)
+
+
+def project(normed, got, weight_kept, weight_got, parts):
+    rows, width = normed.shape[0], weight_kept.shape[1] // 2
+    return pl.pallas_call(
+        functools.partial(project_kernel, parts),
+        in_specs=[in_vmem()] * 4,
+        out_specs=[in_vmem()] * 2,
+        out_shape=[vmem((rows, width), F32), vmem((rows, width), BF16)],
+        compiler_params=pltpu.CompilerParams(vmem_limit_bytes=8 * MIB),
+        cost_estimate=pl.CostEstimate(flops=rows, bytes_accessed=rows, transcendentals=0),
+        name="project",
+    )(normed, got, weight_kept, weight_got)
 
 
 def halving_order(size):
@@ -400,38 +455,18 @@
     return split(list(range(size)), 1)
 
 
-def finish_pass(row, rows, outs, carries, gates, starts, weight, per_key, devices):
-    keys_here = len(outs)
-    half = weight.shape[1] // 2
-    return pl.pallas_call(
-        functools.partial(
-            finish_kernel, row, per_key, len(starts), halving_order(devices)
-        ),
-        in_specs=[in_vmem()] * (3 * keys_here + len(starts) + 1),
-        out_specs=[in_vmem()] * 2,
-        out_shape=[vmem((rows, half), BF16)] * 2,
-        compiler_params=pltpu.CompilerParams(vmem_limit_bytes=16 * MIB),
-        cost_estimate=pl.CostEstimate(
-            flops=rows, bytes_accessed=rows, transcendentals=0
-        ),
-        name="finish_pass",
-    )(*outs, *carries, *gates, *starts, weight)
-
-
-def composed(later, earlier, h):
-    return dot(later[h, :, DV:], earlier[h]) + later[h, :, :DV].astype(F32)
-
-
-def pair_kernel(mine_ref, got_ref, both_ref, begun_ref):
+def composed(state, move, earlier):
+    return (dot(move, earlier) + state.astype(F32)).astype(BF16)
+
+
+def pair_kernel(mine_ref, got_ref, begun_ref, move_ref):
     odd = lax.rem(lax.axis_index("seq"), 2) == 1
 
     def join(second, first):
-        for h in range(both_ref.shape[0]):
+        for h in range(begun_ref.shape[0]):
             moved = dot(second[h, :, DV:], first[h])
-            begun = (moved[:, :DV] + second[h, :, :DV].astype(F32)).astype(BF16)
-            begun_ref[h] = begun
-            both_ref[h, :, :DV] = begun
-            both_ref[h, :, DV:] = moved[:, DV:].astype(BF16)
+            begun_ref[h] = (moved[:, :DV] + second[h, :, :DV].astype(F32)).astype(BF16)
+            move_ref[h] = moved[:, DV:].astype(BF16)
 
     @pl.when(odd)
     def _():
@@ -442,24 +477,24 @@
         join(got_ref, mine_ref)
 
 
-def step_kernel(later_ref, earlier_ref, out_ref):
+def step_kernel(state_ref, move_ref, earlier_ref, out_ref):
     for h in range(out_ref.shape[0]):
-        out_ref[h] = composed(later_ref, earlier_ref, h).astype(BF16)
-
-
-def last_kernel(
-    mine_ref, got_ref, first_ref, before_ref, near_ref, far_ref, own_ref, other_ref
-):
+        out_ref[h] = composed(state_ref[h], move_ref[h], earlier_ref[h])
+
+
+def last_kernel(mine_ref, got_ref, before_ref, turn_ref, near_ref, far_ref, own_ref, other_ref):
     odd = lax.rem(lax.axis_index("seq"), 2) == 1
     pair = lax.div(lax.axis_index("seq"), 2)
 
     def fill(first, here_ref, then_ref):
         for h in range(own_ref.shape[0]):
-            here = composed(before_ref, far_ref, h).astype(BF16)
+            before = before_ref[h]
+            here = composed(before, turn_ref[h], far_ref[h])
             here = jnp.where(pair == 2, near_ref[h], here)
-            here_ref[h] = jnp.where(pair == 1, first_ref[h], here)
+            here = jnp.where(pair == 1, before, here)
+            here_ref[h] = jnp.where(pair == 0, jnp.zeros_like(here), here)
         for h in range(own_ref.shape[0]):
-            then_ref[h] = composed(first, here_ref, h).astype(BF16)
+            then_ref[h] = composed(first[h, :, :DV], first[h, :, DV:], here_ref[h])
 
     @pl.when(odd)
     def _():
@@ -485,10 +520,9 @@
     )(*arrays)
 
 
-def step_call(later, earlier):
-    return small_call(
-        step_kernel, "step", [jax.ShapeDtypeStruct(earlier.shape, BF16)], later, earlier
-    )[0]
+def step_call(state, move, earlier):
+    shape = jax.ShapeDtypeStruct(earlier.shape, BF16)
+    return small_call(step_kernel, "step", [shape], state, move, earlier)[0]
 
 
 def route(axis, target):
@@ -498,17 +532,16 @@
 
 def exchanged(mine, got, work):
     state = jax.ShapeDtypeStruct(mine.shape[:2] + (DV,), BF16)
-    both, begun = small_call(
-        pair_kernel, "pair", [jax.ShapeDtypeStruct(mine.shape, BF16), state], mine, got
-    )
-    first = lax.ppermute(begun, "seq", [(0, 2), (1, 3)])
-    before = lax.ppermute(both, "seq", [(4, 6), (5, 7)])
-    first = work(work(first))
-    third = step_call(both, first)
-    near = lax.ppermute(third, "seq", [(2, 4), (3, 5)])
-    far = work(lax.ppermute(third, "seq", [(2, 6), (3, 7)]))
+    begun, move = small_call(pair_kernel, "pair", [state] * 2, mine, got)
+    before = lax.ppermute(begun, "seq", route("seq", lambda i: i ^ 2))
+    turn = lax.ppermute(move, "seq", route("seq", lambda i: i ^ 2))
+    before = work(before)
+    third = step_call(begun, move, before)
+    near = lax.ppermute(third, "seq", route("seq", lambda i: i ^ 6 if i // 2 in (1, 2) else i ^ 1))
+    far = lax.ppermute(third, "seq", route("seq", lambda i: i ^ 4 if i // 2 in (1, 3) else i ^ 1))
+    turn, far = work((turn, far)), work(far)
     own, other = small_call(
-        last_kernel, "last", [state] * 2, mine, got, first, before, near, far
+        last_kernel, "last", [state] * 2, mine, got, before, turn, near, far
     )
     return own, work(lax.ppermute(other, "seq", route("seq", lambda i: i ^ 1)))
 
@@ -518,7 +551,7 @@
     onward = route("seq", lambda i: i + 1 if i + 1 < size else None)
 
     def hop(step, state):
-        return lax.ppermute(step_call(end, state), "seq", onward)
+        return lax.ppermute(step_call(end[:, :, :DV], end[:, :, DV:], state), "seq", onward)
 
     return lax.fori_loop(0, size - 1, hop, jnp.zeros(end.shape[:2] + (DV,), BF16))
 
@@ -558,18 +591,18 @@
     keys = keys_here // parts
     starts = doc_start.reshape(tokens_here // BLK, BLK)
     gain = norm_gain.reshape(1, DV)
-    queries, out_gate, weight, gain = (
-        pltpu.with_memory_space_constraint(a, pltpu.VMEM)
-        for a in (queries, out_gate, out_weight, gain)
+    queries, out_gate, gain = (
+        pltpu.with_memory_space_constraint(a, pltpu.VMEM) for a in (queries, out_gate, gain)
     )
     shards, got = [], None
-    held = [log_gate, write_rate, starts, key_rows, value_rows]
+    held = [log_gate, write_rate, starts, key_rows, value_rows, out_weight]
     for part in range(parts):
-        shard, here = shard_pass(part, parts, held, heads_here, per_key)
+        shard, here = shard_pass(part, parts, held, heads_here, per_key, devices)
         shards.append(shard)
         if part == 0:
-            held = here
+            held, (weight_kept, weight_given) = here[:5], here[5:]
             nearby_keys = held[3]
+            weight_got = lax.ppermute(weight_given, "head", route("head", lambda i: i ^ 1))
             if parts == 2:
                 got = lax.ppermute(shard[3], "seq", route("seq", lambda i: i ^ 1))
     outs, carries, gates = [], [], []
@@ -579,6 +612,8 @@
         if at == keys_here:
             return coming
         wu, zc, rows, _ = shards[at // keys]
+        if isinstance(coming, tuple):
+            rows, coming = lax.optimization_barrier((rows, coming[0]))
         out, carry, gate = local_pass(
             at // keys, parts, at % keys, rows, queries, nearby_keys, out_gate, gain, wu, zc, per_key
         )
@@ -602,20 +637,23 @@
     unit = tokens_here // 16
     sizes = [unit * share for share in (4, 4, 4, 4)]
     firsts = [sum(sizes[:index]) for index in range(len(sizes))]
+    normed = [
+        norm_pass(first, rows, outs, carries, gates, states, per_key)
+        for first, rows in zip(firsts, sizes)
+    ]
     kept, arrived = [], []
-    for first, rows in zip(firsts, sizes):
-        send, keep = finish_pass(
-            first, rows, outs, carries, gates, states, weight, per_key, devices
-        )
-        bit = 1
+    for piece in normed:
+        across = lax.ppermute(piece, "head", route("head", lambda i: i ^ 1))
+        keep, send = project(piece, across, weight_kept, weight_got, parts)
+        bit = 2
         while bit < devices:
             got = lax.ppermute(send, "head", route("head", lambda i: i ^ bit))
             bit *= 2
             if bit < devices:
-                keep = keep.astype(F32) + got.astype(F32)
+                keep = keep + got.astype(F32)
                 width = keep.shape[1] // 2
                 send = keep[:, width:].astype(BF16)
-                keep = keep[:, :width] if 2 * bit < devices else keep
+                keep = keep[:, :width]
         kept.append(keep)
         arrived.append(got)
     return assemble(kept, arrived)

time: 73.3 us -> 68.4 us (0.933)
  waiting for transfers between devices: 24.8 us -> 22.2 us
  starting transfers between devices: 16 us -> 14 us
  Pallas kernels: 30.4 us -> 31.4 us
    ppermute x8 -> x4, waiting for transfers between devices: 20.2 us -> 17 us  [local(): got = lax.ppermute(send, 'head', route('head', lambda i: i ^ bit))]
    ppermute x8 -> x4, starting transfers between devices: 5.54 us -> 4.31 us  [local(): got = lax.ppermute(send, 'head', route('head', lambda i: i ^ bit))]
    ppermute x4 -> x9, starting transfers between devices: 7.76 us -> 6.55 us  [the longest x1 2.66 us: exchanged(): lax.ppermute(third, 'seq', route('seq', lambda i: i ^ 4 if i // 2 in (1,...]
    pallas_call x4 -> x8, Pallas kernels: 6.3 us -> 7.21 us  [the longest x4 5.08 us: project(): pl.pallas_call(functools.partial(project_kernel, parts), in_specs=[in_vme...]
    ppermute x4 -> x9, waiting for transfers between devices: 2.26 us -> 2.88 us  [the longest x1 2.37 us: exchanged(): before = lax.ppermute(begun, 'seq', route('seq', lambda i: i ^ 2))]
  transfers between devices with their start and end apart: 14 -> 15, of which waited for: 9 -> 8; matrix products, arithmetic and copies ran while one was open for 1% -> 0% of each run, Pallas kernels for 26% -> 33%
where the time goes in v5:
time: 68.4 us; the launch traced here: 67.8 us
  Pallas kernels  31.4 us (46%)
  waiting for transfers between devices  22.2 us (32%)
  starting transfers between devices  14 us (20%)
    ppermute x4, waiting for transfers between devices, local(): got = lax.ppermute(send, 'head', route('head', lambda i: i ^ bit))  17 us
    pallas_call x2, Pallas kernels, shard_pass(): pl.pallas_call(functools.partial(shard_kernel, part, parts, per_key, bloc...  14 us
    pallas_call x4, Pallas kernels, local_pass(): pl.pallas_call(functools.partial(local_kernel, part, parts, per_key, bloc...  7.95 us
    pallas_call x4, Pallas kernels, project(): pl.pallas_call(functools.partial(project_kernel, parts), in_specs=[in_vme...  5.08 us
    ppermute x4, starting transfers between devices, local(): got = lax.ppermute(send, 'head', route('head', lambda i: i ^ bit))  4.31 us
    ppermute x1, starting transfers between devices, exchanged(): lax.ppermute(third, 'seq', route('seq', lambda i: i ^ 4 if i // 2 in (1,...  2.66 us
    ppermute x1, waiting for transfers between devices, exchanged(): before = lax.ppermute(begun, 'seq', route('seq', lambda i: i ^ 2))  2.37 us
    pallas_call x4, Pallas kernels, norm_pass(): pl.pallas_call(functools.partial(norm_kernel, row, per_key, len(starts)),...  2.14 us
  transfers between devices with their start and end apart: 15, of which 8 were waited for; matrix products, arithmetic and copies ran while one was open for 0% of the time, Pallas kernels for 33%

profile of v5, /device:TPU:8, one launch (start us, length us, event | category | flops | bytes accessed | tf_op | source)
XLA Modules:
  0.0 67.8 jit_solution(18179355096113020706)
XLA Ops:
  0.0 7.6 %shard_pass.2 = (bf16[32,128,256]{2,1,0:T(8,128)(2,1)S(1)}, bf16[32,128,256]{2,1,0:T(8,128)(2,1)S(1)}, f32[72,128]{1,0:T(8,128)S(1)}, bf16[4,128,256]{2,1,0:T(8,...) custom-call(f32[8,1024]{1,0:T(8,128)} %refs_0_.1, ...), custom_call_target="tpu_custom_call" | custom-call | flops 2415919104 | bytes 4194304 | tf_op jit(solution)/shard_map/shard_pass/pallas_call | solution.py:307
  7.6 0.1 collective-permute-start.7
  7.7 1.5 %collective-permute-start = (bf16[4,128,256]{2,1,0:T(8,128)(2,1)S(1)}, bf16[4,128,256]{2,1,0:T(8,128)(2,1)S(1)}, u32[]{:S(2)}, u32[]{:S(2)}) collective-permute-start(bf16[4,128,256]{2,1,0:T(8,128)(2,1)S(1)} %get-tuple-element.72), channel_id=1, source_target_pairs={{0,4},{4,0},{8,12},{12,8},{16,20},{20,16},{24,28},{28,24},{1,5},{5... | collective-permute-start | bytes 786440 | tf_op jit(solution)/shard_map/ppermute | solution.py:607
  9.3 0.0 copy-start
  9.3 0.0 copy-start.1
  9.3 0.0 copy-start.2
  9.3 6.4 %shard_pass.3 = (bf16[32,128,256]{2,1,0:T(8,128)(2,1)S(1)}, bf16[32,128,256]{2,1,0:T(8,128)(2,1)S(1)}, f32[72,128]{1,0:T(8,128)S(1)}, bf16[4,128,256]{2,1,0:T(8,128)(2,1)S(1)}) custom-call(f32[8,1024]{1,0:T(8,128)S(1)} %get-tuple-element.65.refs_0_, f32[8,1024]{1,0:T(8,128)S(1)} %get-tuple-element.66.refs_1_, s32[8,128]{1,0:T(8,128)S(1)} %get-tuple-element.67.refs_2_, ...), custom_call_target="tpu_custom_call" | custom-call | flops 2415919104 | bytes 4194304 | tf_op jit(solution)/shard_map/shard_pass/pallas_call | solution.py:307
  15.6 0.8 %collective-permute-done.got_ref = bf16[4,128,256]{2,1,0:T(8,128)(2,1)S(1)} collective-permute-done((bf16[4,128,256]{2,1,0:T(8,128)(2,1)S(1)}, bf16[4,128,256]{2,1,0:T(8,128)(2,1)S(1)}, u32[]{:S(2)}, u32[]{:S(2)}) %collective-permute-start) | collective-permute-done | bytes 262176 | tf_op jit(solution)/shard_map/ppermute | solution.py:607
  16.4 0.4 pair.1
  16.8 0.2 collective-permute-start.1
  17.1 1.9 %collective-permute-start.2 = (bf16[4,128,128]{2,1,0:T(8,128)(2,1)S(1)}, bf16[4,128,128]{2,1,0:T(8,128)(2,1)S(1)}, u32[]{:S(2)}, u32[]{:S(2)}) collective-permute-start(bf16[4,128,128]{2,1,0:T(8,128)(2,1)S(1)} %get-tuple-element.81.move_ref), channel_id=1, source_target_pairs={{0,8},{4,12},{8,0},{12,4},{16,24},{20,28},{24,16},{28,20},{1,9},{5... | collective-permute-start | bytes 393224 | tf_op jit(solution)/shard_map/ppermute | solution.py:537
  18.9 0.0 copy-done
  18.9 0.0 copy-done.1
  18.9 0.0 copy-done.2
  18.9 2.0 %local_pass.4 = (f32[1024,256]{1,0:T(8,128)S(1)}, bf16[1024,256]{1,0:T(8,128)(2,1)S(1)}, f32[1024,256]{1,0:T(8,128)S(1)}) custom-call(f32[72,128]{1,0:T(8,128)S(1)} %get-tuple-element.83.rows_ref, bf16[1024,512]{1,0:T(8,128)(2,1)S(1)} %copy-done.1, bf16[1024,512]{1,0:T(8,128)(2,1)S(1)} %get-tuple-element.68.refs_3_.k_ref, bf16[1024,1024]{1,0:T(8,128)(2,1)S(1)} %copy-done, ...), custom_call_target="tpu_custom_call" | custom-call | flops 536870912 | bytes 4194304 | tf_op jit(solution)/shard_map/local_pass/pallas_call | solution.py:370
  20.9 2.4 %collective-permute-done.1.earlier_ref.before_ref = bf16[4,128,128]{2,1,0:T(8,128)(2,1)S(1)} collective-permute-done((bf16[4,128,128]{2,1,0:T(8,128)(2,1)S(1)}, bf16[4,128,128]{2,1,0:T(8,128)(2,1)S(1)}, u32[]{:S(2)}, u32[]{:S(2)}) %collective-permute-start.1) | collective-permute-done | bytes 131104 | tf_op jit(solution)/shard_map/ppermute | solution.py:536
  23.3 0.2 step.1
  23.5 2.7 %collective-permute-start.3 = (bf16[4,128,128]{2,1,0:T(8,128)(2,1)S(1)}, bf16[4,128,128]{2,1,0:T(8,128)(2,1)S(1)}, u32[]{:S(2)}, u32[]{:S(2)}) collective-permute-start(bf16[4,128,128]{2,1,0:T(8,128)(2,1)S(1)} %step.1), channel_id=1, source_target_pairs={{0,4},{4,0},{8,24},{12,28},{16,20},{20,16},{24,8},{28,12},{1,5},{5... | collective-permute-start | bytes 393224 | tf_op jit(solution)/shard_map/ppermute | solution.py:541
  26.1 0.5 collective-permute-start.4
  26.6 2.0 %local_pass.6 = (f32[1024,256]{1,0:T(8,128)S(1)}, bf16[1024,256]{1,0:T(8,128)(2,1)S(1)}, f32[1024,256]{1,0:T(8,128)S(1)}) custom-call(f32[72,128]{1,0:T(8,128)S(1)} %get-tuple-element.89.rows_ref, bf16[1024,512]{1,0:T(8,128)(2,1)S(1)} %copy-done.1, bf16[1024,512]{1,0:T(8,128)(2,1)S(1)} %get-tuple-element.68.refs_3_.k_ref, bf16[1024,1024]{1,0:T(8,128)(2,1)S(1)} %copy-done, ...), custom_call_target="tpu_custom_call" | custom-call | flops 536870912 | bytes 4194304 | tf_op jit(solution)/shard_map/local_pass/pallas_call | solution.py:370
  28.6 0.0 collective-permute-done.2.turn_ref
  28.6 2.0 %local_pass.5 = (f32[1024,256]{1,0:T(8,128)S(1)}, bf16[1024,256]{1,0:T(8,128)(2,1)S(1)}, f32[1024,256]{1,0:T(8,128)S(1)}) custom-call(f32[72,128]{1,0:T(8,128)S(1)} %get-tuple-element.83.rows_ref, bf16[1024,512]{1,0:T(8,128)(2,1)S(1)} %copy-done.1, bf16[1024,512]{1,0:T(8,128)(2,1)S(1)} %get-tuple-element.68.refs_3_.k_ref, bf16[1024,1024]{1,0:T(8,128)(2,1)S(1)} %copy-done, ...), custom_call_target="tpu_custom_call" | custom-call | flops 536870912 | bytes 4194304 | tf_op jit(solution)/shard_map/local_pass/pallas_call | solution.py:370
  30.6 0.0 collective-permute-done.3.far_ref
  30.6 0.5 collective-permute-done.4.near_ref
  31.1 0.6 last.1
  31.7 1.5 %collective-permute-start.5 = (bf16[4,128,128]{2,1,0:T(8,128)(2,1)S(1)}, bf16[4,128,128]{2,1,0:T(8,128)(2,1)S(1)}, u32[]{:S(2)}, u32[]{:S(2)}) collective-permute-start(bf16[4,128,128]{2,1,0:T(8,128)(2,1)S(1)} %get-tuple-element.98), channel_id=1, source_target_pairs={{0,4},{4,0},{8,12},{12,8},{16,20},{20,16},{24,28},{28,24},{1,5},{5... | collective-permute-start | bytes 393224 | tf_op jit(solution)/shard_map/ppermute | solution.py:546
  33.2 2.0 %local_pass.7 = (f32[1024,256]{1,0:T(8,128)S(1)}, bf16[1024,256]{1,0:T(8,128)(2,1)S(1)}, f32[1024,256]{1,0:T(8,128)S(1)}) custom-call(f32[72,128]{1,0:T(8,128)S(1)} %get-tuple-element.89.rows_ref, bf16[1024,512]{1,0:T(8,128)(2,1)S(1)} %copy-done.1, bf16[1024,512]{1,0:T(8,128)(2,1)S(1)} %get-tuple-element.68.refs_3_.k_ref, bf16[1024,1024]{1,0:T(8,128)(2,1)S(1)} %copy-done, ...), custom_call_target="tpu_custom_call" | custom-call | flops 536870912 | bytes 4194304 | tf_op jit(solution)/shard_map/local_pass/pallas_call | solution.py:370
  35.2 1.5 %collective-permute-done.5.refs_12_ = bf16[4,128,128]{2,1,0:T(8,128)(2,1)S(1)} collective-permute-done((bf16[4,128,128]{2,1,0:T(8,128)(2,1)S(1)}, bf16[4,128,128]{2,1,0:T(8,128)(2,1)S(1)}, u32[]{:S(2)}, u32[]{:S(2)}) %collective-permute-start.5) | collective-permute-done | bytes 131104 | tf_op jit(solution)/shard_map/ppermute | solution.py:546
  36.7 0.5 norm_pass.4.own_ref
  37.3 0.1 collective-permute-start.6
  37.4 0.5 norm_pass.5.own_ref
  37.9 0.6 collective-permute-start.8
  38.5 0.5 norm_pass.6.own_ref
  39.0 0.1 collective-permute-start.9
  39.1 0.5 norm_pass.7.own_ref
  39.6 0.6 collective-permute-start.10
  40.2 0.0 collective-permute-done.6.got_ref
  40.2 0.0 collective-permute-done.7.given_ref
  40.2 1.3 %project.4 = (f32[256,512]{1,0:T(8,128)S(1)}, bf16[256,512]{1,0:T(8,128)(2,1)S(1)}) custom-call(bf16[256,1024]{1,0:T(8,128)(2,1)S(1)} %norm_pass.4.own_ref, bf16[256,1024]{1,0:T(8,128)(2,1)S(1)} %collective-permute-done.6.got_ref, bf16[1024,1024]{1,0:T(8,128)(2,1)S(1)} %get-tuple-element.113.kept_ref, bf16[1024,1024]{1,0:T(8,128)(2,1)S(1)} %collective-permute-done.7.given_ref), custom_call_target="tpu_custom_call" | custom-call | flops 256 | bytes 256 | tf_op jit(solution)/shard_map/project/pallas_call | solution.py:437
  41.5 1.6 %collective-permute-start.11 = (bf16[256,512]{1,0:T(8,128)(2,1)S(1)}, bf16[256,512]{1,0:T(8,128)(2,1)S(1)}, u32[]{:S(2)}, u32[]{:S(2)}) collective-permute-start(bf16[256,512]{1,0:T(8,128)(2,1)S(1)} %get-tuple-element.119), channel_id=1, source_target_pairs={{0,2},{1,3},{2,0},{3,1},{4,6},{5,7},{6,4},{7,5},{8,10},{9,11},{10,... | collective-permute-start | bytes 786440 | tf_op jit(solution)/shard_map/ppermute | solution.py:650
  43.0 0.0 collective-permute-done.8.got_ref
  43.1 1.3 %project.5 = (f32[256,512]{1,0:T(8,128)S(1)}, bf16[256,512]{1,0:T(8,128)(2,1)S(1)}) custom-call(bf16[256,1024]{1,0:T(8,128)(2,1)S(1)} %norm_pass.5.own_ref, bf16[256,1024]{1,0:T(8,128)(2,1)S(1)} %collective-permute-done.8.got_ref, bf16[1024,1024]{1,0:T(8,128)(2,1)S(1)} %get-tuple-element.113.kept_ref, bf16[1024,1024]{1,0:T(8,128)(2,1)S(1)} %collective-permute-done.7.given_ref), custom_call_target="tpu_custom_call" | custom-call | flops 256 | bytes 256 | tf_op jit(solution)/shard_map/project/pallas_call | solution.py:437
  44.3 0.6 collective-permute-start.12
  44.9 0.0 collective-permute-done.9.got_ref
  44.9 1.3 %project.6 = (f32[256,512]{1,0:T(8,128)S(1)}, bf16[256,512]{1,0:T(8,128)(2,1)S(1)}) custom-call(bf16[256,1024]{1,0:T(8,128)(2,1)S(1)} %norm_pass.6.own_ref, bf16[256,1024]{1,0:T(8,128)(2,1)S(1)} %collective-permute-done.9.got_ref, bf16[1024,1024]{1,0:T(8,128)(2,1)S(1)} %get-tuple-element.113.kept_ref, bf16[1024,1024]{1,0:T(8,128)(2,1)S(1)} %collective-permute-done.7.given_ref), custom_call_target="tpu_custom_call" | custom-call | flops 256 | bytes 256 | tf_op jit(solution)/shard_map/project/pallas_call | solution.py:437
  46.2 1.6 %collective-permute-start.13 = (bf16[256,512]{1,0:T(8,128)(2,1)S(1)}, bf16[256,512]{1,0:T(8,128)(2,1)S(1)}, u32[]{:S(2)}, u32[]{:S(2)}) collective-permute-start(bf16[256,512]{1,0:T(8,128)(2,1)S(1)} %get-tuple-element.121), channel_id=1, source_target_pairs={{0,2},{1,3},{2,0},{3,1},{4,6},{5,7},{6,4},{7,5},{8,10},{9,11},{10,... | collective-permute-start | bytes 786440 | tf_op jit(solution)/shard_map/ppermute | solution.py:650
  47.8 0.0 collective-permute-done.10.got_ref
  47.8 1.3 %project.7 = (f32[256,512]{1,0:T(8,128)S(1)}, bf16[256,512]{1,0:T(8,128)(2,1)S(1)}) custom-call(bf16[256,1024]{1,0:T(8,128)(2,1)S(1)} %norm_pass.7.own_ref, bf16[256,1024]{1,0:T(8,128)(2,1)S(1)} %collective-permute-done.10.got_ref, bf16[1024,1024]{1,0:T(8,128)(2,1)S(1)} %get-tuple-element.113.kept_ref, bf16[1024,1024]{1,0:T(8,128)(2,1)S(1)} %collective-permute-done.7.given_ref), custom_call_target="tpu_custom_call" | custom-call | flops 256 | bytes 256 | tf_op jit(solution)/shard_map/project/pallas_call | solution.py:437
  49.0 0.6 collective-permute-start.14
  49.6 1.1 %collective-permute-done.11.refs_4_ = bf16[256,512]{1,0:T(8,128)(2,1)S(1)} collective-permute-done((bf16[256,512]{1,0:T(8,128)(2,1)S(1)}, bf16[256,512]{1,0:T(8,128)(2,1)S(1)}, u32[]{:S(2)}, u32[]{:S(2)}) %collective-permute-start.11) | collective-permute-done | bytes 262176 | tf_op jit(solution)/shard_map/ppermute | solution.py:650
  50.7 5.6 %collective-permute-done.12.refs_5_ = bf16[256,512]{1,0:T(8,128)(2,1)S(1)} collective-permute-done((bf16[256,512]{1,0:T(8,128)(2,1)S(1)}, bf16[256,512]{1,0:T(8,128)(2,1)S(1)}, u32[]{:S(2)}, u32[]{:S(2)}) %collective-permute-start.12) | collective-permute-done | bytes 262176 | tf_op jit(solution)/shard_map/ppermute | solution.py:650
  56.3 5.6 %collective-permute-done.13.refs_6_ = bf16[256,512]{1,0:T(8,128)(2,1)S(1)} collective-permute-done((bf16[256,512]{1,0:T(8,128)(2,1)S(1)}, bf16[256,512]{1,0:T(8,128)(2,1)S(1)}, u32[]{:S(2)}, u32[]{:S(2)}) %collective-permute-start.13) | collective-permute-done | bytes 262176 | tf_op jit(solution)/shard_map/ppermute | solution.py:650
  61.9 4.7 %collective-permute-done.14.refs_7_ = bf16[256,512]{1,0:T(8,128)(2,1)S(1)} collective-permute-done((bf16[256,512]{1,0:T(8,128)(2,1)S(1)}, bf16[256,512]{1,0:T(8,128)(2,1)S(1)}, u32[]{:S(2)}, u32[]{:S(2)}) %collective-permute-start.14) | collective-permute-done | bytes 262176 | tf_op jit(solution)/shard_map/ppermute | solution.py:650
  66.6 1.2 %assemble.1 = bf16[1024,512]{1,0:T(8,128)(2,1)} custom-call(f32[256,512]{1,0:T(8,128)S(1)} %get-tuple-element.115.refs_0_, f32[256,512]{1,0:T(8,128)S(1)} %get-tuple-element.116.refs_1_, f32[256,512]{1,0:T(8,128)S(1)} %get-tuple-element.117.refs_2_, f32[256,512]{1,0:T(8,128)S(1)} %get-tuple-element.118.refs_3_, ...), custom_call_target="tpu_custom_call" | custom-call | tf_op jit(solution)/shard_map/assemble/pallas_call | solution.py:571
Async XLA Ops:
  7.6 32.6 %collective-permute-start.7 = (bf16[1024,1024]{1,0:T(8,128)(2,1)S(1)}, bf16[1024,1024]{1,0:T(8,128)(2,1)S(1)}, u32[]{:S(2)}, u32[]{:S(2)}) collective-permute-start(bf16[1024,1024]{1,0:T(8,128)(2,1)S(1)} %get-tuple-element.114), channel_id=1, source_target_pairs={{0,1},{1,0},{2,3},{3,2},{4,5},{5,4},{6,7},{7,6},{8,9},{9,8},{10,11... | collective-permute-start | bytes 6291464 | tf_op jit(solution)/shard_map/ppermute | solution.py:605
  7.7 8.7 %collective-permute-start = (bf16[4,128,256]{2,1,0:T(8,128)(2,1)S(1)}, bf16[4,128,256]{2,1,0:T(8,128)(2,1)S(1)}, u32[]{:S(2)}, u32[]{:S(2)}) collective-permute-start(bf16[4,128,256]{2,1,0:T(8,128)(2,1)S(1)} %get-tuple-element.72), channel_id=1, source_target_pairs={{0,4},{4,0},{8,12},{12,8},{16,20},{20,16},{24,28},{28,24},{1,5},{5... | collective-permute-start | bytes 786440 | tf_op jit(solution)/shard_map/ppermute | solution.py:607
  9.3 9.7 %copy-start = (bf16[1024,1024]{1,0:T(8,128)(2,1)S(1)}, bf16[1024,1024]{1,0:T(8,128)(2,1)}, u32[]{:S(2)}) copy-start(bf16[1024,1024]{1,0:T(8,128)(2,1)} %gate_ref.7) | copy-start | bytes 6291460
  9.3 9.7 %copy-start.1 = (bf16[1024,512]{1,0:T(8,128)(2,1)S(1)}, bf16[1024,512]{1,0:T(8,128)(2,1)}, u32[]{:S(2)}) copy-start(bf16[1024,512]{1,0:T(8,128)(2,1)} %q_ref.7) | copy-start | bytes 3145732
  9.3 9.7 %copy-start.2 = (f32[128]{0:T(128)S(1)}, f32[128]{0:T(128)}, u32[]{:S(2)}) copy-start(f32[128]{0:T(128)} %param.16) | copy-start | bytes 1540
  16.8 6.5 %collective-permute-start.1 = (bf16[4,128,128]{2,1,0:T(8,128)(2,1)S(1)}, bf16[4,128,128]{2,1,0:T(8,128)(2,1)S(1)}, u32[]{:S(2)}, u32[]{:S(2)}) collective-permute-start(bf16[4,128,128]{2,1,0:T(8,128)(2,1)S(1)} %get-tuple-element.73.state_ref), channel_id=1, source_target_pairs={{0,8},{4,12},{8,0},{12,4},{16,24},{20,28},{24,16},{28,20},{1,9},{5... | collective-permute-start | bytes 393224 | tf_op jit(solution)/shard_map/ppermute | solution.py:536
  17.1 11.5 %collective-permute-start.2 = (bf16[4,128,128]{2,1,0:T(8,128)(2,1)S(1)}, bf16[4,128,128]{2,1,0:T(8,128)(2,1)S(1)}, u32[]{:S(2)}, u32[]{:S(2)}) collective-permute-start(bf16[4,128,128]{2,1,0:T(8,128)(2,1)S(1)} %get-tuple-element.81.move_ref), channel_id=1, source_target_pairs={{0,8},{4,12},{8,0},{12,4},{16,24},{20,28},{24,16},{28,20},{1,9},{5... | collective-permute-start | bytes 393224 | tf_op jit(solution)/shard_map/ppermute | solution.py:537
  23.5 7.1 %collective-permute-start.3 = (bf16[4,128,128]{2,1,0:T(8,128)(2,1)S(1)}, bf16[4,128,128]{2,1,0:T(8,128)(2,1)S(1)}, u32[]{:S(2)}, u32[]{:S(2)}) collective-permute-start(bf16[4,128,128]{2,1,0:T(8,128)(2,1)S(1)} %step.1), channel_id=1, source_target_pairs={{0,4},{4,0},{8,24},{12,28},{16,20},{20,16},{24,8},{28,12},{1,5},{5... | collective-permute-start | bytes 393224 | tf_op jit(solution)/shard_map/ppermute | solution.py:541
  26.1 5.0 %collective-permute-start.4 = (bf16[4,128,128]{2,1,0:T(8,128)(2,1)S(1)}, bf16[4,128,128]{2,1,0:T(8,128)(2,1)S(1)}, u32[]{:S(2)}, u32[]{:S(2)}) collective-permute-start(bf16[4,128,128]{2,1,0:T(8,128)(2,1)S(1)} %step.1), channel_id=1, source_target_pairs={{0,4},{4,0},{8,16},{12,20},{16,8},{20,12},{24,28},{28,24},{1,5},{5... | collective-permute-start | bytes 393224 | tf_op jit(solution)/shard_map/ppermute | solution.py:540
  31.7 5.0 %collective-permute-start.5 = (bf16[4,128,128]{2,1,0:T(8,128)(2,1)S(1)}, bf16[4,128,128]{2,1,0:T(8,128)(2,1)S(1)}, u32[]{:S(2)}, u32[]{:S(2)}) collective-permute-start(bf16[4,128,128]{2,1,0:T(8,128)(2,1)S(1)} %get-tuple-element.98), channel_id=1, source_target_pairs={{0,4},{4,0},{8,12},{12,8},{16,20},{20,16},{24,28},{28,24},{1,5},{5... | collective-permute-start | bytes 393224 | tf_op jit(solution)/shard_map/ppermute | solution.py:546
  37.3 2.9 %collective-permute-start.6 = (bf16[256,1024]{1,0:T(8,128)(2,1)S(1)}, bf16[256,1024]{1,0:T(8,128)(2,1)S(1)}, u32[]{:S(2)}, u32[]{:S(2)}) collective-permute-start(bf16[256,1024]{1,0:T(8,128)(2,1)S(1)} %norm_pass.4.own_ref), channel_id=1, source_target_pairs={{0,1},{1,0},{2,3},{3,2},{4,5},{5,4},{6,7},{7,6},{8,9},{9,8},{10,11... | collective-permute-start | bytes 1572872 | tf_op jit(solution)/shard_map/ppermute | solution.py:646
  37.9 5.2 %collective-permute-start.8 = (bf16[256,1024]{1,0:T(8,128)(2,1)S(1)}, bf16[256,1024]{1,0:T(8,128)(2,1)S(1)}, u32[]{:S(2)}, u32[]{:S(2)}) collective-permute-start(bf16[256,1024]{1,0:T(8,128)(2,1)S(1)} %norm_pass.5.own_ref), channel_id=1, source_target_pairs={{0,1},{1,0},{2,3},{3,2},{4,5},{5,4},{6,7},{7,6},{8,9},{9,8},{10,11... | collective-permute-start | bytes 1572872 | tf_op jit(solution)/shard_map/ppermute | solution.py:646
  39.0 5.9 %collective-permute-start.9 = (bf16[256,1024]{1,0:T(8,128)(2,1)S(1)}, bf16[256,1024]{1,0:T(8,128)(2,1)S(1)}, u32[]{:S(2)}, u32[]{:S(2)}) collective-permute-start(bf16[256,1024]{1,0:T(8,128)(2,1)S(1)} %norm_pass.6.own_ref), channel_id=1, source_target_pairs={{0,1},{1,0},{2,3},{3,2},{4,5},{5,4},{6,7},{7,6},{8,9},{9,8},{10,11... | collective-permute-start | bytes 1572872 | tf_op jit(solution)/shard_map/ppermute | solution.py:646
  39.6 8.2 %collective-permute-start.10 = (bf16[256,1024]{1,0:T(8,128)(2,1)S(1)}, bf16[256,1024]{1,0:T(8,128)(2,1)S(1)}, u32[]{:S(2)}, u32[]{:S(2)}) collective-permute-start(bf16[256,1024]{1,0:T(8,128)(2,1)S(1)} %norm_pass.7.own_ref), channel_id=1, source_target_pairs={{0,1},{1,0},{2,3},{3,2},{4,5},{5,4},{6,7},{7,6},{8,9},{9,8},{10,11... | collective-permute-start | bytes 1572872 | tf_op jit(solution)/shard_map/ppermute | solution.py:646
  41.5 9.2 %collective-permute-start.11 = (bf16[256,512]{1,0:T(8,128)(2,1)S(1)}, bf16[256,512]{1,0:T(8,128)(2,1)S(1)}, u32[]{:S(2)}, u32[]{:S(2)}) collective-permute-start(bf16[256,512]{1,0:T(8,128)(2,1)S(1)} %get-tuple-element.119), channel_id=1, source_target_pairs={{0,2},{1,3},{2,0},{3,1},{4,6},{5,7},{6,4},{7,5},{8,10},{9,11},{10,... | collective-permute-start | bytes 786440 | tf_op jit(solution)/shard_map/ppermute | solution.py:650
  44.3 12.0 %collective-permute-start.12 = (bf16[256,512]{1,0:T(8,128)(2,1)S(1)}, bf16[256,512]{1,0:T(8,128)(2,1)S(1)}, u32[]{:S(2)}, u32[]{:S(2)}) collective-permute-start(bf16[256,512]{1,0:T(8,128)(2,1)S(1)} %get-tuple-element.120), channel_id=1, source_target_pairs={{0,2},{1,3},{2,0},{3,1},{4,6},{5,7},{6,4},{7,5},{8,10},{9,11},{10,... | collective-permute-start | bytes 786440 | tf_op jit(solution)/shard_map/ppermute | solution.py:650
  46.2 15.7 %collective-permute-start.13 = (bf16[256,512]{1,0:T(8,128)(2,1)S(1)}, bf16[256,512]{1,0:T(8,128)(2,1)S(1)}, u32[]{:S(2)}, u32[]{:S(2)}) collective-permute-start(bf16[256,512]{1,0:T(8,128)(2,1)S(1)} %get-tuple-element.121), channel_id=1, source_target_pairs={{0,2},{1,3},{2,0},{3,1},{4,6},{5,7},{6,4},{7,5},{8,10},{9,11},{10,... | collective-permute-start | bytes 786440 | tf_op jit(solution)/shard_map/ppermute | solution.py:650
  49.0 17.6 %collective-permute-start.14 = (bf16[256,512]{1,0:T(8,128)(2,1)S(1)}, bf16[256,512]{1,0:T(8,128)(2,1)S(1)}, u32[]{:S(2)}, u32[]{:S(2)}) collective-permute-start(bf16[256,512]{1,0:T(8,128)(2,1)S(1)} %get-tuple-element.122), channel_id=1, source_target_pairs={{0,2},{1,3},{2,0},{3,1},{4,6},{5,7},{6,4},{7,5},{8,10},{9,11},{10,... | collective-permute-start | bytes 786440 | tf_op jit(solution)/shard_map/ppermute | solution.py:650

commit v6 on v5

--- a/solution.py
+++ b/solution.py
@@ -534,8 +534,8 @@
     state = jax.ShapeDtypeStruct(mine.shape[:2] + (DV,), BF16)
     begun, move = small_call(pair_kernel, "pair", [state] * 2, mine, got)
     before = lax.ppermute(begun, "seq", route("seq", lambda i: i ^ 2))
+    before, move = work([before, move])
     turn = lax.ppermute(move, "seq", route("seq", lambda i: i ^ 2))
-    before = work(before)
     third = step_call(begun, move, before)
     near = lax.ppermute(third, "seq", route("seq", lambda i: i ^ 6 if i // 2 in (1, 2) else i ^ 1))
     far = lax.ppermute(third, "seq", route("seq", lambda i: i ^ 4 if i // 2 in (1, 3) else i ^ 1))
@@ -557,26 +557,38 @@
 
 
 def assemble_kernel(pieces, *refs):
-    kept, got, out_ref = refs[:pieces], refs[pieces : 2 * pieces], refs[2 * pieces]
+    kept, got, out_ref = refs[:pieces], refs[pieces : 2 * pieces], refs[-1]
     row = 0
     for keep_ref, got_ref in zip(kept, got):
-        rows, columns = got_ref.shape
-        total = keep_ref[:, :columns].astype(F32) + got_ref[...].astype(F32)
-        out_ref[row : row + rows, :] = total.astype(BF16)
+        rows = got_ref.shape[0]
+        out_ref[row : row + rows, :] = (keep_ref[...] + got_ref[...].astype(F32)).astype(BF16)
         row += rows
 
 
 def assemble(kept, got):
-    shape = (sum(piece.shape[0] for piece in got), got[0].shape[1])
+    ends = [sum(piece.shape[0] for piece in got[: at + 1]) for at in range(len(got))]
+    out = jax.ShapeDtypeStruct((ends[-1], got[0].shape[1]), BF16)
+    last = got[-1].shape[0]
+    params = pltpu.CompilerParams(vmem_limit_bytes=8 * MIB)
+    first = pl.pallas_call(
+        functools.partial(assemble_kernel, len(got) - 1),
+        grid=(1,),
+        in_specs=[in_vmem()] * (2 * len(got) - 2),
+        out_specs=pl.BlockSpec((ends[-2], out.shape[1]), lambda i: (0, 0)),
+        out_shape=out,
+        compiler_params=params,
+        name="assemble",
+    )(*kept[:-1], *got[:-1])
     return pl.pallas_call(
-        functools.partial(assemble_kernel, len(got)),
+        functools.partial(assemble_kernel, 1),
         grid=(1,),
-        in_specs=[in_vmem()] * (2 * len(got)),
-        out_specs=pl.BlockSpec(shape, lambda i: (0, 0)),
-        out_shape=jax.ShapeDtypeStruct(shape, BF16),
-        compiler_params=pltpu.CompilerParams(vmem_limit_bytes=8 * MIB),
-        name="assemble",
-    )(*kept, *got)
+        in_specs=[in_vmem()] * 2 + [pl.BlockSpec(memory_space=pl.ANY)],
+        out_specs=pl.BlockSpec((last, out.shape[1]), lambda i: (ends[-2] // last, 0)),
+        out_shape=out,
+        input_output_aliases={2: 0},
+        compiler_params=params,
+        name="assemble_last",
+    )(kept[-1], got[-1], first)
 
 
 def local(
@@ -617,7 +629,12 @@
         out, carry, gate = local_pass(
             at // keys, parts, at % keys, rows, queries, nearby_keys, out_gate, gain, wu, zc, per_key
         )
-        coming, out, carry, gate = lax.optimization_barrier((coming, out, carry, gate))
+        if isinstance(coming, list):
+            move, out = lax.optimization_barrier((coming[1], out))
+            before, out = lax.optimization_barrier((coming[0], out))
+            coming = [before, move]
+        else:
+            coming, out, carry, gate = lax.optimization_barrier((coming, out, carry, gate))
         outs.append(out)
         carries.append(carry)
         gates.append(gate)

time: 68.4 us -> 67.3 us (0.984)
  Pallas kernels: 31.4 us -> 32.1 us
  waiting for transfers between devices: 22.2 us -> 21.5 us
    ppermute x1, waiting for transfers between devices: 0.49 us -> 1.5 us  [exchanged(): lax.ppermute(third, 'seq', route('seq', lambda i: i ^ 6 if i // 2 in (1,...]
    ppermute x4, waiting for transfers between devices: 17 us -> 16 us  [local(): got = lax.ppermute(send, 'head', route('head', lambda i: i ^ bit))]
    ppermute x1, waiting for transfers between devices: 2.37 us -> 1.64 us  [exchanged(): before = lax.ppermute(begun, 'seq', route('seq', lambda i: i ^ 2))]
    pallas_call x1 -> x2, Pallas kernels: 1.16 us -> 1.76 us  [the longest x1 1.01 us: assemble(): pl.pallas_call(functools.partial(assemble_kernel, len(got) - 1), grid=(1,...]
  transfers between devices with their start and end apart: 15 -> 15, of which waited for: 8 -> 8; matrix products, arithmetic and copies ran while one was open for 0% -> 0% of each run, Pallas kernels for 33% -> 35%
where the time goes in v6:
time: 67.3 us; the launch traced here: 67.2 us
  Pallas kernels  32.1 us (48%)
  waiting for transfers between devices  21.5 us (32%)
  starting transfers between devices  13.5 us (20%)
    ppermute x4, waiting for transfers between devices, local(): got = lax.ppermute(send, 'head', route('head', lambda i: i ^ bit))  16 us
    pallas_call x2, Pallas kernels, shard_pass(): pl.pallas_call(functools.partial(shard_kernel, part, parts, per_key, bloc...  14 us
    pallas_call x4, Pallas kernels, local_pass(): pl.pallas_call(functools.partial(local_kernel, part, parts, per_key, bloc...  7.95 us
    pallas_call x4, Pallas kernels, project(): pl.pallas_call(functools.partial(project_kernel, parts), in_specs=[in_vme...  5.08 us
    ppermute x4, starting transfers between devices, local(): got = lax.ppermute(send, 'head', route('head', lambda i: i ^ bit))  4.31 us
    ppermute x1, starting transfers between devices, exchanged(): lax.ppermute(third, 'seq', route('seq', lambda i: i ^ 4 if i // 2 in (1,...  2.56 us
    pallas_call x4, Pallas kernels, norm_pass(): pl.pallas_call(functools.partial(norm_kernel, row, per_key, len(starts)),...  2.14 us
    ppermute x1, starting transfers between devices, exchanged(): turn = lax.ppermute(move, 'seq', route('seq', lambda i: i ^ 2))  1.92 us
  transfers between devices with their start and end apart: 15, of which 8 were waited for; matrix products, arithmetic and copies ran while one was open for 0% of the time, Pallas kernels for 35%

profile of v6, /device:TPU:8, one launch (start us, length us, event | category | flops | bytes accessed | tf_op | source)
XLA Modules:
  0.0 67.2 jit_solution(4784653346506727501)
XLA Ops:
  0.0 7.6 %shard_pass.2 = (bf16[32,128,256]{2,1,0:T(8,128)(2,1)S(1)}, bf16[32,128,256]{2,1,0:T(8,128)(2,1)S(1)}, f32[72,128]{1,0:T(8,128)S(1)}, bf16[4,128,256]{2,1,0:T(8,...) custom-call(f32[8,1024]{1,0:T(8,128)} %refs_0_.1, ...), custom_call_target="tpu_custom_call" | custom-call | flops 2415919104 | bytes 4194304 | tf_op jit(solution)/shard_map/shard_pass/pallas_call | solution.py:307
  7.6 0.1 collective-permute-start.7
  7.7 1.5 %collective-permute-start = (bf16[4,128,256]{2,1,0:T(8,128)(2,1)S(1)}, bf16[4,128,256]{2,1,0:T(8,128)(2,1)S(1)}, u32[]{:S(2)}, u32[]{:S(2)}) collective-permute-start(bf16[4,128,256]{2,1,0:T(8,128)(2,1)S(1)} %get-tuple-element.72), channel_id=1, source_target_pairs={{0,4},{4,0},{8,12},{12,8},{16,20},{20,16},{24,28},{28,24},{1,5},{5... | collective-permute-start | bytes 786440 | tf_op jit(solution)/shard_map/ppermute | solution.py:619
  9.3 0.0 copy-start
  9.3 0.0 copy-start.1
  9.3 0.0 copy-start.2
  9.3 6.4 %shard_pass.3 = (bf16[32,128,256]{2,1,0:T(8,128)(2,1)S(1)}, bf16[32,128,256]{2,1,0:T(8,128)(2,1)S(1)}, f32[72,128]{1,0:T(8,128)S(1)}, bf16[4,128,256]{2,1,0:T(8,128)(2,1)S(1)}) custom-call(f32[8,1024]{1,0:T(8,128)S(1)} %get-tuple-element.65.refs_0_, f32[8,1024]{1,0:T(8,128)S(1)} %get-tuple-element.66.refs_1_, s32[8,128]{1,0:T(8,128)S(1)} %get-tuple-element.67.refs_2_, ...), custom_call_target="tpu_custom_call" | custom-call | flops 2415919104 | bytes 4194304 | tf_op jit(solution)/shard_map/shard_pass/pallas_call | solution.py:307
  15.6 0.8 %collective-permute-done.got_ref = bf16[4,128,256]{2,1,0:T(8,128)(2,1)S(1)} collective-permute-done((bf16[4,128,256]{2,1,0:T(8,128)(2,1)S(1)}, bf16[4,128,256]{2,1,0:T(8,128)(2,1)S(1)}, u32[]{:S(2)}, u32[]{:S(2)}) %collective-permute-start) | collective-permute-done | bytes 262176 | tf_op jit(solution)/shard_map/ppermute | solution.py:619
  16.4 0.4 pair.1
  16.8 0.2 collective-permute-start.1
  17.1 0.0 copy-done
  17.1 0.0 copy-done.1
  17.1 0.0 copy-done.2
  17.1 2.0 %local_pass.4 = (f32[1024,256]{1,0:T(8,128)S(1)}, bf16[1024,256]{1,0:T(8,128)(2,1)S(1)}, f32[1024,256]{1,0:T(8,128)S(1)}) custom-call(f32[72,128]{1,0:T(8,128)S(1)} %get-tuple-element.83.rows_ref, bf16[1024,512]{1,0:T(8,128)(2,1)S(1)} %copy-done.1, bf16[1024,512]{1,0:T(8,128)(2,1)S(1)} %get-tuple-element.68.refs_3_.k_ref, bf16[1024,1024]{1,0:T(8,128)(2,1)S(1)} %copy-done, ...), custom_call_target="tpu_custom_call" | custom-call | flops 536870912 | bytes 4194304 | tf_op jit(solution)/shard_map/local_pass/pallas_call | solution.py:370
  19.1 1.9 %collective-permute-start.2 = (bf16[4,128,128]{2,1,0:T(8,128)(2,1)S(1)}, bf16[4,128,128]{2,1,0:T(8,128)(2,1)S(1)}, u32[]{:S(2)}, u32[]{:S(2)}) collective-permute-start(bf16[4,128,128]{2,1,0:T(8,128)(2,1)S(1)} %get-tuple-element.81.move_ref), channel_id=1, source_target_pairs={{0,8},{4,12},{8,0},{12,4},{16,24},{20,28},{24,16},{28,20},{1,9},{5... | collective-permute-start | bytes 393224 | tf_op jit(solution)/shard_map/ppermute | solution.py:538
  21.0 1.6 %collective-permute-done.1.earlier_ref.before_ref = bf16[4,128,128]{2,1,0:T(8,128)(2,1)S(1)} collective-permute-done((bf16[4,128,128]{2,1,0:T(8,128)(2,1)S(1)}, bf16[4,128,128]{2,1,0:T(8,128)(2,1)S(1)}, u32[]{:S(2)}, u32[]{:S(2)}) %collective-permute-start.1) | collective-permute-done | bytes 131104 | tf_op jit(solution)/shard_map/ppermute | solution.py:536
  22.6 0.2 step.1
  22.8 2.6 %collective-permute-start.3 = (bf16[4,128,128]{2,1,0:T(8,128)(2,1)S(1)}, bf16[4,128,128]{2,1,0:T(8,128)(2,1)S(1)}, u32[]{:S(2)}, u32[]{:S(2)}) collective-permute-start(bf16[4,128,128]{2,1,0:T(8,128)(2,1)S(1)} %step.1), channel_id=1, source_target_pairs={{0,4},{4,0},{8,24},{12,28},{16,20},{20,16},{24,8},{28,12},{1,5},{5... | collective-permute-start | bytes 393224 | tf_op jit(solution)/shard_map/ppermute | solution.py:541
  25.4 0.0 collective-permute-start.4
  25.4 2.0 %local_pass.6 = (f32[1024,256]{1,0:T(8,128)S(1)}, bf16[1024,256]{1,0:T(8,128)(2,1)S(1)}, f32[1024,256]{1,0:T(8,128)S(1)}) custom-call(f32[72,128]{1,0:T(8,128)S(1)} %get-tuple-element.89.rows_ref, bf16[1024,512]{1,0:T(8,128)(2,1)S(1)} %copy-done.1, bf16[1024,512]{1,0:T(8,128)(2,1)S(1)} %get-tuple-element.68.refs_3_.k_ref, bf16[1024,1024]{1,0:T(8,128)(2,1)S(1)} %copy-done, ...), custom_call_target="tpu_custom_call" | custom-call | flops 536870912 | bytes 4194304 | tf_op jit(solution)/shard_map/local_pass/pallas_call | solution.py:370
  27.4 0.0 collective-permute-done.2.turn_ref
  27.4 2.0 %local_pass.5 = (f32[1024,256]{1,0:T(8,128)S(1)}, bf16[1024,256]{1,0:T(8,128)(2,1)S(1)}, f32[1024,256]{1,0:T(8,128)S(1)}) custom-call(f32[72,128]{1,0:T(8,128)S(1)} %get-tuple-element.83.rows_ref, bf16[1024,512]{1,0:T(8,128)(2,1)S(1)} %copy-done.1, bf16[1024,512]{1,0:T(8,128)(2,1)S(1)} %get-tuple-element.68.refs_3_.k_ref, bf16[1024,1024]{1,0:T(8,128)(2,1)S(1)} %copy-done, ...), custom_call_target="tpu_custom_call" | custom-call | flops 536870912 | bytes 4194304 | tf_op jit(solution)/shard_map/local_pass/pallas_call | solution.py:370
  29.4 0.0 collective-permute-done.3.far_ref
  29.4 1.5 %collective-permute-done.4.near_ref = bf16[4,128,128]{2,1,0:T(8,128)(2,1)S(1)} collective-permute-done((bf16[4,128,128]{2,1,0:T(8,128)(2,1)S(1)}, bf16[4,128,128]{2,1,0:T(8,128)(2,1)S(1)}, u32[]{:S(2)}, u32[]{:S(2)}) %collective-permute-start.4) | collective-permute-done | bytes 131104 | tf_op jit(solution)/shard_map/ppermute | solution.py:540
  30.9 0.6 last.1
  31.5 1.5 %collective-permute-start.5 = (bf16[4,128,128]{2,1,0:T(8,128)(2,1)S(1)}, bf16[4,128,128]{2,1,0:T(8,128)(2,1)S(1)}, u32[]{:S(2)}, u32[]{:S(2)}) collective-permute-start(bf16[4,128,128]{2,1,0:T(8,128)(2,1)S(1)} %get-tuple-element.98), channel_id=1, source_target_pairs={{0,4},{4,0},{8,12},{12,8},{16,20},{20,16},{24,28},{28,24},{1,5},{5... | collective-permute-start | bytes 393224 | tf_op jit(solution)/shard_map/ppermute | solution.py:546
  33.0 2.0 %local_pass.7 = (f32[1024,256]{1,0:T(8,128)S(1)}, bf16[1024,256]{1,0:T(8,128)(2,1)S(1)}, f32[1024,256]{1,0:T(8,128)S(1)}) custom-call(f32[72,128]{1,0:T(8,128)S(1)} %get-tuple-element.89.rows_ref, bf16[1024,512]{1,0:T(8,128)(2,1)S(1)} %copy-done.1, bf16[1024,512]{1,0:T(8,128)(2,1)S(1)} %get-tuple-element.68.refs_3_.k_ref, bf16[1024,1024]{1,0:T(8,128)(2,1)S(1)} %copy-done, ...), custom_call_target="tpu_custom_call" | custom-call | flops 536870912 | bytes 4194304 | tf_op jit(solution)/shard_map/local_pass/pallas_call | solution.py:370
  35.0 1.5 %collective-permute-done.5.refs_12_ = bf16[4,128,128]{2,1,0:T(8,128)(2,1)S(1)} collective-permute-done((bf16[4,128,128]{2,1,0:T(8,128)(2,1)S(1)}, bf16[4,128,128]{2,1,0:T(8,128)(2,1)S(1)}, u32[]{:S(2)}, u32[]{:S(2)}) %collective-permute-start.5) | collective-permute-done | bytes 131104 | tf_op jit(solution)/shard_map/ppermute | solution.py:546
  36.5 0.5 norm_pass.5.own_ref
  37.1 0.1 collective-permute-start.9
  37.1 0.5 norm_pass.6.own_ref
  37.7 0.6 collective-permute-start.10
  38.2 0.5 norm_pass.7.own_ref
  38.8 0.1 collective-permute-start.11
  38.9 0.5 norm_pass.4.own_ref
  39.4 0.6 collective-permute-start.6
  40.0 0.0 collective-permute-done.9.got_ref
  40.0 0.0 collective-permute-done.7.given_ref
  40.0 1.3 %project.5 = (f32[256,512]{1,0:T(8,128)S(1)}, bf16[256,512]{1,0:T(8,128)(2,1)S(1)}) custom-call(bf16[256,1024]{1,0:T(8,128)(2,1)S(1)} %norm_pass.5.own_ref, bf16[256,1024]{1,0:T(8,128)(2,1)S(1)} %collective-permute-done.9.got_ref, bf16[1024,1024]{1,0:T(8,128)(2,1)S(1)} %get-tuple-element.113.kept_ref, bf16[1024,1024]{1,0:T(8,128)(2,1)S(1)} %collective-permute-done.7.given_ref), custom_call_target="tpu_custom_call" | custom-call | flops 256 | bytes 256 | tf_op jit(solution)/shard_map/project/pallas_call | solution.py:437
  41.2 1.6 %collective-permute-start.12 = (bf16[256,512]{1,0:T(8,128)(2,1)S(1)}, bf16[256,512]{1,0:T(8,128)(2,1)S(1)}, u32[]{:S(2)}, u32[]{:S(2)}) collective-permute-start(bf16[256,512]{1,0:T(8,128)(2,1)S(1)} %get-tuple-element.120), channel_id=1, source_target_pairs={{0,2},{1,3},{2,0},{3,1},{4,6},{5,7},{6,4},{7,5},{8,10},{9,11},{10,... | collective-permute-start | bytes 786440 | tf_op jit(solution)/shard_map/ppermute | solution.py:667
  42.8 0.0 collective-permute-done.10.got_ref
  42.8 1.3 %project.6 = (f32[256,512]{1,0:T(8,128)S(1)}, bf16[256,512]{1,0:T(8,128)(2,1)S(1)}) custom-call(bf16[256,1024]{1,0:T(8,128)(2,1)S(1)} %norm_pass.6.own_ref, bf16[256,1024]{1,0:T(8,128)(2,1)S(1)} %collective-permute-done.10.got_ref, bf16[1024,1024]{1,0:T(8,128)(2,1)S(1)} %get-tuple-element.113.kept_ref, bf16[1024,1024]{1,0:T(8,128)(2,1)S(1)} %collective-permute-done.7.given_ref), custom_call_target="tpu_custom_call" | custom-call | flops 256 | bytes 256 | tf_op jit(solution)/shard_map/project/pallas_call | solution.py:437
  44.1 0.6 collective-permute-start.13
  44.7 0.0 collective-permute-done.11.got_ref
  44.7 1.3 %project.7 = (f32[256,512]{1,0:T(8,128)S(1)}, bf16[256,512]{1,0:T(8,128)(2,1)S(1)}) custom-call(bf16[256,1024]{1,0:T(8,128)(2,1)S(1)} %norm_pass.7.own_ref, bf16[256,1024]{1,0:T(8,128)(2,1)S(1)} %collective-permute-done.11.got_ref, bf16[1024,1024]{1,0:T(8,128)(2,1)S(1)} %get-tuple-element.113.kept_ref, bf16[1024,1024]{1,0:T(8,128)(2,1)S(1)} %collective-permute-done.7.given_ref), custom_call_target="tpu_custom_call" | custom-call | flops 256 | bytes 256 | tf_op jit(solution)/shard_map/project/pallas_call | solution.py:437
  46.0 1.6 %collective-permute-start.14 = (bf16[256,512]{1,0:T(8,128)(2,1)S(1)}, bf16[256,512]{1,0:T(8,128)(2,1)S(1)}, u32[]{:S(2)}, u32[]{:S(2)}) collective-permute-start(bf16[256,512]{1,0:T(8,128)(2,1)S(1)} %get-tuple-element.122), channel_id=1, source_target_pairs={{0,2},{1,3},{2,0},{3,1},{4,6},{5,7},{6,4},{7,5},{8,10},{9,11},{10,... | collective-permute-start | bytes 786440 | tf_op jit(solution)/shard_map/ppermute | solution.py:667
  47.6 0.0 collective-permute-done.6.got_ref
  47.6 1.3 %project.4 = (f32[256,512]{1,0:T(8,128)S(1)}, bf16[256,512]{1,0:T(8,128)(2,1)S(1)}) custom-call(bf16[256,1024]{1,0:T(8,128)(2,1)S(1)} %norm_pass.4.own_ref, bf16[256,1024]{1,0:T(8,128)(2,1)S(1)} %collective-permute-done.6.got_ref, bf16[1024,1024]{1,0:T(8,128)(2,1)S(1)} %get-tuple-element.113.kept_ref, bf16[1024,1024]{1,0:T(8,128)(2,1)S(1)} %collective-permute-done.7.given_ref), custom_call_target="tpu_custom_call" | custom-call | flops 256 | bytes 256 | tf_op jit(solution)/shard_map/project/pallas_call | solution.py:437
  48.8 0.6 collective-permute-start.8
  49.4 1.1 %collective-permute-done.12.refs_3_ = bf16[256,512]{1,0:T(8,128)(2,1)S(1)} collective-permute-done((bf16[256,512]{1,0:T(8,128)(2,1)S(1)}, bf16[256,512]{1,0:T(8,128)(2,1)S(1)}, u32[]{:S(2)}, u32[]{:S(2)}) %collective-permute-start.12) | collective-permute-done | bytes 262176 | tf_op jit(solution)/shard_map/ppermute | solution.py:667
  50.5 5.6 %collective-permute-done.13.refs_4_ = bf16[256,512]{1,0:T(8,128)(2,1)S(1)} collective-permute-done((bf16[256,512]{1,0:T(8,128)(2,1)S(1)}, bf16[256,512]{1,0:T(8,128)(2,1)S(1)}, u32[]{:S(2)}, u32[]{:S(2)}) %collective-permute-start.13) | collective-permute-done | bytes 262176 | tf_op jit(solution)/shard_map/ppermute | solution.py:667
  56.1 5.6 %collective-permute-done.14.refs_5_ = bf16[256,512]{1,0:T(8,128)(2,1)S(1)} collective-permute-done((bf16[256,512]{1,0:T(8,128)(2,1)S(1)}, bf16[256,512]{1,0:T(8,128)(2,1)S(1)}, u32[]{:S(2)}, u32[]{:S(2)}) %collective-permute-start.14) | collective-permute-done | bytes 262176 | tf_op jit(solution)/shard_map/ppermute | solution.py:667
  61.7 1.0 %assemble.1.refs_2_ = bf16[1024,512]{1,0:T(8,128)(2,1)} custom-call(f32[256,512]{1,0:T(8,128)S(1)} %get-tuple-element.117.refs_0_, f32[256,512]{1,0:T(8,128)S(1)} %get-tuple-element.118.refs_1_, f32[256,512]{1,0:T(8,128)S(1)} %get-tuple-element.119.refs_2_, bf16[256,512]{1,0:T(8,128)(2,1)S(1)} %collective-permute-done.12.refs_3_, ...), custom_call_target="tpu_custom_call" | custom-call | tf_op jit(solution)/shard_map/assemble/pallas_call | solution.py:573
  62.7 3.7 %collective-permute-done.8.refs_1_ = bf16[256,512]{1,0:T(8,128)(2,1)S(1)} collective-permute-done((bf16[256,512]{1,0:T(8,128)(2,1)S(1)}, bf16[256,512]{1,0:T(8,128)(2,1)S(1)}, u32[]{:S(2)}, u32[]{:S(2)}) %collective-permute-start.8) | collective-permute-done | bytes 262176 | tf_op jit(solution)/shard_map/ppermute | solution.py:667
  66.4 0.7 %assemble_last.1 = bf16[1024,512]{1,0:T(8,128)(2,1)} custom-call(f32[256,512]{1,0:T(8,128)S(1)} %get-tuple-element.115.refs_0_, bf16[256,512]{1,0:T(8,128)(2,1)S(1)} %collective-permute-done.8.refs_1_, bf16[1024,512]{1,0:T(8,128)(2,1)} %assemble.1.refs_2_), custom_call_target="tpu_custom_call", output_to_operand_aliasing={{}: (2, {})} | custom-call | tf_op jit(solution)/shard_map/assemble_last/pallas_call | solution.py:582
Async XLA Ops:
  7.6 32.3 %collective-permute-start.7 = (bf16[1024,1024]{1,0:T(8,128)(2,1)S(1)}, bf16[1024,1024]{1,0:T(8,128)(2,1)S(1)}, u32[]{:S(2)}, u32[]{:S(2)}) collective-permute-start(bf16[1024,1024]{1,0:T(8,128)(2,1)S(1)} %get-tuple-element.114), channel_id=1, source_target_pairs={{0,1},{1,0},{2,3},{3,2},{4,5},{5,4},{6,7},{7,6},{8,9},{9,8},{10,11... | collective-permute-start | bytes 6291464 | tf_op jit(solution)/shard_map/ppermute | solution.py:617
  7.7 8.7 %collective-permute-start = (bf16[4,128,256]{2,1,0:T(8,128)(2,1)S(1)}, bf16[4,128,256]{2,1,0:T(8,128)(2,1)S(1)}, u32[]{:S(2)}, u32[]{:S(2)}) collective-permute-start(bf16[4,128,256]{2,1,0:T(8,128)(2,1)S(1)} %get-tuple-element.72), channel_id=1, source_target_pairs={{0,4},{4,0},{8,12},{12,8},{16,20},{20,16},{24,28},{28,24},{1,5},{5... | collective-permute-start | bytes 786440 | tf_op jit(solution)/shard_map/ppermute | solution.py:619
  9.3 7.8 %copy-start = (bf16[1024,1024]{1,0:T(8,128)(2,1)S(1)}, bf16[1024,1024]{1,0:T(8,128)(2,1)}, u32[]{:S(2)}) copy-start(bf16[1024,1024]{1,0:T(8,128)(2,1)} %gate_ref.7) | copy-start | bytes 6291460
  9.3 7.8 %copy-start.1 = (bf16[1024,512]{1,0:T(8,128)(2,1)S(1)}, bf16[1024,512]{1,0:T(8,128)(2,1)}, u32[]{:S(2)}) copy-start(bf16[1024,512]{1,0:T(8,128)(2,1)} %q_ref.7) | copy-start | bytes 3145732
  9.3 7.8 %copy-start.2 = (f32[128]{0:T(128)S(1)}, f32[128]{0:T(128)}, u32[]{:S(2)}) copy-start(f32[128]{0:T(128)} %param.16) | copy-start | bytes 1540
  16.8 5.8 %collective-permute-start.1 = (bf16[4,128,128]{2,1,0:T(8,128)(2,1)S(1)}, bf16[4,128,128]{2,1,0:T(8,128)(2,1)S(1)}, u32[]{:S(2)}, u32[]{:S(2)}) collective-permute-start(bf16[4,128,128]{2,1,0:T(8,128)(2,1)S(1)} %get-tuple-element.73.state_ref), channel_id=1, source_target_pairs={{0,8},{4,12},{8,0},{12,4},{16,24},{20,28},{24,16},{28,20},{1,9},{5... | collective-permute-start | bytes 393224 | tf_op jit(solution)/shard_map/ppermute | solution.py:536
  19.1 8.3 %collective-permute-start.2 = (bf16[4,128,128]{2,1,0:T(8,128)(2,1)S(1)}, bf16[4,128,128]{2,1,0:T(8,128)(2,1)S(1)}, u32[]{:S(2)}, u32[]{:S(2)}) collective-permute-start(bf16[4,128,128]{2,1,0:T(8,128)(2,1)S(1)} %get-tuple-element.81.move_ref), channel_id=1, source_target_pairs={{0,8},{4,12},{8,0},{12,4},{16,24},{20,28},{24,16},{28,20},{1,9},{5... | collective-permute-start | bytes 393224 | tf_op jit(solution)/shard_map/ppermute | solution.py:538
  22.8 6.6 %collective-permute-start.3 = (bf16[4,128,128]{2,1,0:T(8,128)(2,1)S(1)}, bf16[4,128,128]{2,1,0:T(8,128)(2,1)S(1)}, u32[]{:S(2)}, u32[]{:S(2)}) collective-permute-start(bf16[4,128,128]{2,1,0:T(8,128)(2,1)S(1)} %step.1), channel_id=1, source_target_pairs={{0,4},{4,0},{8,24},{12,28},{16,20},{20,16},{24,8},{28,12},{1,5},{5... | collective-permute-start | bytes 393224 | tf_op jit(solution)/shard_map/ppermute | solution.py:541
  25.4 5.5 %collective-permute-start.4 = (bf16[4,128,128]{2,1,0:T(8,128)(2,1)S(1)}, bf16[4,128,128]{2,1,0:T(8,128)(2,1)S(1)}, u32[]{:S(2)}, u32[]{:S(2)}) collective-permute-start(bf16[4,128,128]{2,1,0:T(8,128)(2,1)S(1)} %step.1), channel_id=1, source_target_pairs={{0,4},{4,0},{8,16},{12,20},{16,8},{20,12},{24,28},{28,24},{1,5},{5... | collective-permute-start | bytes 393224 | tf_op jit(solution)/shard_map/ppermute | solution.py:540
  31.5 5.0 %collective-permute-start.5 = (bf16[4,128,128]{2,1,0:T(8,128)(2,1)S(1)}, bf16[4,128,128]{2,1,0:T(8,128)(2,1)S(1)}, u32[]{:S(2)}, u32[]{:S(2)}) collective-permute-start(bf16[4,128,128]{2,1,0:T(8,128)(2,1)S(1)} %get-tuple-element.98), channel_id=1, source_target_pairs={{0,4},{4,0},{8,12},{12,8},{16,20},{20,16},{24,28},{28,24},{1,5},{5... | collective-permute-start | bytes 393224 | tf_op jit(solution)/shard_map/ppermute | solution.py:546
  37.1 2.9 %collective-permute-start.9 = (bf16[256,1024]{1,0:T(8,128)(2,1)S(1)}, bf16[256,1024]{1,0:T(8,128)(2,1)S(1)}, u32[]{:S(2)}, u32[]{:S(2)}) collective-permute-start(bf16[256,1024]{1,0:T(8,128)(2,1)S(1)} %norm_pass.5.own_ref), channel_id=1, source_target_pairs={{0,1},{1,0},{2,3},{3,2},{4,5},{5,4},{6,7},{7,6},{8,9},{9,8},{10,11... | collective-permute-start | bytes 1572872 | tf_op jit(solution)/shard_map/ppermute | solution.py:663
  37.7 5.2 %collective-permute-start.10 = (bf16[256,1024]{1,0:T(8,128)(2,1)S(1)}, bf16[256,1024]{1,0:T(8,128)(2,1)S(1)}, u32[]{:S(2)}, u32[]{:S(2)}) collective-permute-start(bf16[256,1024]{1,0:T(8,128)(2,1)S(1)} %norm_pass.6.own_ref), channel_id=1, source_target_pairs={{0,1},{1,0},{2,3},{3,2},{4,5},{5,4},{6,7},{7,6},{8,9},{9,8},{10,11... | collective-permute-start | bytes 1572872 | tf_op jit(solution)/shard_map/ppermute | solution.py:663
  38.8 5.9 %collective-permute-start.11 = (bf16[256,1024]{1,0:T(8,128)(2,1)S(1)}, bf16[256,1024]{1,0:T(8,128)(2,1)S(1)}, u32[]{:S(2)}, u32[]{:S(2)}) collective-permute-start(bf16[256,1024]{1,0:T(8,128)(2,1)S(1)} %norm_pass.7.own_ref), channel_id=1, source_target_pairs={{0,1},{1,0},{2,3},{3,2},{4,5},{5,4},{6,7},{7,6},{8,9},{9,8},{10,11... | collective-permute-start | bytes 1572872 | tf_op jit(solution)/shard_map/ppermute | solution.py:663
  39.4 8.2 %collective-permute-start.6 = (bf16[256,1024]{1,0:T(8,128)(2,1)S(1)}, bf16[256,1024]{1,0:T(8,128)(2,1)S(1)}, u32[]{:S(2)}, u32[]{:S(2)}) collective-permute-start(bf16[256,1024]{1,0:T(8,128)(2,1)S(1)} %norm_pass.4.own_ref), channel_id=1, source_target_pairs={{0,1},{1,0},{2,3},{3,2},{4,5},{5,4},{6,7},{7,6},{8,9},{9,8},{10,11... | collective-permute-start | bytes 1572872 | tf_op jit(solution)/shard_map/ppermute | solution.py:663
  41.2 9.2 %collective-permute-start.12 = (bf16[256,512]{1,0:T(8,128)(2,1)S(1)}, bf16[256,512]{1,0:T(8,128)(2,1)S(1)}, u32[]{:S(2)}, u32[]{:S(2)}) collective-permute-start(bf16[256,512]{1,0:T(8,128)(2,1)S(1)} %get-tuple-element.120), channel_id=1, source_target_pairs={{0,2},{1,3},{2,0},{3,1},{4,6},{5,7},{6,4},{7,5},{8,10},{9,11},{10,... | collective-permute-start | bytes 786440 | tf_op jit(solution)/shard_map/ppermute | solution.py:667
  44.1 12.0 %collective-permute-start.13 = (bf16[256,512]{1,0:T(8,128)(2,1)S(1)}, bf16[256,512]{1,0:T(8,128)(2,1)S(1)}, u32[]{:S(2)}, u32[]{:S(2)}) collective-permute-start(bf16[256,512]{1,0:T(8,128)(2,1)S(1)} %get-tuple-element.121), channel_id=1, source_target_pairs={{0,2},{1,3},{2,0},{3,1},{4,6},{5,7},{6,4},{7,5},{8,10},{9,11},{10,... | collective-permute-start | bytes 786440 | tf_op jit(solution)/shard_map/ppermute | solution.py:667
  46.0 15.7 %collective-permute-start.14 = (bf16[256,512]{1,0:T(8,128)(2,1)S(1)}, bf16[256,512]{1,0:T(8,128)(2,1)S(1)}, u32[]{:S(2)}, u32[]{:S(2)}) collective-permute-start(bf16[256,512]{1,0:T(8,128)(2,1)S(1)} %get-tuple-element.122), channel_id=1, source_target_pairs={{0,2},{1,3},{2,0},{3,1},{4,6},{5,7},{6,4},{7,5},{8,10},{9,11},{10,... | collective-permute-start | bytes 786440 | tf_op jit(solution)/shard_map/ppermute | solution.py:667
  48.8 17.6 %collective-permute-start.8 = (bf16[256,512]{1,0:T(8,128)(2,1)S(1)}, bf16[256,512]{1,0:T(8,128)(2,1)S(1)}, u32[]{:S(2)}, u32[]{:S(2)}) collective-permute-start(bf16[256,512]{1,0:T(8,128)(2,1)S(1)} %get-tuple-element.116), channel_id=1, source_target_pairs={{0,2},{1,3},{2,0},{3,1},{4,6},{5,7},{6,4},{7,5},{8,10},{9,11},{10,... | collective-permute-start | bytes 786440 | tf_op jit(solution)/shard_map/ppermute | solution.py:667

commit v7 on v6

--- a/solution.py
+++ b/solution.py
@@ -652,7 +652,7 @@
         states[0] = work(states[0])
 
     unit = tokens_here // 16
-    sizes = [unit * share for share in (4, 4, 4, 4)]
+    sizes = [unit * share for share in (5, 5, 4, 2)]
     firsts = [sum(sizes[:index]) for index in range(len(sizes))]
     normed = [
         norm_pass(first, rows, outs, carries, gates, states, per_key)

time: 67.3 us -> 67.6 us (level)
  transfers between devices with their start and end apart: 15 -> 15, of which waited for: 8 -> 6; matrix products, arithmetic and copies ran while one was open for 0% -> 0% of each run, Pallas kernels for 35% -> 35%
where the time goes in v7:
time: 67.6 us; the launch traced here: 67.4 us
  Pallas kernels  32.1 us (47%)
  waiting for transfers between devices  21.7 us (32%)
  starting transfers between devices  13.5 us (20%)
    ppermute x4, waiting for transfers between devices, local(): got = lax.ppermute(send, 'head', route('head', lambda i: i ^ bit))  16.2 us
    pallas_call x2, Pallas kernels, shard_pass(): pl.pallas_call(functools.partial(shard_kernel, part, parts, per_key, bloc...  14 us
    pallas_call x4, Pallas kernels, local_pass(): pl.pallas_call(functools.partial(local_kernel, part, parts, per_key, bloc...  7.95 us
    pallas_call x4, Pallas kernels, project(): pl.pallas_call(functools.partial(project_kernel, parts), in_specs=[in_vme...  5.1 us
    ppermute x4, starting transfers between devices, local(): got = lax.ppermute(send, 'head', route('head', lambda i: i ^ bit))  4.31 us
    ppermute x1, starting transfers between devices, exchanged(): lax.ppermute(third, 'seq', route('seq', lambda i: i ^ 4 if i // 2 in (1,...  2.56 us
    pallas_call x4, Pallas kernels, norm_pass(): pl.pallas_call(functools.partial(norm_kernel, row, per_key, len(starts)),...  2.18 us
    ppermute x1, starting transfers between devices, exchanged(): turn = lax.ppermute(move, 'seq', route('seq', lambda i: i ^ 2))  1.92 us
  transfers between devices with their start and end apart: 15, of which 6 were waited for; matrix products, arithmetic and copies ran while one was open for 0% of the time, Pallas kernels for 35%

profile of v7, /device:TPU:8, one launch (start us, length us, event | category | flops | bytes accessed | tf_op | source)
XLA Modules:
  0.0 67.4 jit_solution(8141975041096380994)
XLA Ops:
  0.0 7.6 %shard_pass.2 = (bf16[32,128,256]{2,1,0:T(8,128)(2,1)S(1)}, bf16[32,128,256]{2,1,0:T(8,128)(2,1)S(1)}, f32[72,128]{1,0:T(8,128)S(1)}, bf16[4,128,256]{2,1,0:T(8,...) custom-call(f32[8,1024]{1,0:T(8,128)} %refs_0_.1, ...), custom_call_target="tpu_custom_call" | custom-call | flops 2415919104 | bytes 4194304 | tf_op jit(solution)/shard_map/shard_pass/pallas_call | solution.py:307
  7.6 0.1 collective-permute-start.7
  7.7 1.5 %collective-permute-start = (bf16[4,128,256]{2,1,0:T(8,128)(2,1)S(1)}, bf16[4,128,256]{2,1,0:T(8,128)(2,1)S(1)}, u32[]{:S(2)}, u32[]{:S(2)}) collective-permute-start(bf16[4,128,256]{2,1,0:T(8,128)(2,1)S(1)} %get-tuple-element.72), channel_id=1, source_target_pairs={{0,4},{4,0},{8,12},{12,8},{16,20},{20,16},{24,28},{28,24},{1,5},{5... | collective-permute-start | bytes 786440 | tf_op jit(solution)/shard_map/ppermute | solution.py:619
  9.3 0.0 copy-start
  9.3 0.0 copy-start.1
  9.3 0.0 copy-start.2
  9.3 6.4 %shard_pass.3 = (bf16[32,128,256]{2,1,0:T(8,128)(2,1)S(1)}, bf16[32,128,256]{2,1,0:T(8,128)(2,1)S(1)}, f32[72,128]{1,0:T(8,128)S(1)}, bf16[4,128,256]{2,1,0:T(8,128)(2,1)S(1)}) custom-call(f32[8,1024]{1,0:T(8,128)S(1)} %get-tuple-element.65.refs_0_, f32[8,1024]{1,0:T(8,128)S(1)} %get-tuple-element.66.refs_1_, s32[8,128]{1,0:T(8,128)S(1)} %get-tuple-element.67.refs_2_, ...), custom_call_target="tpu_custom_call" | custom-call | flops 2415919104 | bytes 4194304 | tf_op jit(solution)/shard_map/shard_pass/pallas_call | solution.py:307
  15.6 0.8 %collective-permute-done.got_ref = bf16[4,128,256]{2,1,0:T(8,128)(2,1)S(1)} collective-permute-done((bf16[4,128,256]{2,1,0:T(8,128)(2,1)S(1)}, bf16[4,128,256]{2,1,0:T(8,128)(2,1)S(1)}, u32[]{:S(2)}, u32[]{:S(2)}) %collective-permute-start) | collective-permute-done | bytes 262176 | tf_op jit(solution)/shard_map/ppermute | solution.py:619
  16.4 0.4 pair.1
  16.8 0.2 collective-permute-start.1
  17.1 0.0 copy-done
  17.1 0.0 copy-done.1
  17.1 0.0 copy-done.2
  17.1 2.0 %local_pass.4 = (f32[1024,256]{1,0:T(8,128)S(1)}, bf16[1024,256]{1,0:T(8,128)(2,1)S(1)}, f32[1024,256]{1,0:T(8,128)S(1)}) custom-call(f32[72,128]{1,0:T(8,128)S(1)} %get-tuple-element.83.rows_ref, bf16[1024,512]{1,0:T(8,128)(2,1)S(1)} %copy-done.1, bf16[1024,512]{1,0:T(8,128)(2,1)S(1)} %get-tuple-element.68.refs_3_.k_ref, bf16[1024,1024]{1,0:T(8,128)(2,1)S(1)} %copy-done, ...), custom_call_target="tpu_custom_call" | custom-call | flops 536870912 | bytes 4194304 | tf_op jit(solution)/shard_map/local_pass/pallas_call | solution.py:370
  19.1 1.9 %collective-permute-start.2 = (bf16[4,128,128]{2,1,0:T(8,128)(2,1)S(1)}, bf16[4,128,128]{2,1,0:T(8,128)(2,1)S(1)}, u32[]{:S(2)}, u32[]{:S(2)}) collective-permute-start(bf16[4,128,128]{2,1,0:T(8,128)(2,1)S(1)} %get-tuple-element.81.move_ref), channel_id=1, source_target_pairs={{0,8},{4,12},{8,0},{12,4},{16,24},{20,28},{24,16},{28,20},{1,9},{5... | collective-permute-start | bytes 393224 | tf_op jit(solution)/shard_map/ppermute | solution.py:538
  21.0 1.6 %collective-permute-done.1.earlier_ref.before_ref = bf16[4,128,128]{2,1,0:T(8,128)(2,1)S(1)} collective-permute-done((bf16[4,128,128]{2,1,0:T(8,128)(2,1)S(1)}, bf16[4,128,128]{2,1,0:T(8,128)(2,1)S(1)}, u32[]{:S(2)}, u32[]{:S(2)}) %collective-permute-start.1) | collective-permute-done | bytes 131104 | tf_op jit(solution)/shard_map/ppermute | solution.py:536
  22.6 0.2 step.1
  22.8 2.6 %collective-permute-start.3 = (bf16[4,128,128]{2,1,0:T(8,128)(2,1)S(1)}, bf16[4,128,128]{2,1,0:T(8,128)(2,1)S(1)}, u32[]{:S(2)}, u32[]{:S(2)}) collective-permute-start(bf16[4,128,128]{2,1,0:T(8,128)(2,1)S(1)} %step.1), channel_id=1, source_target_pairs={{0,4},{4,0},{8,24},{12,28},{16,20},{20,16},{24,8},{28,12},{1,5},{5... | collective-permute-start | bytes 393224 | tf_op jit(solution)/shard_map/ppermute | solution.py:541
  25.4 0.0 collective-permute-start.4
  25.4 2.0 %local_pass.6 = (f32[1024,256]{1,0:T(8,128)S(1)}, bf16[1024,256]{1,0:T(8,128)(2,1)S(1)}, f32[1024,256]{1,0:T(8,128)S(1)}) custom-call(f32[72,128]{1,0:T(8,128)S(1)} %get-tuple-element.89.rows_ref, bf16[1024,512]{1,0:T(8,128)(2,1)S(1)} %copy-done.1, bf16[1024,512]{1,0:T(8,128)(2,1)S(1)} %get-tuple-element.68.refs_3_.k_ref, bf16[1024,1024]{1,0:T(8,128)(2,1)S(1)} %copy-done, ...), custom_call_target="tpu_custom_call" | custom-call | flops 536870912 | bytes 4194304 | tf_op jit(solution)/shard_map/local_pass/pallas_call | solution.py:370
  27.4 0.0 collective-permute-done.2.turn_ref
  27.4 2.0 %local_pass.5 = (f32[1024,256]{1,0:T(8,128)S(1)}, bf16[1024,256]{1,0:T(8,128)(2,1)S(1)}, f32[1024,256]{1,0:T(8,128)S(1)}) custom-call(f32[72,128]{1,0:T(8,128)S(1)} %get-tuple-element.83.rows_ref, bf16[1024,512]{1,0:T(8,128)(2,1)S(1)} %copy-done.1, bf16[1024,512]{1,0:T(8,128)(2,1)S(1)} %get-tuple-element.68.refs_3_.k_ref, bf16[1024,1024]{1,0:T(8,128)(2,1)S(1)} %copy-done, ...), custom_call_target="tpu_custom_call" | custom-call | flops 536870912 | bytes 4194304 | tf_op jit(solution)/shard_map/local_pass/pallas_call | solution.py:370
  29.4 0.0 collective-permute-done.3.far_ref
  29.4 1.5 %collective-permute-done.4.near_ref = bf16[4,128,128]{2,1,0:T(8,128)(2,1)S(1)} collective-permute-done((bf16[4,128,128]{2,1,0:T(8,128)(2,1)S(1)}, bf16[4,128,128]{2,1,0:T(8,128)(2,1)S(1)}, u32[]{:S(2)}, u32[]{:S(2)}) %collective-permute-start.4) | collective-permute-done | bytes 131104 | tf_op jit(solution)/shard_map/ppermute | solution.py:540
  30.9 0.6 last.1
  31.5 1.5 %collective-permute-start.5 = (bf16[4,128,128]{2,1,0:T(8,128)(2,1)S(1)}, bf16[4,128,128]{2,1,0:T(8,128)(2,1)S(1)}, u32[]{:S(2)}, u32[]{:S(2)}) collective-permute-start(bf16[4,128,128]{2,1,0:T(8,128)(2,1)S(1)} %get-tuple-element.98), channel_id=1, source_target_pairs={{0,4},{4,0},{8,12},{12,8},{16,20},{20,16},{24,28},{28,24},{1,5},{5... | collective-permute-start | bytes 393224 | tf_op jit(solution)/shard_map/ppermute | solution.py:546
  33.0 2.0 %local_pass.7 = (f32[1024,256]{1,0:T(8,128)S(1)}, bf16[1024,256]{1,0:T(8,128)(2,1)S(1)}, f32[1024,256]{1,0:T(8,128)S(1)}) custom-call(f32[72,128]{1,0:T(8,128)S(1)} %get-tuple-element.89.rows_ref, bf16[1024,512]{1,0:T(8,128)(2,1)S(1)} %copy-done.1, bf16[1024,512]{1,0:T(8,128)(2,1)S(1)} %get-tuple-element.68.refs_3_.k_ref, bf16[1024,1024]{1,0:T(8,128)(2,1)S(1)} %copy-done, ...), custom_call_target="tpu_custom_call" | custom-call | flops 536870912 | bytes 4194304 | tf_op jit(solution)/shard_map/local_pass/pallas_call | solution.py:370
  35.0 1.5 %collective-permute-done.5.refs_12_ = bf16[4,128,128]{2,1,0:T(8,128)(2,1)S(1)} collective-permute-done((bf16[4,128,128]{2,1,0:T(8,128)(2,1)S(1)}, bf16[4,128,128]{2,1,0:T(8,128)(2,1)S(1)}, u32[]{:S(2)}, u32[]{:S(2)}) %collective-permute-start.5) | collective-permute-done | bytes 131104 | tf_op jit(solution)/shard_map/ppermute | solution.py:546
  36.5 0.6 norm_pass.5.own_ref
  37.1 0.1 collective-permute-start.9
  37.2 0.6 norm_pass.6.own_ref
  37.9 0.6 collective-permute-start.10
  38.4 0.5 norm_pass.7.own_ref
  39.0 0.1 collective-permute-start.11
  39.1 0.4 norm_pass.4.own_ref
  39.4 0.6 collective-permute-start.6
  40.0 0.0 collective-permute-done.9.got_ref
  40.0 0.0 collective-permute-done.7.given_ref
  40.0 1.6 %project.5 = (f32[320,512]{1,0:T(8,128)S(1)}, bf16[320,512]{1,0:T(8,128)(2,1)S(1)}) custom-call(bf16[320,1024]{1,0:T(8,128)(2,1)S(1)} %norm_pass.5.own_ref, bf16[320,1024]{1,0:T(8,128)(2,1)S(1)} %collective-permute-done.9.got_ref, bf16[1024,1024]{1,0:T(8,128)(2,1)S(1)} %get-tuple-element.113.kept_ref, bf16[1024,1024]{1,0:T(8,128)(2,1)S(1)} %collective-permute-done.7.given_ref), custom_call_target="tpu_custom_call" | custom-call | flops 320 | bytes 320 | tf_op jit(solution)/shard_map/project/pallas_call | solution.py:437
  41.6 1.6 %collective-permute-start.12 = (bf16[320,512]{1,0:T(8,128)(2,1)S(1)}, bf16[320,512]{1,0:T(8,128)(2,1)S(1)}, u32[]{:S(2)}, u32[]{:S(2)}) collective-permute-start(bf16[320,512]{1,0:T(8,128)(2,1)S(1)} %get-tuple-element.120), channel_id=1, source_target_pairs={{0,2},{1,3},{2,0},{3,1},{4,6},{5,7},{6,4},{7,5},{8,10},{9,11},{10,... | collective-permute-start | bytes 983048 | tf_op jit(solution)/shard_map/ppermute | solution.py:667
  43.2 0.0 collective-permute-done.10.got_ref
  43.2 1.5 %project.6 = (f32[320,512]{1,0:T(8,128)S(1)}, bf16[320,512]{1,0:T(8,128)(2,1)S(1)}) custom-call(bf16[320,1024]{1,0:T(8,128)(2,1)S(1)} %norm_pass.6.own_ref, bf16[320,1024]{1,0:T(8,128)(2,1)S(1)} %collective-permute-done.10.got_ref, bf16[1024,1024]{1,0:T(8,128)(2,1)S(1)} %get-tuple-element.113.kept_ref, bf16[1024,1024]{1,0:T(8,128)(2,1)S(1)} %collective-permute-done.7.given_ref), custom_call_target="tpu_custom_call" | custom-call | flops 320 | bytes 320 | tf_op jit(solution)/shard_map/project/pallas_call | solution.py:437
  44.7 0.6 collective-permute-start.13
  45.3 0.0 collective-permute-done.11.got_ref
  45.3 1.3 %project.7 = (f32[256,512]{1,0:T(8,128)S(1)}, bf16[256,512]{1,0:T(8,128)(2,1)S(1)}) custom-call(bf16[256,1024]{1,0:T(8,128)(2,1)S(1)} %norm_pass.7.own_ref, bf16[256,1024]{1,0:T(8,128)(2,1)S(1)} %collective-permute-done.11.got_ref, bf16[1024,1024]{1,0:T(8,128)(2,1)S(1)} %get-tuple-element.113.kept_ref, bf16[1024,1024]{1,0:T(8,128)(2,1)S(1)} %collective-permute-done.7.given_ref), custom_call_target="tpu_custom_call" | custom-call | flops 256 | bytes 256 | tf_op jit(solution)/shard_map/project/pallas_call | solution.py:437
  46.6 1.6 %collective-permute-start.14 = (bf16[256,512]{1,0:T(8,128)(2,1)S(1)}, bf16[256,512]{1,0:T(8,128)(2,1)S(1)}, u32[]{:S(2)}, u32[]{:S(2)}) collective-permute-start(bf16[256,512]{1,0:T(8,128)(2,1)S(1)} %get-tuple-element.122), channel_id=1, source_target_pairs={{0,2},{1,3},{2,0},{3,1},{4,6},{5,7},{6,4},{7,5},{8,10},{9,11},{10,... | collective-permute-start | bytes 786440 | tf_op jit(solution)/shard_map/ppermute | solution.py:667
  48.1 0.0 collective-permute-done.6.got_ref
  48.2 0.7 %project.4 = (f32[128,512]{1,0:T(8,128)S(1)}, bf16[128,512]{1,0:T(8,128)(2,1)S(1)}) custom-call(bf16[128,1024]{1,0:T(8,128)(2,1)S(1)} %norm_pass.4.own_ref, bf16[128,1024]{1,0:T(8,128)(2,1)S(1)} %collective-permute-done.6.got_ref, bf16[1024,1024]{1,0:T(8,128)(2,1)S(1)} %get-tuple-element.113.kept_ref, bf16[1024,1024]{1,0:T(8,128)(2,1)S(1)} %collective-permute-done.7.given_ref), custom_call_target="tpu_custom_call" | custom-call | flops 128 | bytes 128 | tf_op jit(solution)/shard_map/project/pallas_call | solution.py:437
  48.9 0.6 collective-permute-start.8
  49.5 15.4 %collective-permute-done.14.refs_5_ = bf16[256,512]{1,0:T(8,128)(2,1)S(1)} collective-permute-done((bf16[256,512]{1,0:T(8,128)(2,1)S(1)}, bf16[256,512]{1,0:T(8,128)(2,1)S(1)}, u32[]{:S(2)}, u32[]{:S(2)}) %collective-permute-start.14) | collective-permute-done | bytes 262176 | tf_op jit(solution)/shard_map/ppermute | solution.py:667
  64.8 0.0 collective-permute-done.12.refs_3_
  64.9 0.0 collective-permute-done.13.refs_4_
  64.9 1.1 %assemble.1.refs_2_ = bf16[1024,512]{1,0:T(8,128)(2,1)} custom-call(f32[320,512]{1,0:T(8,128)S(1)} %get-tuple-element.117.refs_0_, f32[320,512]{1,0:T(8,128)S(1)} %get-tuple-element.118.refs_1_, f32[256,512]{1,0:T(8,128)S(1)} %get-tuple-element.119.refs_2_, bf16[320,512]{1,0:T(8,128)(2,1)S(1)} %collective-permute-done.12.refs_3_, ...), custom_call_target="tpu_custom_call" | custom-call | tf_op jit(solution)/shard_map/assemble/pallas_call | solution.py:573
  65.9 0.8 %collective-permute-done.8.refs_1_ = bf16[128,512]{1,0:T(8,128)(2,1)S(1)} collective-permute-done((bf16[128,512]{1,0:T(8,128)(2,1)S(1)}, bf16[128,512]{1,0:T(8,128)(2,1)S(1)}, u32[]{:S(2)}, u32[]{:S(2)}) %collective-permute-start.8) | collective-permute-done | bytes 131104 | tf_op jit(solution)/shard_map/ppermute | solution.py:667
  66.7 0.7 %assemble_last.1 = bf16[1024,512]{1,0:T(8,128)(2,1)} custom-call(f32[128,512]{1,0:T(8,128)S(1)} %get-tuple-element.115.refs_0_, bf16[128,512]{1,0:T(8,128)(2,1)S(1)} %collective-permute-done.8.refs_1_, bf16[1024,512]{1,0:T(8,128)(2,1)} %assemble.1.refs_2_), custom_call_target="tpu_custom_call", output_to_operand_aliasing={{}: (2, {})} | custom-call | tf_op jit(solution)/shard_map/assemble_last/pallas_call | solution.py:582
Async XLA Ops:
  7.6 32.4 %collective-permute-start.7 = (bf16[1024,1024]{1,0:T(8,128)(2,1)S(1)}, bf16[1024,1024]{1,0:T(8,128)(2,1)S(1)}, u32[]{:S(2)}, u32[]{:S(2)}) collective-permute-start(bf16[1024,1024]{1,0:T(8,128)(2,1)S(1)} %get-tuple-element.114), channel_id=1, source_target_pairs={{0,1},{1,0},{2,3},{3,2},{4,5},{5,4},{6,7},{7,6},{8,9},{9,8},{10,11... | collective-permute-start | bytes 6291464 | tf_op jit(solution)/shard_map/ppermute | solution.py:617
  7.7 8.7 %collective-permute-start = (bf16[4,128,256]{2,1,0:T(8,128)(2,1)S(1)}, bf16[4,128,256]{2,1,0:T(8,128)(2,1)S(1)}, u32[]{:S(2)}, u32[]{:S(2)}) collective-permute-start(bf16[4,128,256]{2,1,0:T(8,128)(2,1)S(1)} %get-tuple-element.72), channel_id=1, source_target_pairs={{0,4},{4,0},{8,12},{12,8},{16,20},{20,16},{24,28},{28,24},{1,5},{5... | collective-permute-start | bytes 786440 | tf_op jit(solution)/shard_map/ppermute | solution.py:619
  9.3 7.8 %copy-start = (bf16[1024,1024]{1,0:T(8,128)(2,1)S(1)}, bf16[1024,1024]{1,0:T(8,128)(2,1)}, u32[]{:S(2)}) copy-start(bf16[1024,1024]{1,0:T(8,128)(2,1)} %gate_ref.7) | copy-start | bytes 6291460
  9.3 7.8 %copy-start.1 = (bf16[1024,512]{1,0:T(8,128)(2,1)S(1)}, bf16[1024,512]{1,0:T(8,128)(2,1)}, u32[]{:S(2)}) copy-start(bf16[1024,512]{1,0:T(8,128)(2,1)} %q_ref.7) | copy-start | bytes 3145732
  9.3 7.8 %copy-start.2 = (f32[128]{0:T(128)S(1)}, f32[128]{0:T(128)}, u32[]{:S(2)}) copy-start(f32[128]{0:T(128)} %param.16) | copy-start | bytes 1540
  16.8 5.8 %collective-permute-start.1 = (bf16[4,128,128]{2,1,0:T(8,128)(2,1)S(1)}, bf16[4,128,128]{2,1,0:T(8,128)(2,1)S(1)}, u32[]{:S(2)}, u32[]{:S(2)}) collective-permute-start(bf16[4,128,128]{2,1,0:T(8,128)(2,1)S(1)} %get-tuple-element.73.state_ref), channel_id=1, source_target_pairs={{0,8},{4,12},{8,0},{12,4},{16,24},{20,28},{24,16},{28,20},{1,9},{5... | collective-permute-start | bytes 393224 | tf_op jit(solution)/shard_map/ppermute | solution.py:536
  19.1 8.3 %collective-permute-start.2 = (bf16[4,128,128]{2,1,0:T(8,128)(2,1)S(1)}, bf16[4,128,128]{2,1,0:T(8,128)(2,1)S(1)}, u32[]{:S(2)}, u32[]{:S(2)}) collective-permute-start(bf16[4,128,128]{2,1,0:T(8,128)(2,1)S(1)} %get-tuple-element.81.move_ref), channel_id=1, source_target_pairs={{0,8},{4,12},{8,0},{12,4},{16,24},{20,28},{24,16},{28,20},{1,9},{5... | collective-permute-start | bytes 393224 | tf_op jit(solution)/shard_map/ppermute | solution.py:538
  22.8 6.6 %collective-permute-start.3 = (bf16[4,128,128]{2,1,0:T(8,128)(2,1)S(1)}, bf16[4,128,128]{2,1,0:T(8,128)(2,1)S(1)}, u32[]{:S(2)}, u32[]{:S(2)}) collective-permute-start(bf16[4,128,128]{2,1,0:T(8,128)(2,1)S(1)} %step.1), channel_id=1, source_target_pairs={{0,4},{4,0},{8,24},{12,28},{16,20},{20,16},{24,8},{28,12},{1,5},{5... | collective-permute-start | bytes 393224 | tf_op jit(solution)/shard_map/ppermute | solution.py:541
  25.4 5.5 %collective-permute-start.4 = (bf16[4,128,128]{2,1,0:T(8,128)(2,1)S(1)}, bf16[4,128,128]{2,1,0:T(8,128)(2,1)S(1)}, u32[]{:S(2)}, u32[]{:S(2)}) collective-permute-start(bf16[4,128,128]{2,1,0:T(8,128)(2,1)S(1)} %step.1), channel_id=1, source_target_pairs={{0,4},{4,0},{8,16},{12,20},{16,8},{20,12},{24,28},{28,24},{1,5},{5... | collective-permute-start | bytes 393224 | tf_op jit(solution)/shard_map/ppermute | solution.py:540
  31.5 5.0 %collective-permute-start.5 = (bf16[4,128,128]{2,1,0:T(8,128)(2,1)S(1)}, bf16[4,128,128]{2,1,0:T(8,128)(2,1)S(1)}, u32[]{:S(2)}, u32[]{:S(2)}) collective-permute-start(bf16[4,128,128]{2,1,0:T(8,128)(2,1)S(1)} %get-tuple-element.98), channel_id=1, source_target_pairs={{0,4},{4,0},{8,12},{12,8},{16,20},{20,16},{24,28},{28,24},{1,5},{5... | collective-permute-start | bytes 393224 | tf_op jit(solution)/shard_map/ppermute | solution.py:546
  37.1 2.9 %collective-permute-start.9 = (bf16[320,1024]{1,0:T(8,128)(2,1)S(1)}, bf16[320,1024]{1,0:T(8,128)(2,1)S(1)}, u32[]{:S(2)}, u32[]{:S(2)}) collective-permute-start(bf16[320,1024]{1,0:T(8,128)(2,1)S(1)} %norm_pass.5.own_ref), channel_id=1, source_target_pairs={{0,1},{1,0},{2,3},{3,2},{4,5},{5,4},{6,7},{7,6},{8,9},{9,8},{10,11... | collective-permute-start | bytes 1966088 | tf_op jit(solution)/shard_map/ppermute | solution.py:663
  37.9 5.3 %collective-permute-start.10 = (bf16[320,1024]{1,0:T(8,128)(2,1)S(1)}, bf16[320,1024]{1,0:T(8,128)(2,1)S(1)}, u32[]{:S(2)}, u32[]{:S(2)}) collective-permute-start(bf16[320,1024]{1,0:T(8,128)(2,1)S(1)} %norm_pass.6.own_ref), channel_id=1, source_target_pairs={{0,1},{1,0},{2,3},{3,2},{4,5},{5,4},{6,7},{7,6},{8,9},{9,8},{10,11... | collective-permute-start | bytes 1966088 | tf_op jit(solution)/shard_map/ppermute | solution.py:663
  39.0 6.3 %collective-permute-start.11 = (bf16[256,1024]{1,0:T(8,128)(2,1)S(1)}, bf16[256,1024]{1,0:T(8,128)(2,1)S(1)}, u32[]{:S(2)}, u32[]{:S(2)}) collective-permute-start(bf16[256,1024]{1,0:T(8,128)(2,1)S(1)} %norm_pass.7.own_ref), channel_id=1, source_target_pairs={{0,1},{1,0},{2,3},{3,2},{4,5},{5,4},{6,7},{7,6},{8,9},{9,8},{10,11... | collective-permute-start | bytes 1572872 | tf_op jit(solution)/shard_map/ppermute | solution.py:663
  39.4 8.7 %collective-permute-start.6 = (bf16[128,1024]{1,0:T(8,128)(2,1)S(1)}, bf16[128,1024]{1,0:T(8,128)(2,1)S(1)}, u32[]{:S(2)}, u32[]{:S(2)}) collective-permute-start(bf16[128,1024]{1,0:T(8,128)(2,1)S(1)} %norm_pass.4.own_ref), channel_id=1, source_target_pairs={{0,1},{1,0},{2,3},{3,2},{4,5},{5,4},{6,7},{7,6},{8,9},{9,8},{10,11... | collective-permute-start | bytes 786440 | tf_op jit(solution)/shard_map/ppermute | solution.py:663
  41.6 23.3 %collective-permute-start.12 = (bf16[320,512]{1,0:T(8,128)(2,1)S(1)}, bf16[320,512]{1,0:T(8,128)(2,1)S(1)}, u32[]{:S(2)}, u32[]{:S(2)}) collective-permute-start(bf16[320,512]{1,0:T(8,128)(2,1)S(1)} %get-tuple-element.120), channel_id=1, source_target_pairs={{0,2},{1,3},{2,0},{3,1},{4,6},{5,7},{6,4},{7,5},{8,10},{9,11},{10,... | collective-permute-start | bytes 983048 | tf_op jit(solution)/shard_map/ppermute | solution.py:667
  44.7 20.1 %collective-permute-start.13 = (bf16[320,512]{1,0:T(8,128)(2,1)S(1)}, bf16[320,512]{1,0:T(8,128)(2,1)S(1)}, u32[]{:S(2)}, u32[]{:S(2)}) collective-permute-start(bf16[320,512]{1,0:T(8,128)(2,1)S(1)} %get-tuple-element.121), channel_id=1, source_target_pairs={{0,2},{1,3},{2,0},{3,1},{4,6},{5,7},{6,4},{7,5},{8,10},{9,11},{10,... | collective-permute-start | bytes 983048 | tf_op jit(solution)/shard_map/ppermute | solution.py:667
  46.6 18.3 %collective-permute-start.14 = (bf16[256,512]{1,0:T(8,128)(2,1)S(1)}, bf16[256,512]{1,0:T(8,128)(2,1)S(1)}, u32[]{:S(2)}, u32[]{:S(2)}) collective-permute-start(bf16[256,512]{1,0:T(8,128)(2,1)S(1)} %get-tuple-element.122), channel_id=1, source_target_pairs={{0,2},{1,3},{2,0},{3,1},{4,6},{5,7},{6,4},{7,5},{8,10},{9,11},{10,... | collective-permute-start | bytes 786440 | tf_op jit(solution)/shard_map/ppermute | solution.py:667
  48.9 17.8 %collective-permute-start.8 = (bf16[128,512]{1,0:T(8,128)(2,1)S(1)}, bf16[128,512]{1,0:T(8,128)(2,1)S(1)}, u32[]{:S(2)}, u32[]{:S(2)}) collective-permute-start(bf16[128,512]{1,0:T(8,128)(2,1)S(1)} %get-tuple-element.116), channel_id=1, source_target_pairs={{0,2},{1,3},{2,0},{3,1},{4,6},{5,7},{6,4},{7,5},{8,10},{9,11},{10,... | collective-permute-start | bytes 393224 | tf_op jit(solution)/shard_map/ppermute | solution.py:667
